TPU v7x, 32 devices: a whole 2x2x4 slice. The times are simulated.
32 devices in a mesh: view: 4 (over y, core), tile: 8 (over z, x).
Axes of the slice: x: 2, y: 2, z: 4, core: 2. Of those that a mesh axis runs over, the one named last changes fastest.
Arguments:
- objects: float32 [4, 2, 128, 1024], P('view', None, None, 'tile'), may hold values from -6 to 6
- probe: float32 [2, 128, 128], replicated, may hold values from -1.5 to 1.5
- positions: int32 [4, 64], P('view', 'tile'), may hold values from 0 to 896, as said below
- amplitudes: float32 [4, 64, 128, 128], P('view', 'tile'), may hold values from 0 to 1.0606601
- reproj_prev: float32 [4, 2, 128, 1024], P('view', None, None, 'tile'), may hold values from -6 to 6
- multipliers: float32 [4, 2, 128, 1024], P('view', None, None, 'tile'), may hold values from -4 to 4
- volume: float32 [2, 128, 1024, 1024], P(None, ('view', 'tile')), may hold values from -6 to 6
- angles: int32 [4], replicated, may hold values from 0 to 3
- penalty: int32 [2], replicated, may hold values from 1 to 5, as said below
Outputs:
- reprojections: float32 [4, 2, 128, 1024], P('view', None, None, 'tile')
- new_multipliers: float32 [4, 2, 128, 1024], P('view', None, None, 'tile')
Inputs may be any that keep to these rules, and one draw needn't show every extreme that they name: `positions`: the window of a scan covers 128 columns inside the strip. The penalty is the first entry divided by the second; the first is 1 to 4, the second is 5. `angles`: angle index k is a view at k times 90 degrees.
All inputs are finite; a program needn't handle non-finite values.
Results may differ from a plain program's by a relative error of at most 0.0001.
Values sent between devices are 32-bit elements; how exact they have to be, the bound alone decides.
No kernel may reach another device: no remote copies, remote signals or barrier semaphores. Data moves between devices by JAX's collectives and lax.ppermute only.
A program may use at most 128 MiB of HBM per device.

v0:
```python
import math

import jax
import jax.numpy as jnp
from jax import lax
from jax.sharding import PartitionSpec as P

ITERS = 2


HIGHEST = lax.Precision.HIGHEST


def dft_tables(length):
    indices = jnp.arange(length, dtype=jnp.int32)
    phase = (indices[:, None] * indices[None, :] % length).astype(jnp.float32) * (
        2.0 * math.pi / length
    )
    factor = 1.0 / math.sqrt(length)
    return (jnp.cos(phase) * factor, -jnp.sin(phase) * factor)


def left_apply(cosine, sine, sign, real_part, imag_part):
    first = jnp.einsum("rk,nkc->nrc", cosine, real_part, precision=HIGHEST)
    second = jnp.einsum("rk,nkc->nrc", sine, imag_part, precision=HIGHEST)
    third = jnp.einsum("rk,nkc->nrc", cosine, imag_part, precision=HIGHEST)
    fourth = jnp.einsum("rk,nkc->nrc", sine, real_part, precision=HIGHEST)
    return (first - sign * second, third + sign * fourth)


def right_apply(cosine, sine, sign, real_part, imag_part):
    first = jnp.einsum("nrk,kc->nrc", real_part, cosine, precision=HIGHEST)
    second = jnp.einsum("nrk,kc->nrc", imag_part, sine, precision=HIGHEST)
    third = jnp.einsum("nrk,kc->nrc", imag_part, cosine, precision=HIGHEST)
    fourth = jnp.einsum("nrk,kc->nrc", real_part, sine, precision=HIGHEST)
    return (first - sign * second, third + sign * fourth)


def window_columns(starts, width):
    return (starts[:, None] + jnp.arange(width, dtype=jnp.int32)[None, :]).reshape(-1)


def strip_gradient(strip, starts, measured, probe, floor):
    rows = strip.shape[1]
    width = probe.shape[2]
    total = strip.shape[2]
    windows = jax.vmap(lambda start: lax.dynamic_slice_in_dim(strip, start, width, axis=2))(starts)
    window_re = windows[:, 0]
    window_im = windows[:, 1]
    probe_re = probe[0]
    probe_im = probe[1]
    exit_re = probe_re * window_re - probe_im * window_im
    exit_im = probe_re * window_im + probe_im * window_re
    row_cos, row_sin = dft_tables(rows)
    col_cos, col_sin = dft_tables(width)
    mid_re, mid_im = left_apply(row_cos, row_sin, 1.0, exit_re, exit_im)
    far_re, far_im = right_apply(col_cos, col_sin, 1.0, mid_re, mid_im)
    modulus = jnp.sqrt(far_re * far_re + far_im * far_im)
    keep = 1.0 - measured / jnp.maximum(modulus, floor)
    back_re, back_im = left_apply(row_cos, row_sin, -1.0, far_re * keep, far_im * keep)
    back_re, back_im = right_apply(col_cos, col_sin, -1.0, back_re, back_im)
    grad_re = probe_re * back_re + probe_im * back_im
    grad_im = probe_re * back_im - probe_im * back_re
    columns = window_columns(starts, width)
    values = jnp.stack([grad_re, grad_im], axis=0).transpose(0, 2, 1, 3).reshape(2, rows, -1)
    return jnp.zeros((2, rows, total), jnp.float32).at[:, :, columns].add(values)


def illumination(starts, probe, total):
    rows = probe.shape[1]
    width = probe.shape[2]
    power = probe[0] * probe[0] + probe[1] * probe[1]
    values = jnp.broadcast_to(power[:, None, :], (rows, starts.shape[0], width)).reshape(rows, -1)
    return jnp.zeros((rows, total), jnp.float32).at[:, window_columns(starts, width)].add(values)


def project(column_sum, row_sum, angles):
    length = column_sum.shape[-1]
    angle_grid = angles[:, None]
    along = column_sum[..., None, :]
    across = row_sum[..., None, :]
    result = jnp.where(
        angle_grid == 0,
        along,
        jnp.where(
            angle_grid == 1,
            across,
            jnp.where(angle_grid == 2, jnp.flip(along, -1), jnp.flip(across, -1)),
        ),
    )
    return result * (1.0 / math.sqrt(length))


def backproject(lines, angles):
    length = lines.shape[-1]
    angle_grid = angles[:, None]
    zero = jnp.zeros_like(lines)
    column_term = jnp.sum(jnp.where(angle_grid == 0, lines, zero), -2) + jnp.flip(
        jnp.sum(jnp.where(angle_grid == 2, lines, zero), -2), -1
    )
    row_term = jnp.sum(jnp.where(angle_grid == 1, lines, zero), -2) + jnp.flip(
        jnp.sum(jnp.where(angle_grid == 3, lines, zero), -2), -1
    )
    return (column_term[..., None, :] + row_term[..., :, None]) * (1.0 / math.sqrt(length))


def shards(
    objects, probe, positions, amplitudes, reproj_prev, multipliers, volume, angles, penalty
):
    tiles = lax.axis_size("tile")
    views = lax.axis_size("view")
    strip = objects[0]
    previous = reproj_prev[0]
    lagrange = multipliers[0]
    starts = positions[0]
    measured = amplitudes[0]
    tile_width = strip.shape[2]
    total = tile_width * tiles
    width = probe.shape[2]
    cover = starts.shape[0] * tiles * width // total
    floor = 0.25 / math.sqrt(cover)
    penalty_value = penalty[0].astype(jnp.float32) / penalty[1].astype(jnp.float32)
    power = lax.psum_scatter(
        illumination(starts, probe, total), "tile", scatter_dimension=1, tiled=True
    )
    for sweep in range(ITERS):
        whole = lax.all_gather(strip, "tile", axis=2, tiled=True)
        grad = lax.psum_scatter(
            strip_gradient(whole, starts, measured, probe, floor),
            "tile",
            scatter_dimension=2,
            tiled=True,
        )
        strip = strip - (grad + penalty_value * (strip - previous) + lagrange) / (
            power + penalty_value
        )
    owned = volume.shape[1]
    slabs, slab_lagrange = (
        lax.all_to_all(strip, ("view", "tile"), split_axis=1, concat_axis=2, tiled=True),
        lax.all_to_all(lagrange, ("view", "tile"), split_axis=1, concat_axis=2, tiled=True),
    )
    slabs = slabs.reshape(2, owned, views, total)
    slab_lagrange = slab_lagrange.reshape(2, owned, views, total)
    projected = project(volume.sum(2), volume.sum(3), angles)
    misfit = projected - slabs - slab_lagrange / penalty_value
    updated = volume - backproject(misfit, angles) / views
    fresh = project(updated.sum(2), updated.sum(3), angles)
    renewed = slab_lagrange + penalty_value * (slabs - fresh)
    fresh_strip, renewed_strip = (
        lax.all_to_all(
            fresh.reshape(2, owned, views * total),
            ("view", "tile"),
            split_axis=2,
            concat_axis=1,
            tiled=True,
        ),
        lax.all_to_all(
            renewed.reshape(2, owned, views * total),
            ("view", "tile"),
            split_axis=2,
            concat_axis=1,
            tiled=True,
        ),
    )
    return (fresh_strip[None], renewed_strip[None])


def solution(mesh):
    return jax.shard_map(
        shards,
        mesh=mesh,
        in_specs=(
            P("view", None, None, "tile"),
            P(),
            P("view", "tile"),
            P("view", "tile", None, None),
            P("view", None, None, "tile"),
            P("view", None, None, "tile"),
            P(None, ("view", "tile"), None, None),
            P(),
            P(),
        ),
        out_specs=(P("view", None, None, "tile"), P("view", None, None, "tile")),
        check_vma=False,
    )
```

profile of v0, /device:TPU:0, one launch (start us, length us, event | category | flops | bytes accessed | tf_op | source)
XLA Modules:
  0.0 482.5 jit_solution(60233305305366370)
XLA Ops:
  7.3 1.7 copy.342
  10.8 6.8 %scatter_custom_fusion.1 = f32[128,1024]{0,1:T(8,128)} fusion(s32[1024]{0:T(1024)S(1)} %bitcast.314, f32[1024,128]{1,0:T(8,128)S(1)} %bitcast.310, f32[]{:T(128)} %constant.20.clone.1), kind=kCustom, calls=%fused_computation.66 | custom fusion | flops 131072 | bytes 524292 | tf_op jit(solution)/shard_map/scatter-add | solution.py:74
  19.2 34.4 %all-gather.6.cloned.1.call-done = f32[1,2,128,1024]{2,1,0,3:T(2,128)} async-done(((f32[1,2,128,128]{2,1,0,3:T(2,128)}), f32[1,2,128,1024]{2,1,0,3:T(2,128)}) %all-gather.6.cloned.1.call-update) | async-done | bytes 1048592 | tf_op jit(solution)/shard_map/all_gather | solution.py:127
  53.6 2.9 gather_fusion
  58.5 1.2 fusion.34
  59.7 1.2 fusion.38
  60.9 1.2 fusion.16
  62.1 1.1 fusion.87
  63.2 1.2 fusion.17
  64.4 1.1 fusion.90
  65.6 1.1 convolution_subtract_fusion.2
  66.7 2.3 fusion.26
  69.0 1.1 fusion.75
  70.1 1.6 fusion.85
  71.7 1.1 fusion.13
  72.9 1.1 fusion.15
  74.0 1.1 fusion.83
  75.1 1.1 fusion.81
  76.3 1.1 fusion.10
  77.4 1.1 add_bitcast_fusion.1
  80.0 32.8 %scatter_fusion = f32[2,128,1024]{1,0,2:T(2,128)S(1)} fusion(f32[2,128,1024]{1,0,2:T(2,128)S(1)} %broadcast.156.clone, s32[1024]{0:T(1024)S(1)} %bitcast.315, f32[1024,2,128]{2,1,0:T(2,128)S(1)} %copy.378), kind=kCustom, calls=%fused_computation.2 | custom fusion | flops 262144 | bytes 3149824 | tf_op jit(solution)/shard_map/scatter-add | solution.py:66
  112.9 1.0 copy-done.1
  119.3 79.4 %all-reduce.6.cloned.1.call-done = f32[2,128,1024]{1,0,2:T(2,128)} async-done(((f32[2,128,1024]{1,0,2:T(2,128)}), f32[2,128,1024]{1,0,2:T(2,128)}) %all-reduce.6.cloned.1.call-update) | async-done | bytes 1048592
  198.7 1.7 divide_subtract_fusion.1
  200.4 1.7 copy.534
  202.1 4.2 all-to-all-start.1
  206.3 1.2 broadcast_compare_fusion
  207.5 33.6 %all-gather.4.cloned.1.call-done = f32[2,128,1024]{1,0,2:T(2,128)} async-done(((f32[2,128,128]{1,0,2:T(2,128)}), f32[2,128,1024]{1,0,2:T(2,128)}) %all-gather.4.cloned.1.call-update) | async-done | bytes 1048592 | tf_op jit(solution)/shard_map/all_gather | solution.py:127
  241.1 2.9 gather_fusion.1
  245.9 1.2 fusion.40
  247.1 1.2 fusion.44
  248.3 1.2 fusion.8
  249.5 1.1 fusion.69
  250.7 1.2 fusion.9
  251.9 1.1 fusion.72
  253.0 1.1 convolution_subtract_fusion
  254.1 2.3 fusion.24
  256.4 1.1 fusion.65
  257.6 1.3 fusion.67
  258.9 1.1 fusion.5
  260.1 1.1 fusion.7
  261.2 1.1 fusion.79
  262.3 1.1 fusion.77
  263.4 1.1 fusion.2
  264.6 1.1 add_bitcast_fusion
  267.2 32.8 %scatter_fusion.1 = f32[2,128,1024]{1,0,2:T(2,128)S(1)} fusion(f32[2,128,1024]{1,0,2:T(2,128)S(1)} %broadcast.156, s32[1024]{0:T(1024)S(1)} %bitcast.316, f32[1024,2,128]{2,1,0:T(2,128)S(1)} %copy.417), kind=kCustom, calls=%fused_computation.4 | custom fusion | flops 262144 | bytes 3149824 | tf_op jit(solution)/shard_map/scatter-add | solution.py:66
  300.0 1.0 copy-done
  301.1 12.5 %fusion.259 = (f32[2,4,1024]{2,1,0:T(4,128)S(1)}, f32[2,4,1024]{2,1,0:T(4,128)S(1)}) fusion(f32[2,4,1024,1024]{3,2,1,0:T(8,128)} %param.15), kind=kLoop, calls=%fused_computation.327 | loop fusion | flops 16760832 | bytes 33619968 | tf_op jit(solution)/shard_map/reduce_sum | solution.py:144
  313.6 64.4 %all-reduce.8.cloned.1.call-done = f32[2,128,1024]{1,0,2:T(2,128)} async-done(((f32[2,128,1024]{1,0,2:T(2,128)}), f32[2,128,1024]{1,0,2:T(2,128)}) %all-reduce.8.cloned.1.call-update) | async-done | bytes 1048592
  378.0 1.1 divide_subtract_fusion
  379.9 4.4 all-to-all-start
  386.1 6.0 %all-to-all-done = f32[2,128,128]{2,0,1:T(2,128)S(1)} async-done(((f32[2,128,128]{2,0,1:T(2,128)}), f32[2,128,128]{2,0,1:T(2,128)S(1)}, u32[]{:S(2)}, u32[]{:S(2)}) %all-to-all-start) | async-done | bytes 131104 | tf_op jit(solution)/shard_map/all_to_all | solution.py:139
  392.2 1.2 select_reduce_fusion.2
  394.8 14.2 %fusion = (f32[2,4,1024]{2,1,0:T(4,128)S(1)}, f32[2,4,1024]{2,1,0:T(4,128)S(1)}) fusion(f32[2,4,1024,1024]{3,2,1,0:T(8,128)} %param.15, f32[2,4,1024]{2,1,0:T(4,128)S(1)} %add.290, f32[2,4,1024]{2,1,0:T(4,128)S(1)} %add.288), kind=kLoop, calls=%fused_computation.6 | loop fusion | flops 41926656 | bytes 33685504 | tf_op jit(solution)/shard_map/reduce_sum | solution.py:147
  411.2 4.4 copy.426
  415.6 8.6 %reshape.222 = f32[32,1,1024]{2,1,0:T(1,128)} reshape(f32[4096,2,4]{2,1,0:T(2,128)} %bitcast.299) | data formatting | bytes 262144
  424.2 2.6 all-to-all-start.3
  426.8 4.4 copy.424
  431.2 8.6 %reshape.220 = f32[32,1,1024]{2,1,0:T(1,128)} reshape(f32[4096,2,4]{2,1,0:T(2,128)} %bitcast.300) | data formatting | bytes 262144
  439.7 6.1 %all-to-all-start.2 = ((f32[32,1,1024]{2,1,0:T(1,128)}), f32[32,1,1024]{2,1,0:T(1,128)S(1)}, u32[]{:S(2)}, u32[]{:S(2)}) async-start(f32[32,1,1024]{2,1,0:T(1,128)} %reshape.220), calls=%async_computation.3 | async-start | bytes 262144 | tf_op jit(solution)/shard_map/all_to_all | solution.py:150
  447.3 7.8 %reshape.223 = f32[4096,2,4]{2,1,0:T(2,128)} reshape(f32[32,1024]{1,0:T(8,128)S(1)} %reduce.1) | data formatting | bytes 262144
  455.1 5.8 %copy.427 = f32[2,32,4,128]{3,2,1,0:T(4,128)} copy(f32[2,32,4,128]{2,0,3,1:T(2,128)} %bitcast.301) | data formatting | bytes 262144 | tf_op jit(solution)/shard_map/all_to_all | solution.py:157
  461.9 7.8 %reshape.221 = f32[4096,2,4]{2,1,0:T(2,128)} reshape(f32[32,1024]{1,0:T(8,128)S(1)} %reduce) | data formatting | bytes 262144
  469.7 5.8 %copy.425 = f32[2,32,4,128]{3,2,1,0:T(4,128)} copy(f32[2,32,4,128]{2,0,3,1:T(2,128)} %bitcast.302) | data formatting | bytes 262144 | tf_op jit(solution)/shard_map/all_to_all | solution.py:150
  (88 shorter events, 22.3 us)
Async XLA Ops:
  7.2 110.0 %copy-start.7 = (u32[32]{0:T(128)S(1)}, u32[32]{0:T(128)}, u32[]{:S(2)}) copy-start(u32[32]{0:T(128)} %constant.116) | copy-start | bytes 388
  7.2 106.8 %copy-start.3 = (f32[1,2,128,128]{3,2,1,0:T(8,128)S(1)}, f32[1,2,128,128]{3,2,1,0:T(8,128)}, u32[]{:S(2)}) copy-start(f32[1,2,128,128]{3,2,1,0:T(8,128)} %param.9) | copy-start | bytes 393220
  7.2 106.9 %copy-start.6 = (s32[2]{0:T(128)S(1)}, s32[2]{0:T(128)}, u32[]{:S(2)}) copy-start(s32[2]{0:T(128)} %param.17) | copy-start | bytes 28
  7.2 108.8 %copy-start.4 = (f32[1,2,128,128]{3,2,1,0:T(8,128)S(1)}, f32[1,2,128,128]{3,2,1,0:T(8,128)}, u32[]{:S(2)}) copy-start(f32[1,2,128,128]{3,2,1,0:T(8,128)} %param.13) | copy-start | bytes 393220
  7.2 46.4 %all-gather.6.cloned.1.call-start = ((), (), s32[]{:S(2)}) async-start(), calls=%async_computation.7 | async-start | bytes 1179648 | tf_op jit(solution)/shard_map/all_gather | solution.py:127
  9.0 109.4 %reduce-scatter.2.cloned.1.call-start = ((), (), s32[]{:S(2)}) async-start(), calls=%async_computation.5 | async-start | bytes 589824 | tf_op jit(solution)/shard_map/reduce_scatter | solution.py:123
  17.6 181.0 %all-reduce.6.cloned.1.call-start = ((), (), s32[]{:S(2)}) async-start(), calls=%async_computation.8 | async-start | bytes 2097152
  112.8 1.0 copy-start.1
  113.9 127.2 %all-gather.4.cloned.1.call-start = ((), (), s32[]{:S(2)}) async-start(), calls=%async_computation.6 | async-start | bytes 1179648 | tf_op jit(solution)/shard_map/all_gather | solution.py:127
  119.3 88.2 %copy-start.2 = (f32[128,128]{0,1:T(8,128)}, f32[128,128]{0,1:T(8,128)S(1)}, u32[]{:S(2)}) copy-start(f32[128,128]{0,1:T(8,128)S(1)} %broadcast_add_fusion) | copy-start | bytes 196612
  202.1 177.8 %all-to-all-start.1 = ((f32[2,128,128]{2,0,1:T(2,128)}), f32[2,128,128]{2,0,1:T(2,128)S(1)}, u32[]{:S(2)}, u32[]{:S(2)}) async-start(f32[2,128,128]{2,0,1:T(2,128)} %bitcast.295), calls=%async_computation.2 | async-start | bytes 262144 | tf_op jit(solution)/shard_map/all_to_all | solution.py:140
  206.3 171.8 %all-reduce.8.cloned.1.call-start = ((), (), s32[]{:S(2)}) async-start(), calls=%async_computation.9 | async-start | bytes 2097152
  248.3 65.2 %copy-start.5 = (pred[4]{0:T(512)(128)(4,1)S(1)}, pred[4]{0:T(512)(128)(4,1)}, u32[]{:S(2)}) copy-start(pred[4]{0:T(512)(128)(4,1)} %get-tuple-element.29) | copy-start | bytes 16
  300.0 1.0 copy-start
  379.9 12.2 %all-to-all-start = ((f32[2,128,128]{2,0,1:T(2,128)}), f32[2,128,128]{2,0,1:T(2,128)S(1)}, u32[]{:S(2)}, u32[]{:S(2)}) async-start(f32[2,128,128]{2,0,1:T(2,128)} %copy.418), calls=%async_computation.1 | async-start | bytes 262144 | tf_op jit(solution)/shard_map/all_to_all | solution.py:139
  424.2 15.6 %all-to-all-start.3 = ((f32[32,1,1024]{2,1,0:T(1,128)}), f32[32,1,1024]{2,1,0:T(1,128)S(1)}, u32[]{:S(2)}, u32[]{:S(2)}) async-start(f32[32,1,1024]{2,1,0:T(1,128)} %reshape.222), calls=%async_computation.4 | async-start | bytes 262144 | tf_op jit(solution)/shard_map/all_to_all | solution.py:157
  439.7 21.2 %all-to-all-start.2 = ((f32[32,1,1024]{2,1,0:T(1,128)}), f32[32,1,1024]{2,1,0:T(1,128)S(1)}, u32[]{:S(2)}, u32[]{:S(2)}) async-start(f32[32,1,1024]{2,1,0:T(1,128)} %reshape.220), calls=%async_computation.3 | async-start | bytes 262144 | tf_op jit(solution)/shard_map/all_to_all | solution.py:150
Sparse Core Ops, SparseCore 0:
  10.7 42.8 all-gather.5
  57.0 60.6 reduce-scatter.1
  121.6 76.9 all-reduce.5
  201.2 39.8 all-gather.3
  301.2 76.7 all-reduce.7
where the time goes:
time: 488 us; the launch traced here: 483 us
  waiting for transfers between devices  218 us (45%)
  other arithmetic  110 us (23%)
  local copies, waits for them, and re-layouts  81.1 us (17%)
  matrix products  39.6 us (8%)
  starting transfers between devices  17.5 us (4%)
  between operations  17 us (3%)
    unnamed x7, waiting for transfers between devices  144 us
    all_gather x2, waiting for transfers between devices, shards(): whole = lax.all_gather(strip, 'tile', axis=2, tiled=True)  68 us
    scatter-add x2, other arithmetic, strip_gradient(): jnp.zeros((2, rows, total), jnp.float32).at[:, :, columns].add(values)  65.6 us
    unnamed x34, local copies, waits for them, and re-layouts  40.3 us
    reduce_sum x1, other arithmetic, shards(): fresh = project(updated.sum(2), updated.sum(3), angles)  14.2 us
    reduce_sum x1, other arithmetic, shards(): projected = project(volume.sum(2), volume.sum(3), angles)  12.5 us
  transfers between devices with their start and end apart: 9, of which 5 were waited for; matrix products, arithmetic and copies ran while one was open for 37% of the time, Pallas kernels for 0%

commit v1 on v0

v1 whole, which is shorter than its diff:
```python
import functools
import math

import jax
import jax.numpy as jnp
import numpy as np
from jax import lax
from jax.experimental import pallas as pl
from jax.experimental.pallas import tpu as pltpu
from jax.sharding import PartitionSpec as P

ITERS = 2
AXES = ("view", "tile")
VMEM = pl.BlockSpec(memory_space=pltpu.VMEM)
SMEM = pl.BlockSpec(memory_space=pltpu.SMEM)
LIMIT = pltpu.CompilerParams(vmem_limit_bytes=48 * 2**20)
HIGHEST = lax.Precision.HIGHEST


class Routes:
    def __init__(self, views, tiles):
        self.views, self.tiles, self.half = views, tiles, tiles // 2
        self.hubs = (tiles // 4, tiles - 1 - tiles // 4)

    def at(self, view, tile):
        return view * self.tiles + tile

    def to_hub(self, part, swap):
        return [
            (
                self.at(2 * k + b, j * self.half + (part ^ b if swap else part)),
                self.at(2 * k + j, self.hubs[b]),
            )
            for k in range(self.views // 2)
            for b in range(2)
            for j in range(2)
        ]

    def from_hub(self, part):
        return [(target, source) for source, target in self.to_hub(part, False)]

    def cores(self):
        return [
            (self.at(v, t), self.at(v ^ 1, t)) for v in range(self.views) for t in range(self.tiles)
        ]


def send(value, pairs):
    return lax.ppermute(value, AXES, pairs)


def dft(length):
    indices = np.arange(length)
    phase = (indices[:, None] * indices[None, :] % length) * (2.0 * math.pi / length)
    return np.cos(phase) / math.sqrt(length), -np.sin(phase) / math.sqrt(length)


def halves(matrix):
    high = matrix.astype(jnp.bfloat16)
    return high, (matrix - high.astype(np.float64)).astype(jnp.bfloat16)


def tables(rows, width):
    result = []
    cosine, sine = dft(rows)
    for sign in (1.0, -1.0):
        high, low = halves(np.block([[cosine, -sign * sine], [sign * sine, cosine]]))
        result.append(np.concatenate([high, low, high], 1))
    cosine, sine = dft(width)
    for sign in (1.0, -1.0):
        high, low = halves(np.block([[cosine, sign * sine], [-sign * sine, cosine]]))
        result.append(np.concatenate([high, low, high], 0))
    return [jnp.asarray(table) for table in result]


def split(value):
    high = value.astype(jnp.bfloat16)
    return high, (value - high.astype(jnp.float32)).astype(jnp.bfloat16)


def left(table, value):
    high, low = split(value)
    return jnp.dot(
        table, jnp.concatenate([high, high, low], 0), preferred_element_type=jnp.float32
    )


def right(value, table):
    high, low = split(value)
    return jnp.dot(
        jnp.concatenate([high, high, low], 1), table, preferred_element_type=jnp.float32
    )


def place(meta, index, chunks, width):
    start = meta[index]
    chunk = start // width
    offset = meta[meta.shape[0] - 2]
    here = lax.rem(chunk + offset, chunks)
    after = lax.rem(jnp.minimum(chunk + 1, chunks - 1) + offset, chunks)
    return here, after, start - chunk * width


def gather_chunks(refs, strip):
    at = 0
    for ref in refs:
        if len(ref.shape) == 3:
            strip[at : at + ref.shape[0]] = ref[...]
            at += ref.shape[0]
        else:
            strip[at] = ref[: strip.shape[1]]
            at += 1


def gradient_kernel(floor, part_list, n_strip, n_parts, first, meta, *refs):
    pieces, refs = refs[:n_strip], refs[n_strip:]
    measured, refs = refs[:n_parts], refs[n_parts:]
    probe, forward_left, back_left, forward_right, back_right = refs[:5]
    refs = refs[5:]
    if not first:
        before, refs = refs[0], refs[1:]
    grad, strip = refs
    chunks = strip.shape[0]
    _, rows, width = probe.shape
    gather_chunks(pieces, strip)
    if first:
        grad[...] = jnp.zeros_like(grad)
    else:
        grad[...] = before[...]
    lane = lax.broadcasted_iota(jnp.int32, (rows, width), 1)
    probe_re = probe[0]
    probe_im = probe[1]
    swapped = meta[meta.shape[0] - 1]
    def work(part, amplitude):
        batch = amplitude.shape[0]
        row = part + swapped * (1 - 2 * lax.rem(part, 2))
        columns = []
        spots = []
        for j in range(batch):
            here, after, shift = place(meta, row * batch + j, chunks, width)
            spots.append((here, after, shift))
            back = lax.rem(width - shift, width)
            keep = lane < width - shift
            re, im = [
                jnp.where(
                    keep,
                    pltpu.roll(strip[here, k * rows : (k + 1) * rows], back, 1),
                    pltpu.roll(strip[after, k * rows : (k + 1) * rows], back, 1),
                )
                for k in range(2)
            ]
            columns.append(
                jnp.concatenate(
                    [probe_re * re - probe_im * im, probe_re * im + probe_im * re], 0
                )
            )
        mid = left(forward_left[...], jnp.concatenate(columns, 1))
        mid = jnp.concatenate(
            [
                jnp.concatenate(
                    [
                        mid[:rows, j * width : (j + 1) * width],
                        mid[rows:, j * width : (j + 1) * width],
                    ],
                    1,
                )
                for j in range(batch)
            ],
            0,
        )
        far = right(mid, forward_right[...])
        far_re = far[:, :width]
        far_im = far[:, width:]
        level = amplitude[...].reshape(batch * rows, width)
        keep = 1.0 - level * jnp.minimum(
            lax.rsqrt(far_re * far_re + far_im * far_im), 1.0 / floor
        )
        mid = right(jnp.concatenate([far_re * keep, far_im * keep], 1), back_right[...])
        mid = jnp.concatenate(
            [
                jnp.concatenate(
                    [
                        mid[j * rows : (j + 1) * rows, :width],
                        mid[j * rows : (j + 1) * rows, width:],
                    ],
                    0,
                )
                for j in range(batch)
            ],
            1,
        )
        back = left(back_left[...], mid)
        for j in range(batch):
            here, after, shift = spots[j]
            back_re = back[:rows, j * width : (j + 1) * width]
            back_im = back[rows:, j * width : (j + 1) * width]
            inside = lane >= shift
            for k, value in enumerate(
                (
                    probe_re * back_re + probe_im * back_im,
                    probe_re * back_im - probe_im * back_re,
                )
            ):
                value = pltpu.roll(value, shift, 1)
                band = slice(k * rows, (k + 1) * rows)
                grad[here, band] += jnp.where(inside, value, 0.0)
                grad[after, band] += jnp.where(inside, 0.0, value)

    if len(part_list) == n_parts:
        for part, amplitude in zip(part_list, measured):
            work(part, amplitude)
    else:

        def step(index, carry):
            work(index, measured[0].at[index])
            return carry

        lax.fori_loop(0, measured[0].shape[0], step, 0)


def gradient(meta, pieces, measured, part_list, probe, dft_tables, floor, chunks, before):
    _, rows, width = probe.shape
    shape = (chunks, 2 * rows, width)
    carried = [] if before is None else [before]
    count = 1 + len(pieces) + len(measured) + 1 + len(dft_tables)
    return pl.pallas_call(
        functools.partial(
            gradient_kernel,
            floor,
            tuple(part_list),
            len(pieces),
            len(measured),
            before is None,
        ),
        out_shape=jax.ShapeDtypeStruct(shape, jnp.float32),
        in_specs=[SMEM] + [VMEM] * (count - 1 + len(carried)),
        out_specs=VMEM,
        scratch_shapes=[pltpu.VMEM(shape, jnp.float32)],
        input_output_aliases={} if before is None else {count: 0},
        compiler_params=LIMIT,
    )(meta, *pieces, *measured, probe, *dft_tables, *carried)


def illumination_kernel(meta, probe, power):
    chunks = power.shape[0]
    _, rows, width = probe.shape
    power[...] = jnp.zeros_like(power)
    lane = lax.broadcasted_iota(jnp.int32, (rows, width), 1)
    value = probe[0] * probe[0] + probe[1] * probe[1]

    def step(index, carry):
        here, after, shift = place(meta, index, chunks, width)
        rolled = pltpu.roll(value, shift, 1)
        power[here] += jnp.where(lane >= shift, rolled, 0.0)
        power[after] += jnp.where(lane >= shift, 0.0, rolled)
        return carry

    lax.fori_loop(0, meta.shape[0] - 2, step, 0)


def illumination(meta, probe, chunks):
    _, rows, width = probe.shape
    return pl.pallas_call(
        illumination_kernel,
        out_shape=jax.ShapeDtypeStruct((chunks, rows, width), jnp.float32),
        in_specs=[SMEM, VMEM],
        out_specs=VMEM,
        compiler_params=LIMIT,
    )(meta, probe)


def update_kernel(n_strip, n_pull, rho, *refs):
    pieces, refs = refs[:n_strip], refs[n_strip:]
    pulls, refs = refs[:n_pull], refs[n_pull:]
    grad, grad_other, power, power_other, out = refs
    count = out.shape[0]
    rows = power.shape[1]
    ratio = rho[0]
    for chunk in range(count):
        inverse = 1.0 / (power[chunk] + power_other[chunk] + ratio)
        for k in range(2):
            band = slice(k * rows, (k + 1) * rows)
            old = pieces[0][chunk, band] if n_strip == 1 else pieces[chunk][band]
            pull = pulls[0][chunk, band] if n_pull == 1 else pulls[chunk][band]
            step = grad[chunk, band] + grad_other[chunk, band] + ratio * old - pull
            out[chunk, band] = old - step * inverse


def update(rho, pieces, pulls, grad, grad_other, power, power_other):
    own = power_other.shape[0]
    return pl.pallas_call(
        functools.partial(update_kernel, len(pieces), len(pulls)),
        out_shape=jax.ShapeDtypeStruct((own,) + grad.shape[1:], jnp.float32),
        in_specs=[SMEM] + [VMEM] * (len(pieces) + len(pulls) + 4),
        out_specs=VMEM,
        compiler_params=LIMIT,
    )(rho, *pieces, *pulls, grad, grad_other, power, power_other)


def sums_kernel(block, column, row, partial):
    index = pl.program_id(0)
    step = pl.program_id(1)
    _, rows, length = block.shape
    value = block[0]
    down = value.reshape(rows // 8, 8, length).sum(0)

    @pl.when(step == 0)
    def _():
        partial[...] = down

    @pl.when(step > 0)
    def _():
        partial[...] += down

    @pl.when(step == pl.num_programs(1) - 1)
    def _():
        column[pl.ds(index, 1), :] = partial[...].sum(0, keepdims=True)

    across = value.reshape(rows, length)
    lanes = 128
    folded = across[:, :lanes]
    for k in range(1, length // lanes):
        folded = folded + across[:, k * lanes : (k + 1) * lanes]
    line = lax.dot_general(
        jnp.ones((8, lanes), jnp.float32),
        folded,
        (((1,), (1,)), ((), ())),
        precision=HIGHEST,
        preferred_element_type=jnp.float32,
    )
    row[pl.ds(index, 1), pl.ds(pl.multiple_of(step * rows, rows), rows)] = line[:1]


def volume_sums(volume):
    planes, length, _ = volume.shape
    rows = length // 2
    out = jax.ShapeDtypeStruct((planes, length), jnp.float32)
    return pl.pallas_call(
        sums_kernel,
        grid=(planes, length // rows),
        out_shape=(out, out),
        in_specs=[pl.BlockSpec((1, rows, length), lambda i, k: (i, k, 0))],
        out_specs=(
            pl.BlockSpec((planes, length), lambda i, k: (0, 0)),
            pl.BlockSpec((planes, length), lambda i, k: (0, 0)),
        ),
        scratch_shapes=[pltpu.VMEM((8, length), jnp.float32)],
        compiler_params=LIMIT,
    )(volume)


def pack_kernel(n_parts, rho, *refs):
    parts, (lagrange, psi, packed) = refs[:n_parts], refs[n_parts:]
    owners, planes, _ = packed.shape
    owned = planes // 2
    for k in range(2):
        value = parts[0][k]
        for part in parts[1:]:
            value = value + part[k]
        psi[k] = value
        value = value + lagrange[k] / rho[0]
        packed[:, k * owned : (k + 1) * owned, :] = value.reshape(owners, owned, value.shape[1])


def slice_kernel(views, angles, lines, column, row, out):
    total, planes, width = lines.shape
    tiles = total // views
    length = column.shape[1]
    scale = 1.0 / math.sqrt(length)
    rows_of = lax.broadcasted_iota(jnp.int32, (width, width), 0)
    columns_of = lax.broadcasted_iota(jnp.int32, (width, width), 1)
    mirror = jnp.where(rows_of + columns_of == width - 1, 1.0, 0.0).astype(jnp.float32)

    def flip(values):
        stacked = jnp.dot(
            jnp.concatenate(values, 0),
            mirror,
            precision=HIGHEST,
            preferred_element_type=jnp.float32,
        )
        return [stacked[k * planes : (k + 1) * planes] for k in range(len(values))]

    base = []
    plain = []
    turned = []
    count = []
    for parity, source in ((0, column), (1, row)):
        for t in range(tiles):
            base.append(source[:, t * width : (t + 1) * width] * scale)
            plain.append(
                sum(
                    jnp.where(angles[u] == parity, lines[u * tiles + t], 0.0)
                    for u in range(views)
                )
            )
            turned.append(
                sum(
                    jnp.where(angles[u] == parity + 2, lines[u * tiles + tiles - 1 - t], 0.0)
                    for u in range(views)
                )
            )
        count.append(
            sum(
                jnp.where((angles[u] == parity) | (angles[u] == parity + 2), 1.0, 0.0)
                for u in range(views)
            )
        )
    turned = flip(turned)
    misfit = [
        base[parity * tiles + t] * count[parity]
        - plain[parity * tiles + t]
        - turned[parity * tiles + t]
        for parity in range(2)
        for t in range(tiles)
    ]
    total_of = [
        jnp.sum(
            functools.reduce(jnp.add, misfit[parity * tiles : (parity + 1) * tiles]),
            1,
            keepdims=True,
        )
        * (1.0 / length)
        for parity in range(2)
    ]
    fresh = [
        base[parity * tiles + t]
        - (misfit[parity * tiles + t] + total_of[1 - parity]) * (1.0 / views)
        for parity in range(2)
        for t in range(tiles)
    ]
    reversed_fresh = flip(fresh)
    for u in range(views):
        for t in range(tiles):
            out[u * tiles + t] = jnp.where(
                angles[u] == 0,
                fresh[t],
                jnp.where(
                    angles[u] == 1,
                    fresh[tiles + t],
                    jnp.where(
                        angles[u] == 2,
                        reversed_fresh[tiles - 1 - t],
                        reversed_fresh[2 * tiles - 1 - t],
                    ),
                ),
            )


def final_kernel(rho, packed, psi, lagrange, fresh, renewed):
    owners, planes, width = packed.shape
    owned = planes // 2
    for k in range(2):
        value = packed[:, k * owned : (k + 1) * owned, :].reshape(owners * owned, width)
        fresh[k] = value
        renewed[k] = lagrange[k] + rho[0] * (psi[k] - value)


def shards(
    objects, probe, positions, amplitudes, reproj_prev, multipliers, volume, angles, penalty
):
    tiles = lax.axis_size("tile")
    views = lax.axis_size("view")
    routes = Routes(views, tiles)
    half = routes.half
    _, _, rows, tile_width = objects.shape
    width = probe.shape[2]
    total = tile_width * tiles
    chunks = total // width
    scans = positions.shape[1]
    owned = volume.shape[1]
    floor = 0.25 / math.sqrt(scans * tiles * width // total)
    rho = penalty[0].astype(jnp.float32) / penalty[1].astype(jnp.float32)
    rho_array = rho[None]
    lagrange = multipliers[0]
    measured = amplitudes[0]
    core = lax.rem(lax.axis_index("view"), 2)
    swapped = (lax.axis_index("tile") == routes.hubs[1]).astype(jnp.int32)
    dft_tables = tables(rows, width)

    def as_chunks(parts):
        if tile_width == width:
            return parts
        joined = jnp.stack([part[: 2 * rows] for part in parts], 0)
        joined = joined.reshape(chunks // 2, width // tile_width, 2 * rows, tile_width)
        return [joined.transpose(0, 2, 1, 3).reshape(chunks // 2, 2 * rows, width)]

    def as_tiles(own):
        if tile_width == width:
            return [own[part].reshape(2, rows, width) for part in range(half)]
        parts = own.reshape(chunks // 2, 2 * rows, width // tile_width, tile_width)
        parts = parts.transpose(0, 2, 1, 3).reshape(half, 2, rows, tile_width)
        return [parts[part] for part in range(half)]

    pad = -scans % tile_width
    starts = jnp.pad(positions.astype(jnp.float32), ((0, 0), (0, pad))).reshape(-1, tile_width)
    starts = jnp.pad(starts, ((0, -starts.shape[0] % 8), (0, 0)))
    message = jnp.concatenate([objects.reshape(2 * rows, tile_width), starts], 0)
    arrived = [send(message, routes.to_hub(part, False)) for part in range(half)]
    levels = [send(measured, routes.to_hub(part, True)) for part in range(half)]
    pull = (rho * reproj_prev - multipliers).reshape(2 * rows, tile_width)
    pulls = as_chunks([send(pull, routes.to_hub(part, False)) for part in range(half)])
    column, row = volume_sums(volume.reshape(2 * owned, total, total))

    meta = jnp.concatenate(
        [part[2 * rows :].reshape(-1)[:scans].astype(jnp.int32) for part in arrived]
        + [(core * (chunks // 2))[None], swapped[None]]
    )
    own = as_chunks(arrived)
    other = [send(part, routes.cores()) for part in own]
    power = illumination(meta, probe, chunks)
    power_other = send(power[chunks // 2 :], routes.cores())

    grad = None
    if half > 4:
        levels = [jnp.stack(levels, 0)]
        grad = gradient(
            meta, own + other, levels, range(half), probe, dft_tables, floor, chunks, None
        )
    else:
        for part in range(half):
            grad = gradient(
                meta, own + other, [levels[part]], [part], probe, dft_tables, floor, chunks, grad
            )
    for sweep in range(ITERS):
        grad_other = send(grad[chunks // 2 :], routes.cores())
        mine = update(rho_array, own, pulls, grad, grad_other, power, power_other)
        if sweep + 1 < ITERS:
            own = [mine]
            other = [send(mine, routes.cores())]
            grad = gradient(
                meta, own + other, levels, range(half), probe, dft_tables, floor, chunks, None
            )

    parts = [send(part, routes.from_hub(index)) for index, part in enumerate(as_tiles(mine))]
    strip = jax.ShapeDtypeStruct((2, rows, tile_width), jnp.float32)
    owners = views * tiles
    exchanged = jax.ShapeDtypeStruct((owners, 2 * owned, tile_width), jnp.float32)
    psi, packed = pl.pallas_call(
        functools.partial(pack_kernel, len(parts)),
        out_shape=(strip, exchanged),
        in_specs=[SMEM] + [VMEM] * (len(parts) + 1),
        out_specs=(VMEM, VMEM),
        compiler_params=LIMIT,
    )(rho_array, *parts, lagrange)
    lines = lax.all_to_all(packed, AXES, split_axis=0, concat_axis=0, tiled=True)
    fresh = pl.pallas_call(
        functools.partial(slice_kernel, views),
        out_shape=exchanged,
        in_specs=[SMEM] + [VMEM] * 3,
        out_specs=VMEM,
        compiler_params=LIMIT,
    )(angles, lines, column, row)
    fresh = lax.all_to_all(fresh, AXES, split_axis=0, concat_axis=0, tiled=True)
    fresh_strip, renewed = pl.pallas_call(
        final_kernel,
        out_shape=(strip, strip),
        in_specs=[SMEM] + [VMEM] * 3,
        out_specs=(VMEM, VMEM),
        compiler_params=LIMIT,
    )(rho_array, fresh, psi, lagrange)
    return (fresh_strip[None], renewed[None])


def solution(mesh):
    return jax.shard_map(
        shards,
        mesh=mesh,
        in_specs=(
            P("view", None, None, "tile"),
            P(),
            P("view", "tile"),
            P("view", "tile", None, None),
            P("view", None, None, "tile"),
            P("view", None, None, "tile"),
            P(None, ("view", "tile"), None, None),
            P(),
            P(),
        ),
        out_specs=(P("view", None, None, "tile"), P("view", None, None, "tile")),
        check_vma=False,
    )
```

time: 488 us -> 148 us (0.30)
  waiting for transfers between devices: 218 us -> 17.7 us
  other arithmetic: 110 us -> 2.61 us
  local copies, waits for them, and re-layouts: 81.1 us -> 15.2 us
  Pallas kernels: 0 us -> 50.9 us
  matrix products: 39.6 us -> 0 us
  starting transfers between devices: 17.5 us -> 44.2 us
  between operations: 17 us -> 2.4 us
  blocking collectives: 0 us -> 13.4 us
    unnamed x7 -> x0, waiting for transfers between devices: 144 us -> none
    scatter-add x3 -> x0, other arithmetic: 72.4 us -> none  [the longest x2 65.6 us: strip_gradient(): jnp.zeros((2, rows, total), jnp.float32).at[:, :, columns].add(values)]
    all_gather x2 -> x0, waiting for transfers between devices: 68 us -> none  [shards(): whole = lax.all_gather(strip, 'tile', axis=2, tiled=True)]
    pallas_call x0 -> x12, Pallas kernels: none -> 50.9 us  [the longest x5 25.7 us: gradient(): pl.pallas_call(functools.partial(gradient_kernel, floor, tuple(part_list)...]
    dot_general x32 -> x0, matrix products: 39.6 us -> none  [the longest x4 6.83 us: right_apply(): fourth = jnp.einsum('nrk,kc->nrc', real_part, sine, precision=HIGHEST)]
    ppermute x0 -> x24, starting transfers between devices: none -> 35.4 us  [send(): return lax.ppermute(value, AXES, pairs)]
    reduce_sum x3 -> x0, other arithmetic: 27.8 us -> none  [the longest x1 14.2 us: shards(): fresh = project(updated.sum(2), updated.sum(3), angles)]
    unnamed x34 -> x32, local copies, waits for them, and re-layouts: 40.3 us -> 13.7 us
  transfers between devices with their start and end apart: 9 -> 25, of which waited for: 5 -> 7; matrix products, arithmetic and copies ran while one was open for 37% -> 2% of each run, Pallas kernels for 0% -> 23%
where the time goes in v1:
time: 148 us; the launch traced here: 147 us
  Pallas kernels  50.9 us (34%)
  starting transfers between devices  44.2 us (30%)
  waiting for transfers between devices  17.7 us (12%)
  local copies, waits for them, and re-layouts  15.2 us (10%)
  blocking collectives  13.4 us (9%)
  other arithmetic  2.61 us (2%)
  between operations  2.4 us (2%)
    ppermute x24, starting transfers between devices, send(): return lax.ppermute(value, AXES, pairs)  35.4 us
    pallas_call x5, Pallas kernels, gradient(): pl.pallas_call(functools.partial(gradient_kernel, floor, tuple(part_list)...  25.7 us
    pallas_call x1, Pallas kernels, volume_sums(): pl.pallas_call(sums_kernel, grid=(planes, length // rows), out_shape=(out...  18.8 us
    ppermute x24, waiting for transfers between devices, send(): return lax.ppermute(value, AXES, pairs)  17.7 us
    unnamed x32, local copies, waits for them, and re-layouts  13.7 us
    all_to_all x1, blocking collectives, shards(): fresh = lax.all_to_all(fresh, AXES, split_axis=0, concat_axis=0, tiled=True)  13.4 us
    all_to_all x1, starting transfers between devices, shards(): lax.all_to_all(packed, AXES, split_axis=0, concat_axis=0, tiled=True)  8.88 us
    pallas_call x1, Pallas kernels, illumination(): pl.pallas_call(illumination_kernel, out_shape=jax.ShapeDtypeStruct((chunk...  3.63 us
  transfers between devices with their start and end apart: 25, of which 7 were waited for; matrix products, arithmetic and copies ran while one was open for 2% of the time, Pallas kernels for 23%

profile of v1, /device:TPU:0, one launch (start us, length us, event | category | flops | bytes accessed | tf_op | source)
XLA Modules:
  0.0 146.5 jit_solution(12936745345866164899)
XLA Ops:
  0.6 0.7 convert_element_type.30
  1.3 0.9 select_maximum_fusion
  2.3 0.7 collective-permute-start.3
  2.9 0.7 collective-permute-start.2
  3.6 0.7 collective-permute-start.1
  4.3 6.2 %collective-permute-start = (f32[264,128]{1,0:T(8,128)S(1)}, f32[264,128]{1,0:T(8,128)S(1)}, u32[]{:S(2)}, u32[]{:S(2)}) collective-permute-start(f32[264,128]{1,0:T(8,128)S(1)} %select_maximum_fusion), channel_id=1, source_target_pairs={{0,2},{4,10},{8,5},{12,13},{16,18},{20,26},{24,21},{28,29}} | collective-permute-start | bytes 405512 | tf_op jit(solution)/shard_map/ppermute | solution.py:49
  10.5 1.3 collective-permute-start.15
  11.8 0.7 collective-permute-start.14
  12.5 0.7 collective-permute-start.13
  13.3 0.7 collective-permute-start.12
  14.0 7.2 %collective-permute-start.10 = (f32[264,128]{1,0:T(8,128)S(1)}, f32[264,128]{1,0:T(8,128)S(1)}, u32[]{:S(2)}, u32[]{:S(2)}) collective-permute-start(f32[264,128]{1,0:T(8,128)S(1)} %collective-permute-done.2.refs_2_), channel_id=1, source_target_pairs={{0,8},{1,9},{2,10},{3,11},{4,12},{5,13},{6,14},{7,15},{8,0},{9,1},... | collective-permute-start | bytes 405512 | tf_op jit(solution)/shard_map/ppermute | solution.py:49
  21.2 1.0 collective-permute-done.10.refs_6_
  22.2 0.4 collective-permute-start.11
  22.6 1.0 collective-permute-done.11.refs_7_
  23.6 0.4 collective-permute-start.8
  23.9 1.0 collective-permute-done.8.refs_4_
  24.9 0.4 collective-permute-start.9
  25.3 0.1 concatenate.7.meta
  25.4 0.9 collective-permute-done.9.refs_5_
  26.3 1.0 copy-done
  27.3 1.0 copy-done.3
  28.3 1.0 copy-done.6
  29.3 1.0 copy-done.9
  30.3 0.9 copy-done.11
  31.2 3.6 %shard_map.140.refs_14_ = f32[8,256,128]{2,1,0:T(8,128)S(1)} custom-call(s32[34]{0:T(128)S(1)} %concatenate.7.meta, f32[264,128]{1,0:T(8,128)S(1)} %collective-permute-done.refs_0_, f32[264,128]{1,0:T(8,128)S(1)} %collective-permute-done.1.refs_1_, f32[264,128]{1,0:T(8,128)S(1)} %collective-permute-done.2.refs_2_, ...), custom_call_target="tpu_custom_call" | custom-call | tf_op jit(solution)/shard_map/pallas_call | solution.py:226
  34.8 1.0 copy-done.1
  35.8 1.0 copy-done.4
  36.8 1.0 copy-done.7
  37.8 0.9 copy-done.12
  38.7 3.7 %shard_map.141.refs_14_ = f32[8,256,128]{2,1,0:T(8,128)S(1)} custom-call(s32[34]{0:T(128)S(1)} %concatenate.7.meta, f32[264,128]{1,0:T(8,128)S(1)} %collective-permute-done.refs_0_, f32[264,128]{1,0:T(8,128)S(1)} %collective-permute-done.1.refs_1_, f32[264,128]{1,0:T(8,128)S(1)} %collective-permute-done.2.refs_2_, ...), custom_call_target="tpu_custom_call", output_to_operand_aliasing={{}: (15, {})} | custom-call | tf_op jit(solution)/shard_map/pallas_call | solution.py:226
  42.4 3.7 %shard_map.142.refs_14_ = f32[8,256,128]{2,1,0:T(8,128)S(1)} custom-call(s32[34]{0:T(128)S(1)} %concatenate.7.meta, f32[264,128]{1,0:T(8,128)S(1)} %collective-permute-done.refs_0_, f32[264,128]{1,0:T(8,128)S(1)} %collective-permute-done.1.refs_1_, f32[264,128]{1,0:T(8,128)S(1)} %collective-permute-done.2.refs_2_, ...), custom_call_target="tpu_custom_call", output_to_operand_aliasing={{}: (15, {})} | custom-call | tf_op jit(solution)/shard_map/pallas_call | solution.py:226
  46.2 3.7 %shard_map.143.refs_8_ = f32[8,256,128]{2,1,0:T(8,128)S(1)} custom-call(s32[34]{0:T(128)S(1)} %concatenate.7.meta, f32[264,128]{1,0:T(8,128)S(1)} %collective-permute-done.refs_0_, f32[264,128]{1,0:T(8,128)S(1)} %collective-permute-done.1.refs_1_, f32[264,128]{1,0:T(8,128)S(1)} %collective-permute-done.2.refs_2_, ...), custom_call_target="tpu_custom_call", output_to_operand_aliasing={{}: (15, {})} | custom-call | tf_op jit(solution)/shard_map/pallas_call | solution.py:226
  49.9 0.4 collective-permute-start.16
  50.4 1.3 fusion.1
  53.0 1.0 multiply_subtract_fusion
  54.0 4.3 %collective-permute-start.4 = (f32[256,128]{1,0:T(8,128)S(1)}, f32[256,128]{1,0:T(8,128)S(1)}, u32[]{:S(2)}, u32[]{:S(2)}) collective-permute-start(f32[256,128]{1,0:T(8,128)S(1)} %bitcast.26), channel_id=1, source_target_pairs={{0,2},{4,10},{8,5},{12,13},{16,18},{20,26},{24,21},{28,29}} | collective-permute-start | bytes 393224 | tf_op jit(solution)/shard_map/ppermute | solution.py:49
  58.3 3.6 %shard_map.144.refs_10_.refs_7_ = f32[8,128,128]{2,1,0:T(8,128)S(1)} custom-call(s32[34]{0:T(128)S(1)} %concatenate.7.meta, f32[2,128,128]{2,1,0:T(8,128)S(1)} %copy-done.12), custom_call_target="tpu_custom_call" | custom-call | tf_op jit(solution)/shard_map/pallas_call | solution.py:263
  61.9 5.0 %collective-permute-start.17 = (f32[4,128,128]{2,1,0:T(8,128)S(1)}, f32[4,128,128]{2,1,0:T(8,128)S(1)}, u32[]{:S(2)}, u32[]{:S(2)}) collective-permute-start(f32[4,128,128]{2,1,0:T(8,128)S(1)} %slice.73), channel_id=1, source_target_pairs={{0,8},{1,9},{2,10},{3,11},{4,12},{5,13},{6,14},{7,15},{8,0},{9,1},... | collective-permute-start | bytes 786440 | tf_op jit(solution)/shard_map/ppermute | solution.py:49
  66.9 0.7 collective-permute-start.5
  67.6 0.7 collective-permute-start.6
  68.3 0.8 collective-permute-start.7
  69.2 0.2 shard_map.145.refs_0_
  69.4 0.1 collective-permute-start.18
  69.5 1.9 %collective-permute-done.18.refs_1_ = f32[4,256,128]{2,1,0:T(8,128)S(1)} collective-permute-done((f32[4,256,128]{2,1,0:T(8,128)S(1)}, f32[4,256,128]{2,1,0:T(8,128)S(1)}, u32[]{:S(2)}, u32[]{:S(2)}) %collective-permute-start.18) | collective-permute-done | bytes 524320 | tf_op jit(solution)/shard_map/ppermute | solution.py:49
  71.3 1.0 copy-done.2
  72.3 1.0 copy-done.5
  73.3 1.0 copy-done.8
  74.3 1.0 copy-done.10
  75.3 0.9 copy-done.13
  76.2 11.0 %shard_map.146.refs_5_ = f32[8,256,128]{2,1,0:T(8,128)S(1)} custom-call(s32[34]{0:T(128)S(1)} %concatenate.7.meta, f32[4,256,128]{2,1,0:T(8,128)S(1)} %shard_map.145.refs_0_, f32[4,256,128]{2,1,0:T(8,128)S(1)} %collective-permute-done.18.refs_1_, f32[8,128,128]{2,1,0:T(8,128)S(1)} %collective-permute-done.15.refs_8_.refs_2_, ...), custom_call_target="tpu_custom_call" | custom-call | tf_op jit(solution)/shard_map/pallas_call | solution.py:226
  87.3 0.2 collective-permute-start.19
  87.5 1.8 %collective-permute-done.19.refs_6_ = f32[4,256,128]{2,1,0:T(8,128)S(1)} collective-permute-done((f32[4,256,128]{2,1,0:T(8,128)S(1)}, f32[4,256,128]{2,1,0:T(8,128)S(1)}, u32[]{:S(2)}, u32[]{:S(2)}) %collective-permute-start.19) | collective-permute-done | bytes 524320 | tf_op jit(solution)/shard_map/ppermute | solution.py:49
  89.2 0.1 shard_map.147
  89.4 1.3 collective-permute-start.20
  90.7 0.7 collective-permute-start.21
  91.4 0.7 collective-permute-start.22
  92.1 0.7 collective-permute-start.23
  92.7 10.2 %collective-permute-done.20.refs_0_ = f32[2,128,128]{2,1,0:T(8,128)S(1)} collective-permute-done((f32[2,128,128]{2,1,0:T(8,128)S(1)}, f32[2,128,128]{2,1,0:T(8,128)S(1)}, u32[]{:S(2)}, u32[]{:S(2)}) %collective-permute-start.20) | collective-permute-done | bytes 131104 | tf_op jit(solution)/shard_map/ppermute | solution.py:49
  102.9 0.7 shard_map.148
  103.6 8.9 %all-to-all-start = ((f32[32,8,128]{2,1,0:T(8,128)}), f32[32,8,128]{2,1,0:T(8,128)S(1)}, u32[]{:S(2)}, u32[]{:S(2)}) async-start(f32[32,8,128]{2,1,0:T(8,128)} %get-tuple-element.8), calls=%async_computation | async-start | bytes 262144 | tf_op jit(solution)/shard_map/all_to_all | solution.py:545
  112.5 18.8 %shard_map.149 = (f32[8,1024]{1,0:T(8,128)S(1)}, f32[8,1024]{1,0:T(8,128)S(1)}) custom-call(f32[8,1024,1024]{2,1,0:T(8,128)} %bitcast.24), custom_call_target="tpu_custom_call" | custom-call | tf_op jit(solution)/shard_map/pallas_call | solution.py:338
  131.3 1.1 shard_map.150
  132.4 13.4 %all_to_all.10.packed = f32[32,8,128]{2,1,0:T(8,128)S(1)} all-to-all(f32[32,8,128]{2,1,0:T(8,128)S(1)} %shard_map.150), channel_id=1, replica_groups=mesh['view'=4,'tile'=8] {'view','tile'}, dimensions={0} | all-to-all | bytes 262144 | tf_op jit(solution)/shard_map/all_to_all | solution.py:553
  145.8 0.7 shard_map.151
  (48 shorter events, 0.2 us)
Async XLA Ops:
  0.6 102.3 %copy-start.14 = (f32[1,2,128,128]{3,2,1,0:T(8,128)S(1)}, f32[1,2,128,128]{3,2,1,0:T(8,128)}, u32[]{:S(2)}) copy-start(f32[1,2,128,128]{3,2,1,0:T(8,128)} %param.18) | copy-start | bytes 393220
  2.3 9.6 %collective-permute-start.3 = (f32[264,128]{1,0:T(8,128)S(1)}, f32[264,128]{1,0:T(8,128)S(1)}, u32[]{:S(2)}, u32[]{:S(2)}) collective-permute-start(f32[264,128]{1,0:T(8,128)S(1)} %select_maximum_fusion), channel_id=1, source_target_pairs={{3,2},{7,10},{11,5},{15,13},{19,18},{23,26},{27,21},{31,29}} | collective-permute-start | bytes 405512 | tf_op jit(solution)/shard_map/ppermute | solution.py:49
  2.9 9.6 %collective-permute-start.2 = (f32[264,128]{1,0:T(8,128)S(1)}, f32[264,128]{1,0:T(8,128)S(1)}, u32[]{:S(2)}, u32[]{:S(2)}) collective-permute-start(f32[264,128]{1,0:T(8,128)S(1)} %select_maximum_fusion), channel_id=1, source_target_pairs={{2,2},{6,10},{10,5},{14,13},{18,18},{22,26},{26,21},{30,29}} | collective-permute-start | bytes 405512 | tf_op jit(solution)/shard_map/ppermute | solution.py:49
  3.6 9.7 %collective-permute-start.1 = (f32[264,128]{1,0:T(8,128)S(1)}, f32[264,128]{1,0:T(8,128)S(1)}, u32[]{:S(2)}, u32[]{:S(2)}) collective-permute-start(f32[264,128]{1,0:T(8,128)S(1)} %select_maximum_fusion), channel_id=1, source_target_pairs={{1,2},{5,10},{9,5},{13,13},{17,18},{21,26},{25,21},{29,29}} | collective-permute-start | bytes 405512 | tf_op jit(solution)/shard_map/ppermute | solution.py:49
  4.3 9.7 %collective-permute-start = (f32[264,128]{1,0:T(8,128)S(1)}, f32[264,128]{1,0:T(8,128)S(1)}, u32[]{:S(2)}, u32[]{:S(2)}) collective-permute-start(f32[264,128]{1,0:T(8,128)S(1)} %select_maximum_fusion), channel_id=1, source_target_pairs={{0,2},{4,10},{8,5},{12,13},{16,18},{20,26},{24,21},{28,29}} | collective-permute-start | bytes 405512 | tf_op jit(solution)/shard_map/ppermute | solution.py:49
  10.5 15.8 %collective-permute-start.15 = (f32[8,128,128]{2,1,0:T(8,128)}, f32[8,128,128]{2,1,0:T(8,128)S(1)}, u32[]{:S(2)}, u32[]{:S(2)}) collective-permute-start(f32[8,128,128]{2,1,0:T(8,128)} %bitcast.34), channel_id=1, source_target_pairs={{0,2},{4,10},{9,5},{13,13},{16,18},{20,26},{25,21},{29,29}} | collective-permute-start | bytes 1572872 | tf_op jit(solution)/shard_map/ppermute | solution.py:49
  11.8 23.0 %collective-permute-start.14 = (f32[8,128,128]{2,1,0:T(8,128)}, f32[8,128,128]{2,1,0:T(8,128)S(1)}, u32[]{:S(2)}, u32[]{:S(2)}) collective-permute-start(f32[8,128,128]{2,1,0:T(8,128)} %bitcast.35), channel_id=1, source_target_pairs={{1,2},{5,10},{8,5},{12,13},{17,18},{21,26},{24,21},{28,29}} | collective-permute-start | bytes 1572872 | tf_op jit(solution)/shard_map/ppermute | solution.py:49
  12.5 29.9 %collective-permute-start.13 = (f32[8,128,128]{2,1,0:T(8,128)}, f32[8,128,128]{2,1,0:T(8,128)S(1)}, u32[]{:S(2)}, u32[]{:S(2)}) collective-permute-start(f32[8,128,128]{2,1,0:T(8,128)} %bitcast.36), channel_id=1, source_target_pairs={{2,2},{6,10},{11,5},{15,13},{18,18},{22,26},{27,21},{31,29}} | collective-permute-start | bytes 1572872 | tf_op jit(solution)/shard_map/ppermute | solution.py:49
  13.3 32.9 %collective-permute-start.12 = (f32[8,128,128]{2,1,0:T(8,128)}, f32[8,128,128]{2,1,0:T(8,128)S(1)}, u32[]{:S(2)}, u32[]{:S(2)}) collective-permute-start(f32[8,128,128]{2,1,0:T(8,128)} %bitcast.37), channel_id=1, source_target_pairs={{3,2},{7,10},{10,5},{14,13},{19,18},{23,26},{26,21},{30,29}} | collective-permute-start | bytes 1572872 | tf_op jit(solution)/shard_map/ppermute | solution.py:49
  14.0 8.2 %collective-permute-start.10 = (f32[264,128]{1,0:T(8,128)S(1)}, f32[264,128]{1,0:T(8,128)S(1)}, u32[]{:S(2)}, u32[]{:S(2)}) collective-permute-start(f32[264,128]{1,0:T(8,128)S(1)} %collective-permute-done.2.refs_2_), channel_id=1, source_target_pairs={{0,8},{1,9},{2,10},{3,11},{4,12},{5,13},{6,14},{7,15},{8,0},{9,1},... | collective-permute-start | bytes 405512 | tf_op jit(solution)/shard_map/ppermute | solution.py:49
  22.2 1.4 collective-permute-start.11
  23.6 1.4 collective-permute-start.8
  24.9 1.4 collective-permute-start.9
  26.3 1.0 copy-start
  27.3 1.0 copy-start.3
  28.3 1.0 copy-start.6
  29.3 1.0 copy-start.9
  30.3 0.9 copy-start.11
  34.8 1.0 copy-start.1
  35.8 1.0 copy-start.4
  36.8 1.0 copy-start.7
  37.8 0.9 copy-start.12
  38.7 92.6 %copy-start.15 = (s32[4]{0:T(128)S(1)}, s32[4]{0:T(128)}, u32[]{:S(2)}) copy-start(s32[4]{0:T(128)} %angles.1) | copy-start | bytes 52
  49.9 19.3 %collective-permute-start.16 = (f32[4,256,128]{2,1,0:T(8,128)S(1)}, f32[4,256,128]{2,1,0:T(8,128)S(1)}, u32[]{:S(2)}, u32[]{:S(2)}) collective-permute-start(f32[4,256,128]{2,1,0:T(8,128)S(1)} %slice.72), channel_id=1, source_target_pairs={{0,8},{1,9},{2,10},{3,11},{4,12},{5,13},{6,14},{7,15},{8,0},{9,1},... | collective-permute-start | bytes 1572872 | tf_op jit(solution)/shard_map/ppermute | solution.py:49
  54.0 14.3 %collective-permute-start.4 = (f32[256,128]{1,0:T(8,128)S(1)}, f32[256,128]{1,0:T(8,128)S(1)}, u32[]{:S(2)}, u32[]{:S(2)}) collective-permute-start(f32[256,128]{1,0:T(8,128)S(1)} %bitcast.26), channel_id=1, source_target_pairs={{0,2},{4,10},{8,5},{12,13},{16,18},{20,26},{24,21},{28,29}} | collective-permute-start | bytes 393224 | tf_op jit(solution)/shard_map/ppermute | solution.py:49
  61.9 7.2 %collective-permute-start.17 = (f32[4,128,128]{2,1,0:T(8,128)S(1)}, f32[4,128,128]{2,1,0:T(8,128)S(1)}, u32[]{:S(2)}, u32[]{:S(2)}) collective-permute-start(f32[4,128,128]{2,1,0:T(8,128)S(1)} %slice.73), channel_id=1, source_target_pairs={{0,8},{1,9},{2,10},{3,11},{4,12},{5,13},{6,14},{7,15},{8,0},{9,1},... | collective-permute-start | bytes 786440 | tf_op jit(solution)/shard_map/ppermute | solution.py:49
  66.9 2.2 %collective-permute-start.5 = (f32[256,128]{1,0:T(8,128)S(1)}, f32[256,128]{1,0:T(8,128)S(1)}, u32[]{:S(2)}, u32[]{:S(2)}) collective-permute-start(f32[256,128]{1,0:T(8,128)S(1)} %bitcast.27), channel_id=1, source_target_pairs={{1,2},{5,10},{9,5},{13,13},{17,18},{21,26},{25,21},{29,29}} | collective-permute-start | bytes 393224 | tf_op jit(solution)/shard_map/ppermute | solution.py:49
  67.6 1.6 %collective-permute-start.6 = (f32[256,128]{1,0:T(8,128)S(1)}, f32[256,128]{1,0:T(8,128)S(1)}, u32[]{:S(2)}, u32[]{:S(2)}) collective-permute-start(f32[256,128]{1,0:T(8,128)S(1)} %bitcast.28), channel_id=1, source_target_pairs={{2,2},{6,10},{10,5},{14,13},{18,18},{22,26},{26,21},{30,29}} | collective-permute-start | bytes 393224 | tf_op jit(solution)/shard_map/ppermute | solution.py:49
  68.3 0.9 collective-permute-start.7
  69.4 2.0 %collective-permute-start.18 = (f32[4,256,128]{2,1,0:T(8,128)S(1)}, f32[4,256,128]{2,1,0:T(8,128)S(1)}, u32[]{:S(2)}, u32[]{:S(2)}) collective-permute-start(f32[4,256,128]{2,1,0:T(8,128)S(1)} %shard_map.145.refs_0_), channel_id=1, source_target_pairs={{0,8},{1,9},{2,10},{3,11},{4,12},{5,13},{6,14},{7,15},{8,0},{9,1},... | collective-permute-start | bytes 1572872 | tf_op jit(solution)/shard_map/ppermute | solution.py:49
  71.3 1.0 copy-start.2
  72.3 1.0 copy-start.5
  73.3 1.0 copy-start.8
  74.3 1.0 copy-start.10
  75.3 0.9 copy-start.13
  87.3 2.0 %collective-permute-start.19 = (f32[4,256,128]{2,1,0:T(8,128)S(1)}, f32[4,256,128]{2,1,0:T(8,128)S(1)}, u32[]{:S(2)}, u32[]{:S(2)}) collective-permute-start(f32[4,256,128]{2,1,0:T(8,128)S(1)} %slice.74), channel_id=1, source_target_pairs={{0,8},{1,9},{2,10},{3,11},{4,12},{5,13},{6,14},{7,15},{8,0},{9,1},... | collective-permute-start | bytes 1572872 | tf_op jit(solution)/shard_map/ppermute | solution.py:49
  89.4 13.5 %collective-permute-start.20 = (f32[2,128,128]{2,1,0:T(8,128)S(1)}, f32[2,128,128]{2,1,0:T(8,128)S(1)}, u32[]{:S(2)}, u32[]{:S(2)}) collective-permute-start(f32[2,128,128]{2,1,0:T(8,128)S(1)} %bitcast.33), channel_id=1, source_target_pairs={{2,0},{10,4},{5,8},{13,12},{18,16},{26,20},{21,24},{29,28}} | collective-permute-start | bytes 393224 | tf_op jit(solution)/shard_map/ppermute | solution.py:49
  90.7 12.2 %collective-permute-start.21 = (f32[2,128,128]{2,1,0:T(8,128)S(1)}, f32[2,128,128]{2,1,0:T(8,128)S(1)}, u32[]{:S(2)}, u32[]{:S(2)}) collective-permute-start(f32[2,128,128]{2,1,0:T(8,128)S(1)} %bitcast.32), channel_id=1, source_target_pairs={{2,1},{10,5},{5,9},{13,13},{18,17},{26,21},{21,25},{29,29}} | collective-permute-start | bytes 393224 | tf_op jit(solution)/shard_map/ppermute | solution.py:49
  91.4 11.5 %collective-permute-start.22 = (f32[2,128,128]{2,1,0:T(8,128)S(1)}, f32[2,128,128]{2,1,0:T(8,128)S(1)}, u32[]{:S(2)}, u32[]{:S(2)}) collective-permute-start(f32[2,128,128]{2,1,0:T(8,128)S(1)} %bitcast.31), channel_id=1, source_target_pairs={{2,2},{10,6},{5,10},{13,14},{18,18},{26,22},{21,26},{29,30}} | collective-permute-start | bytes 393224 | tf_op jit(solution)/shard_map/ppermute | solution.py:49
  92.1 10.8 %collective-permute-start.23 = (f32[2,128,128]{2,1,0:T(8,128)S(1)}, f32[2,128,128]{2,1,0:T(8,128)S(1)}, u32[]{:S(2)}, u32[]{:S(2)}) collective-permute-start(f32[2,128,128]{2,1,0:T(8,128)S(1)} %bitcast.30), channel_id=1, source_target_pairs={{2,3},{10,7},{5,11},{13,15},{18,19},{26,23},{21,27},{29,31}} | collective-permute-start | bytes 393224 | tf_op jit(solution)/shard_map/ppermute | solution.py:49
  103.6 27.6 %all-to-all-start = ((f32[32,8,128]{2,1,0:T(8,128)}), f32[32,8,128]{2,1,0:T(8,128)S(1)}, u32[]{:S(2)}, u32[]{:S(2)}) async-start(f32[32,8,128]{2,1,0:T(8,128)} %get-tuple-element.8), calls=%async_computation | async-start | bytes 262144 | tf_op jit(solution)/shard_map/all_to_all | solution.py:545

commit v2 on v1

v2 whole, which is shorter than its diff:
```python
import functools
import math

import jax
import jax.numpy as jnp
import numpy as np
from jax import lax
from jax.experimental import pallas as pl
from jax.experimental.pallas import tpu as pltpu
from jax.sharding import PartitionSpec as P

ITERS = 2
AXES = ("view", "tile")
VMEM = pl.BlockSpec(memory_space=pltpu.VMEM)
SMEM = pl.BlockSpec(memory_space=pltpu.SMEM)
HBM = pl.BlockSpec(memory_space=pltpu.HBM)
COST = pl.CostEstimate(flops=0, bytes_accessed=0, transcendentals=0)
LIMIT = pltpu.CompilerParams(vmem_limit_bytes=16 * 2**20)
HIGHEST = lax.Precision.HIGHEST


class Routes:
    def __init__(self, views, tiles):
        self.views, self.tiles, self.half = views, tiles, tiles // 2
        self.hubs = (tiles // 4, tiles - 1 - tiles // 4)

    def at(self, view, tile):
        return view * self.tiles + tile

    def to_hub(self, part, swap):
        return [
            (
                self.at(2 * k + b, j * self.half + (self.turn(part, b) if swap else part)),
                self.at(2 * k + j, self.hubs[b]),
            )
            for k in range(self.views // 2)
            for b in range(2)
            for j in range(2)
        ]

    def from_hub(self, part):
        return [(target, source) for source, target in self.to_hub(part, False)]

    def turn(self, part, b):
        return self.half - 1 - part if b else part

    def relays(self):
        return [
            (self.at(v, tile), self.at(v, tile ^ 1))
            for v in range(self.views)
            for tile in ((self.tiles - 2 if v % 2 else 1),)
        ]

    def relayed(self, part):
        hops = dict(self.relays())
        return [(hops.get(source, source), target) for source, target in self.to_hub(part, True)]

    def cores(self):
        return [
            (self.at(v, t), self.at(v ^ 1, t)) for v in range(self.views) for t in self.hubs
        ]


def send(value, pairs):
    return lax.ppermute(value, AXES, pairs)


def dft(length):
    indices = np.arange(length)
    phase = (indices[:, None] * indices[None, :] % length) * (2.0 * math.pi / length)
    return np.cos(phase) / math.sqrt(length), -np.sin(phase) / math.sqrt(length)


def halves(matrix):
    high = matrix.astype(jnp.bfloat16)
    return high, (matrix - high.astype(np.float64)).astype(jnp.bfloat16)


def tables(rows, width):
    result = []
    for length in (rows, width):
        cosine, sine = dft(length)
        for sign in (1.0, -1.0):
            result.append(halves(np.block([[cosine, -sign * sine], [sign * sine, cosine]])))
    return jnp.asarray(np.array(result[:2] if rows == width else result))


def split(value):
    high = value.astype(jnp.bfloat16)
    return high, (value - high.astype(jnp.float32)).astype(jnp.bfloat16)


def left(table, value):
    high, low = split(value)
    first, second = table
    return jnp.dot(
        jnp.concatenate([first, second, first], 1),
        jnp.concatenate([high, high, low], 0),
        preferred_element_type=jnp.float32,
    )


def right(value, table):
    high, low = split(value)
    first, second = table
    return jnp.dot(
        jnp.concatenate([high, high, low], 1),
        jnp.concatenate([first, second, first], 0),
        preferred_element_type=jnp.float32,
    )


def place(meta, index, chunks, width):
    start = meta[index]
    chunk = start // width
    offset = meta[meta.shape[0] - 2]
    here = lax.rem(chunk + offset, chunks)
    after = lax.rem(jnp.minimum(chunk + 1, chunks - 1) + offset, chunks)
    return here, after, start - chunk * width


def sum_plane(plane, folded, lanes):
    rows, length = plane.shape

    def step(index, down):
        base = pl.multiple_of(index * lanes, lanes)
        for at in range(0, lanes, 8):
            value = plane[pl.ds(base + at, 8)]
            down = down + value
            parts = [value[:, k : k + lanes] for k in range(0, length, lanes)]
            while len(parts) > 1:
                parts = [first + second for first, second in zip(parts[::2], parts[1::2])]
            folded[pl.ds(base + at, 8)] = parts[0]
        return down

    down = lax.fori_loop(0, rows // lanes, step, jnp.zeros((8, length), jnp.float32))
    lines = [folded[at : at + lanes].T.sum(0, keepdims=True) for at in range(0, rows, lanes)]
    return down, jnp.concatenate(lines, 1)


def gradient_kernel(floor, part_list, n_parts, first, scans, meta, own, other, *refs):
    measured, refs = refs[:n_parts], refs[n_parts:]
    probe, table, refs = refs[0], refs[1], refs[2:]
    if not first:
        before, refs = refs[0], refs[1:]
    grad, strip = refs
    chunks = strip.shape[0]
    _, rows, width = probe.shape
    strip[: chunks // 2] = own[:, : 2 * rows]
    strip[chunks // 2 :] = other[:, : 2 * rows]
    if first:
        grad[...] = jnp.zeros_like(grad)
    else:
        grad[...] = before[...]
    lane = lax.broadcasted_iota(jnp.int32, (rows, width), 1)
    probe_re = probe[0]
    probe_im = probe[1]
    swapped = meta[meta.shape[0] - 1]

    def get(index):
        return table[index, 0], table[index, 1]

    across = table.shape[0] - 2

    def work(part, amplitude, batch):
        row = part + swapped * (meta.shape[0] // scans - 1 - 2 * part)
        columns = []
        spots = []
        for j in range(batch):
            here, after, shift = place(meta, row * batch + j, chunks, width)
            spots.append((here, after, shift))
            back = lax.rem(width - shift, width)
            keep = lane < width - shift
            re, im = [
                jnp.where(
                    keep,
                    pltpu.roll(strip[here, k * rows : (k + 1) * rows], back, 1),
                    pltpu.roll(strip[after, k * rows : (k + 1) * rows], back, 1),
                )
                for k in range(2)
            ]
            columns.append(
                jnp.concatenate(
                    [probe_re * re - probe_im * im, probe_re * im + probe_im * re], 0
                )
            )
        mid = left(get(0), jnp.concatenate(columns, 1))
        mid = jnp.concatenate(
            [
                jnp.concatenate(
                    [
                        mid[:rows, j * width : (j + 1) * width],
                        mid[rows:, j * width : (j + 1) * width],
                    ],
                    1,
                )
                for j in range(batch)
            ],
            0,
        )
        far = right(mid, get(across + 1))
        far_re = far[:, :width]
        far_im = far[:, width:]
        level = amplitude[:batch].reshape(batch * rows, width)
        keep = 1.0 - level * jnp.minimum(
            lax.rsqrt(far_re * far_re + far_im * far_im), 1.0 / floor
        )
        mid = right(jnp.concatenate([far_re * keep, far_im * keep], 1), get(across))
        mid = jnp.concatenate(
            [
                jnp.concatenate(
                    [
                        mid[j * rows : (j + 1) * rows, :width],
                        mid[j * rows : (j + 1) * rows, width:],
                    ],
                    0,
                )
                for j in range(batch)
            ],
            1,
        )
        back = left(get(1), mid)
        for j in range(batch):
            here, after, shift = spots[j]
            back_re = back[:rows, j * width : (j + 1) * width]
            back_im = back[rows:, j * width : (j + 1) * width]
            inside = lane >= shift
            for k, value in enumerate(
                (
                    probe_re * back_re + probe_im * back_im,
                    probe_re * back_im - probe_im * back_re,
                )
            ):
                value = pltpu.roll(value, shift, 1)
                band = slice(k * rows, (k + 1) * rows)
                grad[here, band] += jnp.where(inside, value, 0.0)
                grad[after, band] += jnp.where(inside, 0.0, value)

    if len(part_list) == n_parts:
        for part, amplitude in zip(part_list, measured):
            work(part, amplitude, scans)
    else:

        def step(index, carry):
            work(index, measured[0].at[index], scans)
            return carry

        lax.fori_loop(0, measured[0].shape[0], step, 0)


def gradient(meta, own, other, measured, part_list, scans, probe, dft_tables, floor, before):
    _, rows, width = probe.shape
    chunks = own.shape[0] * 2
    shape = (chunks, 2 * rows, width)
    carried = [] if before is None else [before]
    count = 3 + len(measured) + 2
    return pl.pallas_call(
        functools.partial(
            gradient_kernel, floor, tuple(part_list), len(measured), before is None, scans
        ),
        out_shape=jax.ShapeDtypeStruct(shape, jnp.float32),
        in_specs=[SMEM] + [VMEM] * (count - 1 + len(carried)),
        out_specs=VMEM,
        scratch_shapes=[pltpu.VMEM(shape, jnp.float32)],
        input_output_aliases={} if before is None else {count: 0},
        cost_estimate=COST,
        compiler_params=pltpu.CompilerParams(vmem_limit_bytes=24 * 2**20),
    )(meta, own, other, *measured, probe, dft_tables, *carried)


def illumination_kernel(meta, probe, power):
    chunks = power.shape[0]
    _, rows, width = probe.shape
    power[...] = jnp.zeros_like(power)
    lane = lax.broadcasted_iota(jnp.int32, (rows, width), 1)
    value = probe[0] * probe[0] + probe[1] * probe[1]

    group = 8

    def step(index, carry):
        for j in range(group):
            here, after, shift = place(meta, index * group + j, chunks, width)
            rolled = pltpu.roll(value, shift, 1)
            power[here] += jnp.where(lane >= shift, rolled, 0.0)
            power[after] += jnp.where(lane >= shift, 0.0, rolled)
        return carry

    lax.fori_loop(0, (meta.shape[0] - 2) // group, step, 0)


def illumination(meta, probe, chunks):
    _, rows, width = probe.shape
    return pl.pallas_call(
        illumination_kernel,
        out_shape=jax.ShapeDtypeStruct((chunks, rows, width), jnp.float32),
        in_specs=[SMEM, VMEM],
        out_specs=VMEM,
        cost_estimate=COST,
        compiler_params=LIMIT,
    )(meta, probe)


def update_kernel(n_pull, penalty, meta, own, *refs):
    pulls, refs = refs[:n_pull], refs[n_pull:]
    grad, grad_other, power, power_other, out = refs
    count = out.shape[0]
    rows = power.shape[1]
    ratio = ratio_of(penalty)
    swapped = meta[meta.shape[0] - 1] == 1
    for chunk in range(count):
        inverse = 1.0 / (power[chunk] + power_other[chunk] + ratio)
        for k in range(2):
            band = slice(k * rows, (k + 1) * rows)
            old = own[chunk, band]
            if n_pull == 1:
                pull = pulls[0][chunk, band]
            else:
                last = pulls[0].shape[0] - 2 + k
                pull = jnp.where(swapped, pulls[count - 1 - chunk][last], pulls[chunk][last])
            step = grad[chunk, band] + grad_other[chunk, band] + ratio * old - pull
            out[chunk, band] = old - step * inverse


def update(penalty, meta, own, pulls, grad, grad_other, power, power_other):
    count = power_other.shape[0]
    return pl.pallas_call(
        functools.partial(update_kernel, len(pulls)),
        out_shape=jax.ShapeDtypeStruct((count,) + grad.shape[1:], jnp.float32),
        in_specs=[SMEM, SMEM] + [VMEM] * (len(pulls) + 5),
        out_specs=VMEM,
        cost_estimate=COST,
        compiler_params=pltpu.CompilerParams(vmem_limit_bytes=16 * 2**20),
    )(penalty, meta, own, *pulls, grad, grad_other, power, power_other)


def sums_kernel(first, planes, column, row, block, folded, arrived):
    count, length = column.shape
    depth, lots = arrived.shape
    size = length // lots

    def copies(k):
        return [
            pltpu.make_async_copy(
                planes.at[first + k, pl.ds(lot * size, size)],
                block.at[k % depth, pl.ds(lot * size, size)],
                arrived.at[k % depth, lot],
            )
            for lot in range(lots)
        ]

    for k in range(min(depth, count)):
        for copy in copies(k):
            copy.start()
    for k in range(count):
        for copy in copies(k):
            copy.wait()
        down, row[k : k + 1] = sum_plane(block.at[k % depth], folded, folded.shape[1])
        column[k : k + 1] = down.sum(0, keepdims=True)
        if k + depth < count:
            for copy in copies(k + depth):
                copy.start()


def volume_sums(planes, first, count, lanes):
    _, length, _ = planes.shape
    out = jax.ShapeDtypeStruct((count, length), jnp.float32)
    depth = min(count, 3)
    return pl.pallas_call(
        functools.partial(sums_kernel, first),
        out_shape=(out, out),
        in_specs=[HBM],
        out_specs=(VMEM, VMEM),
        scratch_shapes=[
            pltpu.VMEM((depth, length, length), jnp.float32),
            pltpu.VMEM((length, lanes), jnp.float32),
            pltpu.SemaphoreType.DMA((depth, 4)),
        ],
        cost_estimate=COST,
        compiler_params=pltpu.CompilerParams(vmem_limit_bytes=34 * 2**20),
    )(planes)


def pack_kernel(n_parts, penalty, *refs):
    parts, (lagrange, psi, packed) = refs[:n_parts], refs[n_parts:]
    owners, planes, _ = packed.shape
    owned = planes // 2
    for k in range(2):
        value = parts[0][k]
        for part in parts[1:]:
            value = value + part[k]
        psi[k] = value
        value = value + lagrange[k] / ratio_of(penalty)
        packed[:, k * owned : (k + 1) * owned, :] = value.reshape(owners, owned, value.shape[1])


def slice_kernel(views, angles, lines, *refs):
    sums, out = refs[:-1], refs[-1]
    column = jnp.concatenate([ref[...] for ref in sums[::2]], 0)
    row = jnp.concatenate([ref[...] for ref in sums[1::2]], 0)
    total, planes, width = lines.shape
    tiles = total // views
    length = column.shape[1]
    scale = 1.0 / math.sqrt(length)
    rows_of = lax.broadcasted_iota(jnp.int32, (width, width), 0)
    columns_of = lax.broadcasted_iota(jnp.int32, (width, width), 1)
    mirror = jnp.where(rows_of + columns_of == width - 1, 1.0, 0.0).astype(jnp.float32)

    def flip(values):
        stacked = jnp.dot(
            jnp.concatenate(values, 0),
            mirror,
            precision=HIGHEST,
            preferred_element_type=jnp.float32,
        )
        return [stacked[k * planes : (k + 1) * planes] for k in range(len(values))]

    base = []
    plain = []
    turned = []
    count = []
    for parity, source in ((0, column), (1, row)):
        for t in range(tiles):
            base.append(source[:, t * width : (t + 1) * width] * scale)
            plain.append(
                sum(
                    jnp.where(angles[u] == parity, lines[u * tiles + t], 0.0)
                    for u in range(views)
                )
            )
            turned.append(
                sum(
                    jnp.where(angles[u] == parity + 2, lines[u * tiles + tiles - 1 - t], 0.0)
                    for u in range(views)
                )
            )
        count.append(
            sum(
                jnp.where((angles[u] == parity) | (angles[u] == parity + 2), 1.0, 0.0)
                for u in range(views)
            )
        )
    turned = flip(turned)
    misfit = [
        base[parity * tiles + t] * count[parity]
        - plain[parity * tiles + t]
        - turned[parity * tiles + t]
        for parity in range(2)
        for t in range(tiles)
    ]
    total_of = [
        jnp.sum(
            functools.reduce(jnp.add, misfit[parity * tiles : (parity + 1) * tiles]),
            1,
            keepdims=True,
        )
        * (1.0 / length)
        for parity in range(2)
    ]
    fresh = [
        base[parity * tiles + t]
        - (misfit[parity * tiles + t] + total_of[1 - parity]) * (1.0 / views)
        for parity in range(2)
        for t in range(tiles)
    ]
    reversed_fresh = flip(fresh)
    for u in range(views):
        for t in range(tiles):
            out[u * tiles + t] = jnp.where(
                angles[u] == 0,
                fresh[t],
                jnp.where(
                    angles[u] == 1,
                    fresh[tiles + t],
                    jnp.where(
                        angles[u] == 2,
                        reversed_fresh[tiles - 1 - t],
                        reversed_fresh[2 * tiles - 1 - t],
                    ),
                ),
            )


def final_kernel(penalty, packed, psi, lagrange, fresh, renewed):
    owners, planes, width = packed.shape
    owned = planes // 2
    for k in range(2):
        value = packed[:, k * owned : (k + 1) * owned, :].reshape(owners * owned, width)
        fresh[k] = value
        renewed[k] = lagrange[k] + ratio_of(penalty) * (psi[k] - value)


def ratio_of(penalty):
    return penalty[0].astype(jnp.float32) / penalty[1].astype(jnp.float32)


def unpack_kernel(n_parts, *refs):
    parts, (probe, own, starts, held) = refs[:n_parts], refs[n_parts:]
    held[...] = probe[...]
    size = own.shape[1]
    for index, part in enumerate(parts):
        own[index] = part[:size]
        starts[index] = part[size:]


def shards(
    objects, probe, positions, amplitudes, reproj_prev, multipliers, volume, angles, penalty
):
    tiles = lax.axis_size("tile")
    views = lax.axis_size("view")
    routes = Routes(views, tiles)
    half = routes.half
    _, _, rows, tile_width = objects.shape
    width = probe.shape[2]
    total = tile_width * tiles
    chunks = total // width
    scans = positions.shape[1]
    owned = volume.shape[1]
    floor = 0.25 / math.sqrt(scans * tiles * width // total)
    lagrange = multipliers[0]
    measured = amplitudes[0]
    core = lax.rem(lax.axis_index("view"), 2)
    swapped = (lax.axis_index("tile") == routes.hubs[1]).astype(jnp.int32)
    dft_tables = tables(rows, width)

    def as_chunks(parts):
        joined = jnp.stack(parts, 0)
        if tile_width == width:
            return joined
        joined = joined.reshape(chunks // 2, width // tile_width, 2 * rows, tile_width)
        return joined.transpose(0, 2, 1, 3).reshape(chunks // 2, 2 * rows, width)

    def as_tiles(own):
        if tile_width == width:
            return [own[part].reshape(2, rows, width) for part in range(half)]
        parts = own.reshape(chunks // 2, 2 * rows, width // tile_width, tile_width)
        parts = parts.transpose(0, 2, 1, 3).reshape(half, 2, rows, tile_width)
        return [parts[part] for part in range(half)]

    direct = tile_width == width and half <= 4 and scans <= width
    pad = -scans % tile_width
    starts = jnp.pad(positions.astype(jnp.float32), ((0, 0), (0, pad)))
    starts = starts.reshape(-1, tile_width)
    starts = jnp.pad(starts, ((0, -starts.shape[0] % 8), (0, 0)))
    message = jnp.concatenate([objects.reshape(2 * rows, tile_width), starts], 0)
    arrived = [send(message, routes.to_hub(part, False)) for part in range(half)]
    ratio = jnp.broadcast_to(penalty.astype(jnp.float32)[:, None], (2, tile_width))
    ratio = lax.optimization_barrier(ratio)
    pull = (ratio[0] / ratio[1]) * reproj_prev[0] - lagrange
    near = [part for part in range(half) if part % 2 == 0]
    far = [part for part in range(half) if part % 2 == 1]
    planes = volume.reshape(2 * owned, total, total)
    levels = [None] * half
    if direct:
        pull, _ = lax.optimization_barrier((pull, message))
        measured = jnp.concatenate([measured, pull], 0)
        early, _ = lax.optimization_barrier((planes, measured))
        sums = [volume_sums(early, 0, owned, 128)]
        arrived, measured, sums[0] = lax.optimization_barrier((arrived, measured, sums[0]))
        for part in near:
            levels[part] = send(measured, routes.to_hub(part, True))
    else:
        sums = [volume_sums(planes, 0, owned, 128), volume_sums(planes, owned, owned, 128)]
        for part in range(half):
            levels[part] = send(measured, routes.to_hub(part, True))

    if direct:
        strips = jax.ShapeDtypeStruct((half, 2 * rows, width), jnp.float32)
        own, starts, probe = pl.pallas_call(
            functools.partial(unpack_kernel, half),
            out_shape=(
                strips,
                jax.ShapeDtypeStruct((half, 8, width), jnp.float32),
                jax.ShapeDtypeStruct(probe.shape, jnp.float32),
            ),
            in_specs=[VMEM] * (half + 1),
            out_specs=(VMEM, VMEM, VMEM),
            cost_estimate=COST,
        compiler_params=LIMIT,
        )(*arrived, probe)
        starts = starts[:, 0, :scans]
        pulls = levels
    else:
        levels = [jnp.stack(levels, 0)]
        own = as_chunks([part[: 2 * rows] for part in arrived])
        pull = pull.reshape(2 * rows, tile_width)
        pulls = [as_chunks([send(pull, routes.to_hub(part, False)) for part in range(half)])]
        starts = jnp.stack([part[2 * rows :].reshape(-1)[:scans] for part in arrived], 0)
    if direct:
        measured, own = lax.optimization_barrier((measured, own))
        relayed = send(measured, routes.relays())
        levels[far[1]] = send(measured, routes.to_hub(far[1], True))
        hop = jnp.where(core == 0, 0, tiles - 1) == lax.axis_index("tile")
        levels[far[0]] = send(jnp.where(hop, relayed, measured), routes.relayed(far[0]))
    other = send(own, routes.cores())
    meta = jnp.concatenate(
        [
            starts.reshape(-1).astype(jnp.int32),
            (core * (chunks // 2))[None],
            swapped[None],
        ]
    )
    power = illumination(meta, probe, chunks)
    power_other = send(power[chunks // 2 :], routes.cores())

    if direct:
        other, power, power_other = lax.optimization_barrier((other, power, power_other))
    calls = [near, far[1:], far[:1], near + far] if direct else [range(half)] * ITERS
    grad = None

    def run(parts, grad):
        measured = [levels[part] for part in parts] if direct else levels
        return gradient(
            meta, own, other, measured, parts, scans, probe, dft_tables, floor, grad
        )

    for parts in calls[:-1]:
        grad = run(parts, grad)
    for sweep in range(ITERS):
        grad_other = send(grad[chunks // 2 :], routes.cores())
        mine = update(penalty, meta, own, pulls, grad, grad_other, power, power_other)
        if sweep + 1 < ITERS:
            own = mine
            other = send(own, routes.cores())
            grad = run(calls[-1], None)

    parts = [send(part, routes.from_hub(index)) for index, part in enumerate(as_tiles(mine))]
    if direct:
        late, _ = lax.optimization_barrier((planes, mine))
        sums.append(volume_sums(late, owned, owned, 128))
        parts, sums[1] = lax.optimization_barrier((parts, sums[1]))
    strip = jax.ShapeDtypeStruct((2, rows, tile_width), jnp.float32)
    owners = views * tiles
    exchanged = jax.ShapeDtypeStruct((owners, 2 * owned, tile_width), jnp.float32)
    psi, packed = pl.pallas_call(
        functools.partial(pack_kernel, len(parts)),
        out_shape=(strip, exchanged),
        in_specs=[SMEM] + [VMEM] * (len(parts) + 1),
        out_specs=(VMEM, VMEM),
        cost_estimate=COST,
        compiler_params=LIMIT,
    )(penalty, *parts, lagrange)
    lines = lax.all_to_all(packed, AXES, split_axis=0, concat_axis=0, tiled=True)
    fresh = pl.pallas_call(
        functools.partial(slice_kernel, views),
        out_shape=exchanged,
        in_specs=[SMEM] + [VMEM] * 5,
        out_specs=VMEM,
        cost_estimate=COST,
        compiler_params=LIMIT,
    )(angles, lines, *sums[0], *sums[1])
    fresh = lax.all_to_all(fresh, AXES, split_axis=0, concat_axis=0, tiled=True)
    fresh_strip, renewed = pl.pallas_call(
        final_kernel,
        out_shape=(strip, strip),
        in_specs=[SMEM] + [VMEM] * 3,
        out_specs=(VMEM, VMEM),
        cost_estimate=COST,
        compiler_params=LIMIT,
    )(penalty, fresh, psi, lagrange)
    return (fresh_strip[None], renewed[None])


def solution(mesh):
    return jax.shard_map(
        shards,
        mesh=mesh,
        in_specs=(
            P("view", None, None, "tile"),
            P(),
            P("view", "tile"),
            P("view", "tile", None, None),
            P("view", None, None, "tile"),
            P("view", None, None, "tile"),
            P(None, ("view", "tile"), None, None),
            P(),
            P(),
        ),
        out_specs=(P("view", None, None, "tile"), P("view", None, None, "tile")),
        check_vma=False,
    )
```

time: 148 us -> 123 us (0.83)
  starting transfers between devices: 44.2 us -> 22.8 us
  local copies, waits for them, and re-layouts: 15.2 us -> 0.31 us
  blocking collectives: 13.4 us -> 27 us
  Pallas kernels: 50.9 us -> 44.2 us
  other arithmetic: 2.61 us -> 6.51 us
  waiting for transfers between devices: 17.7 us -> 20.7 us
    all_to_all x0 -> x1, blocking collectives: none -> 17 us  [shards(): lax.all_to_all(packed, AXES, split_axis=0, concat_axis=0, tiled=True)]
    unnamed x32 -> x10, local copies, waits for them, and re-layouts: 13.7 us -> 0.03 us
    ppermute x24 -> x18, starting transfers between devices: 35.4 us -> 22.8 us  [send(): return lax.ppermute(value, AXES, pairs)]
    all_to_all x1 -> x0, starting transfers between devices: 8.88 us -> none  [shards(): lax.all_to_all(packed, AXES, split_axis=0, concat_axis=0, tiled=True)]
    pallas_call x3 -> x5, Pallas kernels: 19.1 us -> 15 us  [the longest x2 13.3 us: volume_sums(): pl.pallas_call(functools.partial(sums_kernel, first), out_shape=(out, out...]
    all_to_all x1, blocking collectives: 13.4 us -> 10 us  [shards(): fresh = lax.all_to_all(fresh, AXES, split_axis=0, concat_axis=0, tiled=True)]
    ppermute x24 -> x18, waiting for transfers between devices: 17.7 us -> 20.7 us  [send(): return lax.ppermute(value, AXES, pairs)]
    pallas_call x1, Pallas kernels: 3.63 us -> 1.48 us  [illumination(): pl.pallas_call(illumination_kernel, out_shape=jax.ShapeDtypeStruct((chunk...]
  transfers between devices with their start and end apart: 25 -> 18, of which waited for: 7 -> 3; matrix products, arithmetic and copies ran while one was open for 2% -> 4% of each run, Pallas kernels for 23% -> 20%
where the time goes in v2:
time: 123 us
  Pallas kernels  44.2 us (36%)
  blocking collectives  27 us (22%)
  starting transfers between devices  22.8 us (19%)
  waiting for transfers between devices  20.7 us (17%)
  other arithmetic  6.51 us (5%)
    pallas_call x4, Pallas kernels, gradient(): pl.pallas_call(functools.partial(gradient_kernel, floor, tuple(part_list)...  24.7 us
    ppermute x18, starting transfers between devices, send(): return lax.ppermute(value, AXES, pairs)  22.8 us
    ppermute x18, waiting for transfers between devices, send(): return lax.ppermute(value, AXES, pairs)  20.7 us
    all_to_all x1, blocking collectives, shards(): lax.all_to_all(packed, AXES, split_axis=0, concat_axis=0, tiled=True)  17 us
    pallas_call x2, Pallas kernels, volume_sums(): pl.pallas_call(functools.partial(sums_kernel, first), out_shape=(out, out...  13.3 us
    all_to_all x1, blocking collectives, shards(): fresh = lax.all_to_all(fresh, AXES, split_axis=0, concat_axis=0, tiled=True)  10 us
  transfers between devices with their start and end apart: 18, of which 3 were waited for; matrix products, arithmetic and copies ran while one was open for 4% of the time, Pallas kernels for 20%

profile of v2, /device:TPU:0, one launch (start us, length us, event | category | flops | bytes accessed | tf_op | source)
XLA Modules:
  0.0 122.6 jit_solution(3692625381806996264)
XLA Ops:
  0.6 0.0 copy-start
  0.6 0.0 copy-start.3
  0.7 0.0 copy-start.2
  0.7 0.7 convert_element_type.17
  1.4 0.9 select_maximum_fusion
  2.3 0.7 collective-permute-start.3
  3.0 0.7 collective-permute-start.2
  3.7 0.7 collective-permute-start.1
  4.3 6.2 %collective-permute-start = (f32[264,128]{1,0:T(8,128)S(1)}, f32[264,128]{1,0:T(8,128)S(1)}, u32[]{:S(2)}, u32[]{:S(2)}) collective-permute-start(f32[264,128]{1,0:T(8,128)S(1)} %select_maximum_fusion), channel_id=1, source_target_pairs={{0,2},{4,10},{8,5},{12,13},{16,18},{20,26},{24,21},{28,29}} | collective-permute-start | bytes 405512 | tf_op jit(solution)/shard_map/ppermute | solution.py:65
  10.5 0.7 convert_element_type.18
  11.2 0.1 broadcast_in_dim.22
  11.3 1.0 fusion
  12.3 1.9 %pad_maximum_fusion = f32[10,128,128]{2,1,0:T(8,128)} fusion(f32[2,128,128]{2,1,0:T(8,128)S(1)} %fusion, f32[8,128,128]{2,1,0:T(8,128)} %bitcast.23), kind=kLoop, calls=%fused_computation | loop fusion | flops 163840 | bytes 1310720 | tf_op jit(solution)/shard_map/concatenate | solution.py:555
  14.2 6.6 %shard_map.113 = (f32[4,1024]{1,0:T(4,128)S(1)}, f32[4,1024]{1,0:T(4,128)S(1)}) custom-call(f32[8,1024,1024]{2,1,0:T(8,128)} %bitcast.21), custom_call_target="tpu_custom_call" | custom-call | tf_op jit(solution)/shard_map/pallas_call | solution.py:368
  20.8 0.0 collective-permute-done.3.refs_3_
  20.9 0.0 collective-permute-done.2.refs_2_
  20.9 0.0 collective-permute-done.1.refs_1_
  20.9 0.0 collective-permute-done.refs_0_
  21.0 1.3 %collective-permute-start.5 = (f32[10,128,128]{2,1,0:T(8,128)}, f32[10,128,128]{2,1,0:T(8,128)}, u32[]{:S(2)}, u32[]{:S(2)}) collective-permute-start(f32[10,128,128]{2,1,0:T(8,128)} %pad_maximum_fusion), channel_id=1, source_target_pairs={{1,0},{14,15},{17,16},{30,31}} | collective-permute-start | bytes 1966088 | tf_op jit(solution)/shard_map/ppermute | solution.py:65
  22.3 0.7 collective-permute-start.8
  23.0 0.7 collective-permute-start.7
  23.7 3.2 %collective-permute-start.4 = (f32[10,128,128]{2,1,0:T(8,128)}, f32[10,128,128]{2,1,0:T(8,128)S(1)}, u32[]{:S(2)}, u32[]{:S(2)}) collective-permute-start(f32[10,128,128]{2,1,0:T(8,128)} %pad_maximum_fusion), channel_id=1, source_target_pairs={{0,2},{4,10},{11,5},{15,13},{16,18},{20,26},{27,21},{31,29}} | collective-permute-start | bytes 1966088 | tf_op jit(solution)/shard_map/ppermute | solution.py:65
  26.9 0.1 convert_element_type.20
  27.0 0.1 pad_add_fusion.meta
  27.0 1.5 %shard_map.115.refs_6_ = f32[8,128,128]{2,1,0:T(8,128)S(1)} custom-call(s32[34]{0:T(128)S(1)} %pad_add_fusion.meta, f32[2,128,128]{2,1,0:T(8,128)S(1)} %get-tuple-element.47.probe.refs_2_.refs_1_.refs_4_), custom_call_target="tpu_custom_call" | custom-call | tf_op jit(solution)/shard_map/pallas_call | solution.py:293
  28.5 0.7 collective-permute-start.10
  29.2 4.5 %collective-permute-done.5 = f32[10,128,128]{2,1,0:T(8,128)} collective-permute-done((f32[10,128,128]{2,1,0:T(8,128)}, f32[10,128,128]{2,1,0:T(8,128)}, u32[]{:S(2)}, u32[]{:S(2)}) %collective-permute-start.5) | collective-permute-done | bytes 655392 | tf_op jit(solution)/shard_map/ppermute | solution.py:65
  33.7 1.2 broadcast_select_fusion
  34.9 0.0 copy-start.1
  34.9 0.0 copy-start.4
  34.9 1.6 %collective-permute-start.6 = (f32[10,128,128]{2,1,0:T(8,128)S(1)}, f32[10,128,128]{2,1,0:T(8,128)S(1)}, u32[]{:S(2)}, u32[]{:S(2)}) collective-permute-start(f32[10,128,128]{2,1,0:T(8,128)S(1)} %broadcast_select_fusion), channel_id=1, source_target_pairs={{0,2},{5,10},{10,5},{15,13},{16,18},{21,26},{26,21},{31,29}} | collective-permute-start | bytes 1966088 | tf_op jit(solution)/shard_map/ppermute | solution.py:65
  36.5 0.0 collective-permute-done.10.refs_7_
  36.5 0.9 collective-permute-start.9
  37.4 0.0 collective-permute-done.9.other
  37.4 0.0 collective-permute-done.7.refs_1_.refs_2_
  37.4 1.9 %collective-permute-done.4.refs_0_ = f32[10,128,128]{2,1,0:T(8,128)S(1)} collective-permute-done((f32[10,128,128]{2,1,0:T(8,128)}, f32[10,128,128]{2,1,0:T(8,128)S(1)}, u32[]{:S(2)}, u32[]{:S(2)}) %collective-permute-start.4) | collective-permute-done | bytes 655392 | tf_op jit(solution)/shard_map/ppermute | solution.py:65
  39.3 6.1 %shard_map.116.refs_3_ = f32[8,256,128]{2,1,0:T(8,128)S(1)} custom-call(s32[34]{0:T(128)S(1)} %pad_add_fusion.meta, f32[4,256,128]{2,1,0:T(8,128)S(1)} %get-tuple-element.45.own, f32[4,256,128]{2,1,0:T(8,128)S(1)} %collective-permute-done.9.other, f32[10,128,128]{2,1,0:T(8,128)S(1)} %collective-permute-done.4.refs_0_, ...), custom_call_target="tpu_custom_call" | custom-call | tf_op jit(solution)/shard_map/pallas_call | solution.py:257
  45.5 0.0 collective-permute-done.8.refs_0_.refs_3_
  45.5 3.7 %shard_map.117.refs_3_ = f32[8,256,128]{2,1,0:T(8,128)S(1)} custom-call(s32[34]{0:T(128)S(1)} %pad_add_fusion.meta, f32[4,256,128]{2,1,0:T(8,128)S(1)} %get-tuple-element.45.own, f32[4,256,128]{2,1,0:T(8,128)S(1)} %collective-permute-done.9.other, f32[10,128,128]{2,1,0:T(8,128)S(1)} %collective-permute-done.8.refs_0_.refs_3_, ...), custom_call_target="tpu_custom_call", output_to_operand_aliasing={{}: (6, {})} | custom-call | tf_op jit(solution)/shard_map/pallas_call | solution.py:257
  49.2 0.0 collective-permute-done.6.refs_0_.refs_1_.refs_2_
  49.2 3.7 %shard_map.118.refs_4_ = f32[8,256,128]{2,1,0:T(8,128)S(1)} custom-call(s32[34]{0:T(128)S(1)} %pad_add_fusion.meta, f32[4,256,128]{2,1,0:T(8,128)S(1)} %get-tuple-element.45.own, f32[4,256,128]{2,1,0:T(8,128)S(1)} %collective-permute-done.9.other, f32[10,128,128]{2,1,0:T(8,128)S(1)} %collective-permute-done.6.refs_0_.refs_1_.refs_2_, ...), custom_call_target="tpu_custom_call", output_to_operand_aliasing={{}: (6, {})} | custom-call | tf_op jit(solution)/shard_map/pallas_call | solution.py:257
  53.0 0.7 collective-permute-start.11
  53.7 0.0 collective-permute-done.11.refs_5_
  53.7 0.8 shard_map.119.own
  54.6 0.9 collective-permute-start.12
  55.5 0.0 collective-permute-done.12.other
  55.5 11.2 %shard_map.120.refs_4_ = f32[8,256,128]{2,1,0:T(8,128)S(1)} custom-call(s32[34]{0:T(128)S(1)} %pad_add_fusion.meta, f32[4,256,128]{2,1,0:T(8,128)S(1)} %shard_map.119.own, f32[4,256,128]{2,1,0:T(8,128)S(1)} %collective-permute-done.12.other, f32[10,128,128]{2,1,0:T(8,128)S(1)} %collective-permute-done.4.refs_0_, ...), custom_call_target="tpu_custom_call" | custom-call | tf_op jit(solution)/shard_map/pallas_call | solution.py:257
  66.7 0.7 collective-permute-start.13
  67.4 0.0 collective-permute-done.13.refs_5_
  67.4 0.8 shard_map.121
  68.3 0.7 collective-permute-start.16
  69.0 0.7 collective-permute-start.17
  69.7 0.7 collective-permute-start.15
  70.3 1.3 %collective-permute-start.14 = (f32[2,128,128]{2,1,0:T(8,128)S(1)}, f32[2,128,128]{2,1,0:T(8,128)S(1)}, u32[]{:S(2)}, u32[]{:S(2)}) collective-permute-start(f32[2,128,128]{2,1,0:T(8,128)S(1)} %bitcast.25), channel_id=1, source_target_pairs={{2,0},{10,4},{5,8},{13,12},{18,16},{26,20},{21,24},{29,28}} | collective-permute-start | bytes 393224 | tf_op jit(solution)/shard_map/ppermute | solution.py:65
  71.6 6.6 %shard_map.122 = (f32[4,1024]{1,0:T(4,128)S(1)}, f32[4,1024]{1,0:T(4,128)S(1)}) custom-call(f32[8,1024,1024]{2,1,0:T(8,128)} %bitcast.22), custom_call_target="tpu_custom_call" | custom-call | tf_op jit(solution)/shard_map/pallas_call | solution.py:368
  78.3 0.0 collective-permute-done.16.refs_2_
  78.3 0.0 collective-permute-done.17.refs_3_
  78.3 0.0 collective-permute-done.15.refs_1_
  78.3 14.3 %collective-permute-done.14.refs_0_ = f32[2,128,128]{2,1,0:T(8,128)S(1)} collective-permute-done((f32[2,128,128]{2,1,0:T(8,128)S(1)}, f32[2,128,128]{2,1,0:T(8,128)S(1)}, u32[]{:S(2)}, u32[]{:S(2)}) %collective-permute-start.14) | collective-permute-done | bytes 131104 | tf_op jit(solution)/shard_map/ppermute | solution.py:65
  92.6 0.6 shard_map.123
  93.2 17.0 %all_to_all.10.lines = f32[32,8,128]{2,1,0:T(8,128)S(1)} all-to-all(f32[32,8,128]{2,1,0:T(8,128)S(1)} %get-tuple-element.58), channel_id=1, replica_groups=mesh['view'=4,'tile'=8] {'view','tile'}, dimensions={0} | all-to-all | bytes 262144 | tf_op jit(solution)/shard_map/all_to_all | solution.py:642
  110.2 1.1 shard_map.124
  111.3 10.0 %all_to_all.11.packed = f32[32,8,128]{2,1,0:T(8,128)S(1)} all-to-all(f32[32,8,128]{2,1,0:T(8,128)S(1)} %shard_map.124), channel_id=1, replica_groups=mesh['view'=4,'tile'=8] {'view','tile'}, dimensions={0} | all-to-all | bytes 262144 | tf_op jit(solution)/shard_map/all_to_all | solution.py:651
  121.3 1.3 %shard_map.125 = (f32[2,128,128]{2,1,0:T(8,128)}, f32[2,128,128]{2,1,0:T(8,128)}) custom-call(s32[2]{0:T(128)S(1)} %copy-done.3, f32[32,8,128]{2,1,0:T(8,128)S(1)} %all_to_all.11.packed, f32[2,128,128]{2,1,0:T(8,128)S(1)} %get-tuple-element.63.psi, f32[2,128,128]{2,1,0:T(8,128)S(1)} %bitcast.20), custom_call_target="tpu_custom_call" | custom-call | tf_op jit(solution)/shard_map/pallas_call | solution.py:652
  (12 shorter events, 0.2 us)
Async XLA Ops:
  0.6 38.7 %copy-start = (bf16[2,2,256,256]{3,2,1,0:T(8,128)(2,1)S(1)}, bf16[2,2,256,256]{3,2,1,0:T(8,128)(2,1)}, u32[]{:S(2)}) copy-start(bf16[2,2,256,256]{3,2,1,0:T(8,128)(2,1)} %constant.24.clone.refs_3_.refs_2_.refs_5_) | copy-start | bytes 1572868
  0.6 53.1 %copy-start.3 = (s32[2]{0:T(128)S(1)}, s32[2]{0:T(128)}, u32[]{:S(2)}) copy-start(s32[2]{0:T(128)} %penalty.7) | copy-start | bytes 28
  0.7 20.2 %copy-start.2 = (f32[2,128,128]{2,1,0:T(8,128)S(1)}, f32[2,128,128]{2,1,0:T(8,128)}, u32[]{:S(2)}) copy-start(f32[2,128,128]{2,1,0:T(8,128)} %refs_4_.1) | copy-start | bytes 393220
  2.3 18.5 %collective-permute-start.3 = (f32[264,128]{1,0:T(8,128)S(1)}, f32[264,128]{1,0:T(8,128)S(1)}, u32[]{:S(2)}, u32[]{:S(2)}) collective-permute-start(f32[264,128]{1,0:T(8,128)S(1)} %select_maximum_fusion), channel_id=1, source_target_pairs={{3,2},{7,10},{11,5},{15,13},{19,18},{23,26},{27,21},{31,29}} | collective-permute-start | bytes 405512 | tf_op jit(solution)/shard_map/ppermute | solution.py:65
  3.0 17.9 %collective-permute-start.2 = (f32[264,128]{1,0:T(8,128)S(1)}, f32[264,128]{1,0:T(8,128)S(1)}, u32[]{:S(2)}, u32[]{:S(2)}) collective-permute-start(f32[264,128]{1,0:T(8,128)S(1)} %select_maximum_fusion), channel_id=1, source_target_pairs={{2,2},{6,10},{10,5},{14,13},{18,18},{22,26},{26,21},{30,29}} | collective-permute-start | bytes 405512 | tf_op jit(solution)/shard_map/ppermute | solution.py:65
  3.7 17.2 %collective-permute-start.1 = (f32[264,128]{1,0:T(8,128)S(1)}, f32[264,128]{1,0:T(8,128)S(1)}, u32[]{:S(2)}, u32[]{:S(2)}) collective-permute-start(f32[264,128]{1,0:T(8,128)S(1)} %select_maximum_fusion), channel_id=1, source_target_pairs={{1,2},{5,10},{9,5},{13,13},{17,18},{21,26},{25,21},{29,29}} | collective-permute-start | bytes 405512 | tf_op jit(solution)/shard_map/ppermute | solution.py:65
  4.3 16.5 %collective-permute-start = (f32[264,128]{1,0:T(8,128)S(1)}, f32[264,128]{1,0:T(8,128)S(1)}, u32[]{:S(2)}, u32[]{:S(2)}) collective-permute-start(f32[264,128]{1,0:T(8,128)S(1)} %select_maximum_fusion), channel_id=1, source_target_pairs={{0,2},{4,10},{8,5},{12,13},{16,18},{20,26},{24,21},{28,29}} | collective-permute-start | bytes 405512 | tf_op jit(solution)/shard_map/ppermute | solution.py:65
  21.0 12.8 %collective-permute-start.5 = (f32[10,128,128]{2,1,0:T(8,128)}, f32[10,128,128]{2,1,0:T(8,128)}, u32[]{:S(2)}, u32[]{:S(2)}) collective-permute-start(f32[10,128,128]{2,1,0:T(8,128)} %pad_maximum_fusion), channel_id=1, source_target_pairs={{1,0},{14,15},{17,16},{30,31}} | collective-permute-start | bytes 1966088 | tf_op jit(solution)/shard_map/ppermute | solution.py:65
  22.3 23.2 %collective-permute-start.8 = (f32[10,128,128]{2,1,0:T(8,128)}, f32[10,128,128]{2,1,0:T(8,128)S(1)}, u32[]{:S(2)}, u32[]{:S(2)}) collective-permute-start(f32[10,128,128]{2,1,0:T(8,128)} %pad_maximum_fusion), channel_id=1, source_target_pairs={{3,2},{7,10},{8,5},{12,13},{19,18},{23,26},{24,21},{28,29}} | collective-permute-start | bytes 1966088 | tf_op jit(solution)/shard_map/ppermute | solution.py:65
  23.0 14.5 %collective-permute-start.7 = (f32[10,128,128]{2,1,0:T(8,128)}, f32[10,128,128]{2,1,0:T(8,128)S(1)}, u32[]{:S(2)}, u32[]{:S(2)}) collective-permute-start(f32[10,128,128]{2,1,0:T(8,128)} %pad_maximum_fusion), channel_id=1, source_target_pairs={{2,2},{6,10},{9,5},{13,13},{18,18},{22,26},{25,21},{29,29}} | collective-permute-start | bytes 1966088 | tf_op jit(solution)/shard_map/ppermute | solution.py:65
  23.7 15.6 %collective-permute-start.4 = (f32[10,128,128]{2,1,0:T(8,128)}, f32[10,128,128]{2,1,0:T(8,128)S(1)}, u32[]{:S(2)}, u32[]{:S(2)}) collective-permute-start(f32[10,128,128]{2,1,0:T(8,128)} %pad_maximum_fusion), channel_id=1, source_target_pairs={{0,2},{4,10},{11,5},{15,13},{16,18},{20,26},{27,21},{31,29}} | collective-permute-start | bytes 1966088 | tf_op jit(solution)/shard_map/ppermute | solution.py:65
  28.5 8.0 %collective-permute-start.10 = (f32[4,128,128]{2,1,0:T(8,128)S(1)}, f32[4,128,128]{2,1,0:T(8,128)S(1)}, u32[]{:S(2)}, u32[]{:S(2)}) collective-permute-start(f32[4,128,128]{2,1,0:T(8,128)S(1)} %slice.40), channel_id=1, source_target_pairs={{2,10},{5,13},{10,2},{13,5},{18,26},{21,29},{26,18},{29,21}} | collective-permute-start | bytes 786440 | tf_op jit(solution)/shard_map/ppermute | solution.py:65
  34.9 57.7 %copy-start.1 = (f32[1,2,128,128]{3,2,1,0:T(8,128)S(1)}, f32[1,2,128,128]{3,2,1,0:T(8,128)}, u32[]{:S(2)}) copy-start(f32[1,2,128,128]{3,2,1,0:T(8,128)} %param.15) | copy-start | bytes 393220
  34.9 75.3 %copy-start.4 = (s32[4]{0:T(128)S(1)}, s32[4]{0:T(128)}, u32[]{:S(2)}) copy-start(s32[4]{0:T(128)} %angles.1) | copy-start | bytes 52
  34.9 14.3 %collective-permute-start.6 = (f32[10,128,128]{2,1,0:T(8,128)S(1)}, f32[10,128,128]{2,1,0:T(8,128)S(1)}, u32[]{:S(2)}, u32[]{:S(2)}) collective-permute-start(f32[10,128,128]{2,1,0:T(8,128)S(1)} %broadcast_select_fusion), channel_id=1, source_target_pairs={{0,2},{5,10},{10,5},{15,13},{16,18},{21,26},{26,21},{31,29}} | collective-permute-start | bytes 1966088 | tf_op jit(solution)/shard_map/ppermute | solution.py:65
  36.5 0.9 collective-permute-start.9
  53.0 0.7 collective-permute-start.11
  54.6 0.9 collective-permute-start.12
  66.7 0.7 collective-permute-start.13
  68.3 10.0 %collective-permute-start.16 = (f32[2,128,128]{2,1,0:T(8,128)S(1)}, f32[2,128,128]{2,1,0:T(8,128)S(1)}, u32[]{:S(2)}, u32[]{:S(2)}) collective-permute-start(f32[2,128,128]{2,1,0:T(8,128)S(1)} %bitcast.28), channel_id=1, source_target_pairs={{2,2},{10,6},{5,10},{13,14},{18,18},{26,22},{21,26},{29,30}} | collective-permute-start | bytes 393224 | tf_op jit(solution)/shard_map/ppermute | solution.py:65
  69.0 9.3 %collective-permute-start.17 = (f32[2,128,128]{2,1,0:T(8,128)S(1)}, f32[2,128,128]{2,1,0:T(8,128)S(1)}, u32[]{:S(2)}, u32[]{:S(2)}) collective-permute-start(f32[2,128,128]{2,1,0:T(8,128)S(1)} %bitcast.27), channel_id=1, source_target_pairs={{2,3},{10,7},{5,11},{13,15},{18,19},{26,23},{21,27},{29,31}} | collective-permute-start | bytes 393224 | tf_op jit(solution)/shard_map/ppermute | solution.py:65
  69.7 8.6 %collective-permute-start.15 = (f32[2,128,128]{2,1,0:T(8,128)S(1)}, f32[2,128,128]{2,1,0:T(8,128)S(1)}, u32[]{:S(2)}, u32[]{:S(2)}) collective-permute-start(f32[2,128,128]{2,1,0:T(8,128)S(1)} %bitcast.26), channel_id=1, source_target_pairs={{2,1},{10,5},{5,9},{13,13},{18,17},{26,21},{21,25},{29,29}} | collective-permute-start | bytes 393224 | tf_op jit(solution)/shard_map/ppermute | solution.py:65
  70.3 22.3 %collective-permute-start.14 = (f32[2,128,128]{2,1,0:T(8,128)S(1)}, f32[2,128,128]{2,1,0:T(8,128)S(1)}, u32[]{:S(2)}, u32[]{:S(2)}) collective-permute-start(f32[2,128,128]{2,1,0:T(8,128)S(1)} %bitcast.25), channel_id=1, source_target_pairs={{2,0},{10,4},{5,8},{13,12},{18,16},{26,20},{21,24},{29,28}} | collective-permute-start | bytes 393224 | tf_op jit(solution)/shard_map/ppermute | solution.py:65

commit v3 on v2

--- a/solution.py
+++ b/solution.py
@@ -57,7 +57,7 @@
 
     def cores(self):
         return [
-            (self.at(v, t), self.at(v ^ 1, t)) for v in range(self.views) for t in self.hubs
+            (self.at(v, t), self.at(v ^ 1, t)) for v in range(self.views) for t in range(self.tiles)
         ]
 
 
@@ -550,11 +550,12 @@
     far = [part for part in range(half) if part % 2 == 1]
     planes = volume.reshape(2 * owned, total, total)
     levels = [None] * half
+    cuts = (3 * owned // 4, 3 * owned // 2)
     if direct:
         pull, _ = lax.optimization_barrier((pull, message))
         measured = jnp.concatenate([measured, pull], 0)
         early, _ = lax.optimization_barrier((planes, measured))
-        sums = [volume_sums(early, 0, owned, 128)]
+        sums = [volume_sums(early, 0, cuts[0], 128)]
         arrived, measured, sums[0] = lax.optimization_barrier((arrived, measured, sums[0]))
         for part in near:
             levels[part] = send(measured, routes.to_hub(part, True))
@@ -587,10 +588,7 @@
         starts = jnp.stack([part[2 * rows :].reshape(-1)[:scans] for part in arrived], 0)
     if direct:
         measured, own = lax.optimization_barrier((measured, own))
-        relayed = send(measured, routes.relays())
         levels[far[1]] = send(measured, routes.to_hub(far[1], True))
-        hop = jnp.where(core == 0, 0, tiles - 1) == lax.axis_index("tile")
-        levels[far[0]] = send(jnp.where(hop, relayed, measured), routes.relayed(far[0]))
     other = send(own, routes.cores())
     meta = jnp.concatenate(
         [
@@ -600,11 +598,19 @@
         ]
     )
     power = illumination(meta, probe, chunks)
+    if direct:
+        relayed = send(measured, routes.relays())
+        hop = jnp.where(core == 0, 0, tiles - 1) == lax.axis_index("tile")
+        levels[far[0]] = send(jnp.where(hop, relayed, measured), routes.relayed(far[0]))
     power_other = send(power[chunks // 2 :], routes.cores())
 
     if direct:
-        other, power, power_other = lax.optimization_barrier((other, power, power_other))
-    calls = [near, far[1:], far[:1], near + far] if direct else [range(half)] * ITERS
+        middle, _ = lax.optimization_barrier((planes, own))
+        sums.append(volume_sums(middle, cuts[0], cuts[1] - cuts[0], 128))
+        other, power, power_other, sums[1] = lax.optimization_barrier(
+            (other, power, power_other, sums[1])
+        )
+    calls = [near, far[1:] + far[:1], near + far] if direct else [range(half)] * ITERS
     grad = None
 
     def run(parts, grad):
@@ -626,8 +632,8 @@
     parts = [send(part, routes.from_hub(index)) for index, part in enumerate(as_tiles(mine))]
     if direct:
         late, _ = lax.optimization_barrier((planes, mine))
-        sums.append(volume_sums(late, owned, owned, 128))
-        parts, sums[1] = lax.optimization_barrier((parts, sums[1]))
+        sums.append(volume_sums(late, cuts[1], 2 * owned - cuts[1], 128))
+        parts, sums[2] = lax.optimization_barrier((parts, sums[2]))
     strip = jax.ShapeDtypeStruct((2, rows, tile_width), jnp.float32)
     owners = views * tiles
     exchanged = jax.ShapeDtypeStruct((owners, 2 * owned, tile_width), jnp.float32)
@@ -643,11 +649,11 @@
     fresh = pl.pallas_call(
         functools.partial(slice_kernel, views),
         out_shape=exchanged,
-        in_specs=[SMEM] + [VMEM] * 5,
+        in_specs=[SMEM] + [VMEM] * (1 + 2 * len(sums)),
         out_specs=VMEM,
         cost_estimate=COST,
         compiler_params=LIMIT,
-    )(angles, lines, *sums[0], *sums[1])
+    )(angles, lines, *[line for pair in sums for line in pair])
     fresh = lax.all_to_all(fresh, AXES, split_axis=0, concat_axis=0, tiled=True)
     fresh_strip, renewed = pl.pallas_call(
         final_kernel,

time: 123 us -> 113 us (0.919)
  waiting for transfers between devices: 20.7 us -> 12.9 us
  blocking collectives: 27 us -> 22.7 us
  starting transfers between devices: 22.8 us -> 24.2 us
    ppermute x18, waiting for transfers between devices: 20.7 us -> 12.9 us  [send(): return lax.ppermute(value, AXES, pairs)]
    all_to_all x1, blocking collectives: 17 us -> 12.7 us  [shards(): lax.all_to_all(packed, AXES, split_axis=0, concat_axis=0, tiled=True)]
    ppermute x18, starting transfers between devices: 22.8 us -> 24.2 us  [send(): return lax.ppermute(value, AXES, pairs)]
    pallas_call x2 -> x3, Pallas kernels: 13.3 us -> 14.7 us  [volume_sums(): pl.pallas_call(functools.partial(sums_kernel, first), out_shape=(out, out...]
    pallas_call x4 -> x3, Pallas kernels: 24.7 us -> 23.8 us  [gradient(): pl.pallas_call(functools.partial(gradient_kernel, floor, tuple(part_list)...]
  transfers between devices with their start and end apart: 18 -> 18, of which waited for: 3 -> 6; matrix products, arithmetic and copies ran while one was open for 4% -> 4% of each run, Pallas kernels for 20% -> 20%
where the time goes in v3:
time: 113 us; the launch traced here: 112 us
  Pallas kernels  44.6 us (39%)
  starting transfers between devices  24.2 us (21%)
  blocking collectives  22.7 us (20%)
  waiting for transfers between devices  12.9 us (11%)
  other arithmetic  6.47 us (6%)
    ppermute x18, starting transfers between devices, send(): return lax.ppermute(value, AXES, pairs)  24.2 us
    pallas_call x3, Pallas kernels, gradient(): pl.pallas_call(functools.partial(gradient_kernel, floor, tuple(part_list)...  23.8 us
    pallas_call x3, Pallas kernels, volume_sums(): pl.pallas_call(functools.partial(sums_kernel, first), out_shape=(out, out...  14.7 us
    ppermute x18, waiting for transfers between devices, send(): return lax.ppermute(value, AXES, pairs)  12.9 us
    all_to_all x1, blocking collectives, shards(): lax.all_to_all(packed, AXES, split_axis=0, concat_axis=0, tiled=True)  12.7 us
    all_to_all x1, blocking collectives, shards(): fresh = lax.all_to_all(fresh, AXES, split_axis=0, concat_axis=0, tiled=True)  10 us
  transfers between devices with their start and end apart: 18, of which 6 were waited for; matrix products, arithmetic and copies ran while one was open for 4% of the time, Pallas kernels for 20%

profile of v3, /device:TPU:0, one launch (start us, length us, event | category | flops | bytes accessed | tf_op | source)
XLA Modules:
  0.0 112.2 jit_solution(8546002864165173689)
XLA Ops:
  0.6 0.0 copy-start.2
  0.6 0.7 convert_element_type.17
  1.3 0.9 select_maximum_fusion
  2.2 0.7 collective-permute-start.3
  2.9 0.7 collective-permute-start.2
  3.6 0.7 collective-permute-start.1
  4.3 6.2 %collective-permute-start = (f32[264,128]{1,0:T(8,128)S(1)}, f32[264,128]{1,0:T(8,128)S(1)}, u32[]{:S(2)}, u32[]{:S(2)}) collective-permute-start(f32[264,128]{1,0:T(8,128)S(1)} %select_maximum_fusion), channel_id=1, source_target_pairs={{0,2},{4,10},{8,5},{12,13},{16,18},{20,26},{24,21},{28,29}} | collective-permute-start | bytes 405512 | tf_op jit(solution)/shard_map/ppermute | solution.py:65
  10.5 0.7 convert_element_type.18
  11.1 0.1 broadcast_in_dim.22
  11.2 1.0 fusion
  12.2 1.9 %pad_maximum_fusion = f32[10,128,128]{2,1,0:T(8,128)} fusion(f32[2,128,128]{2,1,0:T(8,128)S(1)} %fusion, f32[8,128,128]{2,1,0:T(8,128)} %bitcast.24), kind=kLoop, calls=%fused_computation | loop fusion | flops 163840 | bytes 1310720 | tf_op jit(solution)/shard_map/concatenate | solution.py:556
  14.2 5.3 %shard_map.113 = (f32[3,1024]{1,0:T(4,128)S(1)}, f32[3,1024]{1,0:T(4,128)S(1)}) custom-call(f32[8,1024,1024]{2,1,0:T(8,128)} %bitcast.21), custom_call_target="tpu_custom_call" | custom-call | tf_op jit(solution)/shard_map/pallas_call | solution.py:368
  19.4 0.0 collective-permute-done.3.refs_3_
  19.4 0.0 collective-permute-done.2.refs_2_
  19.4 0.0 collective-permute-done.1.refs_1_
  19.5 0.0 collective-permute-done.refs_0_
  19.5 0.0 copy-done.2
  19.5 1.3 %collective-permute-start.5 = (f32[10,128,128]{2,1,0:T(8,128)}, f32[10,128,128]{2,1,0:T(8,128)}, u32[]{:S(2)}, u32[]{:S(2)}) collective-permute-start(f32[10,128,128]{2,1,0:T(8,128)} %pad_maximum_fusion), channel_id=1, source_target_pairs={{1,0},{14,15},{17,16},{30,31}} | collective-permute-start | bytes 1966088 | tf_op jit(solution)/shard_map/ppermute | solution.py:65
  20.8 0.7 collective-permute-start.8
  21.6 0.7 collective-permute-start.7
  22.3 3.2 %collective-permute-start.4 = (f32[10,128,128]{2,1,0:T(8,128)}, f32[10,128,128]{2,1,0:T(8,128)S(1)}, u32[]{:S(2)}, u32[]{:S(2)}) collective-permute-start(f32[10,128,128]{2,1,0:T(8,128)} %pad_maximum_fusion), channel_id=1, source_target_pairs={{0,2},{4,10},{11,5},{15,13},{16,18},{20,26},{27,21},{31,29}} | collective-permute-start | bytes 1966088 | tf_op jit(solution)/shard_map/ppermute | solution.py:65
  25.4 0.1 convert_element_type.20
  25.5 0.1 pad_add_fusion.meta
  25.6 1.5 %shard_map.115.refs_6_ = f32[8,128,128]{2,1,0:T(8,128)S(1)} custom-call(s32[34]{0:T(128)S(1)} %pad_add_fusion.meta, f32[2,128,128]{2,1,0:T(8,128)S(1)} %get-tuple-element.52.probe.refs_2_.refs_4_), custom_call_target="tpu_custom_call" | custom-call | tf_op jit(solution)/shard_map/pallas_call | solution.py:293
  27.1 5.0 %collective-permute-start.10 = (f32[4,128,128]{2,1,0:T(8,128)S(1)}, f32[4,128,128]{2,1,0:T(8,128)S(1)}, u32[]{:S(2)}, u32[]{:S(2)}) collective-permute-start(f32[4,128,128]{2,1,0:T(8,128)S(1)} %slice.40), channel_id=1, source_target_pairs={{0,8},{1,9},{2,10},{3,11},{4,12},{5,13},{6,14},{7,15},{8,0},{9,1},... | collective-permute-start | bytes 786440 | tf_op jit(solution)/shard_map/ppermute | solution.py:65
  32.1 0.2 collective-permute-done.5
  32.3 1.2 %broadcast_select_fusion = f32[10,128,128]{2,1,0:T(8,128)S(1)} fusion(f32[10,128,128]{2,1,0:T(8,128)} %collective-permute-done.5, f32[10,128,128]{2,1,0:T(8,128)} %pad_maximum_fusion, pred[]{:T(512)S(6)} %eq.11), kind=kLoop, calls=%fused_computation.1 | loop fusion | flops 163840 | bytes 1966081 | tf_op jit(solution)/shard_map/jit(_where)/select_n | solution.py:604
  33.5 1.3 %collective-permute-start.6 = (f32[10,128,128]{2,1,0:T(8,128)S(1)}, f32[10,128,128]{2,1,0:T(8,128)S(1)}, u32[]{:S(2)}, u32[]{:S(2)}) collective-permute-start(f32[10,128,128]{2,1,0:T(8,128)S(1)} %broadcast_select_fusion), channel_id=1, source_target_pairs={{0,2},{5,10},{10,5},{15,13},{16,18},{21,26},{26,21},{31,29}} | collective-permute-start | bytes 1966088 | tf_op jit(solution)/shard_map/ppermute | solution.py:65
  34.8 0.0 collective-permute-done.10.refs_7_
  34.8 0.1 collective-permute-start.9
  34.9 5.4 %shard_map.116 = (f32[3,1024]{1,0:T(4,128)S(1)}, f32[3,1024]{1,0:T(4,128)S(1)}) custom-call(f32[8,1024,1024]{2,1,0:T(8,128)} %bitcast.22), custom_call_target="tpu_custom_call" | custom-call | tf_op jit(solution)/shard_map/pallas_call | solution.py:368
  40.3 0.0 copy-start.1
  40.3 0.0 copy-start.4
  40.4 0.0 collective-permute-done.9.other
  40.4 0.0 collective-permute-done.7.refs_1_.refs_2_
  40.4 0.0 collective-permute-done.4.refs_0_
  40.4 0.0 copy-done
  40.4 6.1 %shard_map.117.refs_4_ = f32[8,256,128]{2,1,0:T(8,128)S(1)} custom-call(s32[34]{0:T(128)S(1)} %pad_add_fusion.meta, f32[4,256,128]{2,1,0:T(8,128)S(1)} %get-tuple-element.50.own, f32[4,256,128]{2,1,0:T(8,128)S(1)} %collective-permute-done.9.other, f32[10,128,128]{2,1,0:T(8,128)S(1)} %collective-permute-done.4.refs_0_, ...), custom_call_target="tpu_custom_call" | custom-call | tf_op jit(solution)/shard_map/pallas_call | solution.py:257
  46.5 0.0 collective-permute-done.8.refs_0_.refs_3_
  46.5 1.2 %collective-permute-done.6.refs_1_.refs_2_ = f32[10,128,128]{2,1,0:T(8,128)S(1)} collective-permute-done((f32[10,128,128]{2,1,0:T(8,128)S(1)}, f32[10,128,128]{2,1,0:T(8,128)S(1)}, u32[]{:S(2)}, u32[]{:S(2)}) %collective-permute-start.6) | collective-permute-done | bytes 655392 | tf_op jit(solution)/shard_map/ppermute | solution.py:65
  47.7 6.3 %shard_map.118.refs_4_ = f32[8,256,128]{2,1,0:T(8,128)S(1)} custom-call(s32[34]{0:T(128)S(1)} %pad_add_fusion.meta, f32[4,256,128]{2,1,0:T(8,128)S(1)} %get-tuple-element.50.own, f32[4,256,128]{2,1,0:T(8,128)S(1)} %collective-permute-done.9.other, f32[10,128,128]{2,1,0:T(8,128)S(1)} %collective-permute-done.8.refs_0_.refs_3_, ...), custom_call_target="tpu_custom_call", output_to_operand_aliasing={{}: (7, {})} | custom-call | tf_op jit(solution)/shard_map/pallas_call | solution.py:257
  54.0 0.1 collective-permute-start.11
  54.1 1.9 %collective-permute-done.11.refs_5_ = f32[4,256,128]{2,1,0:T(8,128)S(1)} collective-permute-done((f32[4,256,128]{2,1,0:T(8,128)S(1)}, f32[4,256,128]{2,1,0:T(8,128)S(1)}, u32[]{:S(2)}, u32[]{:S(2)}) %collective-permute-start.11) | collective-permute-done | bytes 524320 | tf_op jit(solution)/shard_map/ppermute | solution.py:65
  56.0 0.8 shard_map.119.own
  56.8 0.2 collective-permute-start.12
  57.0 1.8 %collective-permute-done.12.other = f32[4,256,128]{2,1,0:T(8,128)S(1)} collective-permute-done((f32[4,256,128]{2,1,0:T(8,128)S(1)}, f32[4,256,128]{2,1,0:T(8,128)S(1)}, u32[]{:S(2)}, u32[]{:S(2)}) %collective-permute-start.12) | collective-permute-done | bytes 524320 | tf_op jit(solution)/shard_map/ppermute | solution.py:65
  58.8 11.4 %shard_map.120.refs_4_ = f32[8,256,128]{2,1,0:T(8,128)S(1)} custom-call(s32[34]{0:T(128)S(1)} %pad_add_fusion.meta, f32[4,256,128]{2,1,0:T(8,128)S(1)} %shard_map.119.own, f32[4,256,128]{2,1,0:T(8,128)S(1)} %collective-permute-done.12.other, f32[10,128,128]{2,1,0:T(8,128)S(1)} %collective-permute-done.4.refs_0_, ...), custom_call_target="tpu_custom_call" | custom-call | tf_op jit(solution)/shard_map/pallas_call | solution.py:257
  70.2 0.2 collective-permute-start.13
  70.5 1.8 %collective-permute-done.13.refs_5_ = f32[4,256,128]{2,1,0:T(8,128)S(1)} collective-permute-done((f32[4,256,128]{2,1,0:T(8,128)S(1)}, f32[4,256,128]{2,1,0:T(8,128)S(1)}, u32[]{:S(2)}, u32[]{:S(2)}) %collective-permute-start.13) | collective-permute-done | bytes 524320 | tf_op jit(solution)/shard_map/ppermute | solution.py:65
  72.2 0.8 shard_map.121
  73.1 0.7 collective-permute-start.16
  73.8 0.7 collective-permute-start.17
  74.5 0.7 collective-permute-start.15
  75.1 1.3 %collective-permute-start.14 = (f32[2,128,128]{2,1,0:T(8,128)S(1)}, f32[2,128,128]{2,1,0:T(8,128)S(1)}, u32[]{:S(2)}, u32[]{:S(2)}) collective-permute-start(f32[2,128,128]{2,1,0:T(8,128)S(1)} %bitcast.26), channel_id=1, source_target_pairs={{2,0},{10,4},{5,8},{13,12},{18,16},{26,20},{21,24},{29,28}} | collective-permute-start | bytes 393224 | tf_op jit(solution)/shard_map/ppermute | solution.py:65
  76.4 4.0 %shard_map.122 = (f32[2,1024]{1,0:T(2,128)S(1)}, f32[2,1024]{1,0:T(2,128)S(1)}) custom-call(f32[8,1024,1024]{2,1,0:T(8,128)} %bitcast.23), custom_call_target="tpu_custom_call" | custom-call | tf_op jit(solution)/shard_map/pallas_call | solution.py:368
  80.4 0.0 collective-permute-done.16.refs_2_
  80.4 0.0 collective-permute-done.17.refs_3_
  80.5 0.0 collective-permute-done.15.refs_1_
  80.5 6.0 %collective-permute-done.14.refs_0_ = f32[2,128,128]{2,1,0:T(8,128)S(1)} collective-permute-done((f32[2,128,128]{2,1,0:T(8,128)S(1)}, f32[2,128,128]{2,1,0:T(8,128)S(1)}, u32[]{:S(2)}, u32[]{:S(2)}) %collective-permute-start.14) | collective-permute-done | bytes 131104 | tf_op jit(solution)/shard_map/ppermute | solution.py:65
  86.5 0.6 shard_map.123
  87.1 12.7 %all_to_all.10.lines = f32[32,8,128]{2,1,0:T(8,128)S(1)} all-to-all(f32[32,8,128]{2,1,0:T(8,128)S(1)} %get-tuple-element.66), channel_id=1, replica_groups=mesh['view'=4,'tile'=8] {'view','tile'}, dimensions={0} | all-to-all | bytes 262144 | tf_op jit(solution)/shard_map/all_to_all | solution.py:648
  99.8 1.1 shard_map.124
  100.9 10.0 %all_to_all.11.packed = f32[32,8,128]{2,1,0:T(8,128)S(1)} all-to-all(f32[32,8,128]{2,1,0:T(8,128)S(1)} %shard_map.124), channel_id=1, replica_groups=mesh['view'=4,'tile'=8] {'view','tile'}, dimensions={0} | all-to-all | bytes 262144 | tf_op jit(solution)/shard_map/all_to_all | solution.py:657
  111.0 1.3 %shard_map.125 = (f32[2,128,128]{2,1,0:T(8,128)}, f32[2,128,128]{2,1,0:T(8,128)}) custom-call(s32[2]{0:T(128)S(1)} %copy-done.3, f32[32,8,128]{2,1,0:T(8,128)S(1)} %all_to_all.11.packed, f32[2,128,128]{2,1,0:T(8,128)S(1)} %get-tuple-element.73.psi, f32[2,128,128]{2,1,0:T(8,128)S(1)} %bitcast.20), custom_call_target="tpu_custom_call" | custom-call | tf_op jit(solution)/shard_map/pallas_call | solution.py:658
  (12 shorter events, 0.2 us)
Async XLA Ops:
  0.6 18.8 %copy-start.2 = (f32[2,128,128]{2,1,0:T(8,128)S(1)}, f32[2,128,128]{2,1,0:T(8,128)}, u32[]{:S(2)}) copy-start(f32[2,128,128]{2,1,0:T(8,128)} %refs_4_.1) | copy-start | bytes 393220
  2.2 17.2 %collective-permute-start.3 = (f32[264,128]{1,0:T(8,128)S(1)}, f32[264,128]{1,0:T(8,128)S(1)}, u32[]{:S(2)}, u32[]{:S(2)}) collective-permute-start(f32[264,128]{1,0:T(8,128)S(1)} %select_maximum_fusion), channel_id=1, source_target_pairs={{3,2},{7,10},{11,5},{15,13},{19,18},{23,26},{27,21},{31,29}} | collective-permute-start | bytes 405512 | tf_op jit(solution)/shard_map/ppermute | solution.py:65
  2.9 16.5 %collective-permute-start.2 = (f32[264,128]{1,0:T(8,128)S(1)}, f32[264,128]{1,0:T(8,128)S(1)}, u32[]{:S(2)}, u32[]{:S(2)}) collective-permute-start(f32[264,128]{1,0:T(8,128)S(1)} %select_maximum_fusion), channel_id=1, source_target_pairs={{2,2},{6,10},{10,5},{14,13},{18,18},{22,26},{26,21},{30,29}} | collective-permute-start | bytes 405512 | tf_op jit(solution)/shard_map/ppermute | solution.py:65
  3.6 15.8 %collective-permute-start.1 = (f32[264,128]{1,0:T(8,128)S(1)}, f32[264,128]{1,0:T(8,128)S(1)}, u32[]{:S(2)}, u32[]{:S(2)}) collective-permute-start(f32[264,128]{1,0:T(8,128)S(1)} %select_maximum_fusion), channel_id=1, source_target_pairs={{1,2},{5,10},{9,5},{13,13},{17,18},{21,26},{25,21},{29,29}} | collective-permute-start | bytes 405512 | tf_op jit(solution)/shard_map/ppermute | solution.py:65
  4.3 15.2 %collective-permute-start = (f32[264,128]{1,0:T(8,128)S(1)}, f32[264,128]{1,0:T(8,128)S(1)}, u32[]{:S(2)}, u32[]{:S(2)}) collective-permute-start(f32[264,128]{1,0:T(8,128)S(1)} %select_maximum_fusion), channel_id=1, source_target_pairs={{0,2},{4,10},{8,5},{12,13},{16,18},{20,26},{24,21},{28,29}} | collective-permute-start | bytes 405512 | tf_op jit(solution)/shard_map/ppermute | solution.py:65
  14.1 26.2 %copy-start = (bf16[2,2,256,256]{3,2,1,0:T(8,128)(2,1)S(1)}, bf16[2,2,256,256]{3,2,1,0:T(8,128)(2,1)}, u32[]{:S(2)}) copy-start(bf16[2,2,256,256]{3,2,1,0:T(8,128)(2,1)} %constant.24.clone.refs_3_.refs_5_) | copy-start | bytes 1572868
  14.1 41.9 %copy-start.3 = (s32[2]{0:T(128)S(1)}, s32[2]{0:T(128)}, u32[]{:S(2)}) copy-start(s32[2]{0:T(128)} %penalty.7) | copy-start | bytes 28
  19.5 12.8 %collective-permute-start.5 = (f32[10,128,128]{2,1,0:T(8,128)}, f32[10,128,128]{2,1,0:T(8,128)}, u32[]{:S(2)}, u32[]{:S(2)}) collective-permute-start(f32[10,128,128]{2,1,0:T(8,128)} %pad_maximum_fusion), channel_id=1, source_target_pairs={{1,0},{14,15},{17,16},{30,31}} | collective-permute-start | bytes 1966088 | tf_op jit(solution)/shard_map/ppermute | solution.py:65
  20.8 25.7 %collective-permute-start.8 = (f32[10,128,128]{2,1,0:T(8,128)}, f32[10,128,128]{2,1,0:T(8,128)S(1)}, u32[]{:S(2)}, u32[]{:S(2)}) collective-permute-start(f32[10,128,128]{2,1,0:T(8,128)} %pad_maximum_fusion), channel_id=1, source_target_pairs={{3,2},{7,10},{8,5},{12,13},{19,18},{23,26},{24,21},{28,29}} | collective-permute-start | bytes 1966088 | tf_op jit(solution)/shard_map/ppermute | solution.py:65
  21.6 18.8 %collective-permute-start.7 = (f32[10,128,128]{2,1,0:T(8,128)}, f32[10,128,128]{2,1,0:T(8,128)S(1)}, u32[]{:S(2)}, u32[]{:S(2)}) collective-permute-start(f32[10,128,128]{2,1,0:T(8,128)} %pad_maximum_fusion), channel_id=1, source_target_pairs={{2,2},{6,10},{9,5},{13,13},{18,18},{22,26},{25,21},{29,29}} | collective-permute-start | bytes 1966088 | tf_op jit(solution)/shard_map/ppermute | solution.py:65
  22.3 18.1 %collective-permute-start.4 = (f32[10,128,128]{2,1,0:T(8,128)}, f32[10,128,128]{2,1,0:T(8,128)S(1)}, u32[]{:S(2)}, u32[]{:S(2)}) collective-permute-start(f32[10,128,128]{2,1,0:T(8,128)} %pad_maximum_fusion), channel_id=1, source_target_pairs={{0,2},{4,10},{11,5},{15,13},{16,18},{20,26},{27,21},{31,29}} | collective-permute-start | bytes 1966088 | tf_op jit(solution)/shard_map/ppermute | solution.py:65
  27.1 7.7 %collective-permute-start.10 = (f32[4,128,128]{2,1,0:T(8,128)S(1)}, f32[4,128,128]{2,1,0:T(8,128)S(1)}, u32[]{:S(2)}, u32[]{:S(2)}) collective-permute-start(f32[4,128,128]{2,1,0:T(8,128)S(1)} %slice.40), channel_id=1, source_target_pairs={{0,8},{1,9},{2,10},{3,11},{4,12},{5,13},{6,14},{7,15},{8,0},{9,1},... | collective-permute-start | bytes 786440 | tf_op jit(solution)/shard_map/ppermute | solution.py:65
  33.5 14.2 %collective-permute-start.6 = (f32[10,128,128]{2,1,0:T(8,128)S(1)}, f32[10,128,128]{2,1,0:T(8,128)S(1)}, u32[]{:S(2)}, u32[]{:S(2)}) collective-permute-start(f32[10,128,128]{2,1,0:T(8,128)S(1)} %broadcast_select_fusion), channel_id=1, source_target_pairs={{0,2},{5,10},{10,5},{15,13},{16,18},{21,26},{26,21},{31,29}} | collective-permute-start | bytes 1966088 | tf_op jit(solution)/shard_map/ppermute | solution.py:65
  34.8 5.5 %collective-permute-start.9 = (f32[4,256,128]{2,1,0:T(8,128)S(1)}, f32[4,256,128]{2,1,0:T(8,128)S(1)}, u32[]{:S(2)}, u32[]{:S(2)}) collective-permute-start(f32[4,256,128]{2,1,0:T(8,128)S(1)} %get-tuple-element.50.own), channel_id=1, source_target_pairs={{0,8},{1,9},{2,10},{3,11},{4,12},{5,13},{6,14},{7,15},{8,0},{9,1},... | collective-permute-start | bytes 1572872 | tf_op jit(solution)/shard_map/ppermute | solution.py:65
  40.3 46.1 %copy-start.1 = (f32[1,2,128,128]{3,2,1,0:T(8,128)S(1)}, f32[1,2,128,128]{3,2,1,0:T(8,128)}, u32[]{:S(2)}) copy-start(f32[1,2,128,128]{3,2,1,0:T(8,128)} %param.15) | copy-start | bytes 393220
  40.3 59.5 %copy-start.4 = (s32[4]{0:T(128)S(1)}, s32[4]{0:T(128)}, u32[]{:S(2)}) copy-start(s32[4]{0:T(128)} %angles.1) | copy-start | bytes 52
  54.0 2.0 %collective-permute-start.11 = (f32[4,256,128]{2,1,0:T(8,128)S(1)}, f32[4,256,128]{2,1,0:T(8,128)S(1)}, u32[]{:S(2)}, u32[]{:S(2)}) collective-permute-start(f32[4,256,128]{2,1,0:T(8,128)S(1)} %slice.41), channel_id=1, source_target_pairs={{0,8},{1,9},{2,10},{3,11},{4,12},{5,13},{6,14},{7,15},{8,0},{9,1},... | collective-permute-start | bytes 1572872 | tf_op jit(solution)/shard_map/ppermute | solution.py:65
  56.8 2.0 %collective-permute-start.12 = (f32[4,256,128]{2,1,0:T(8,128)S(1)}, f32[4,256,128]{2,1,0:T(8,128)S(1)}, u32[]{:S(2)}, u32[]{:S(2)}) collective-permute-start(f32[4,256,128]{2,1,0:T(8,128)S(1)} %shard_map.119.own), channel_id=1, source_target_pairs={{0,8},{1,9},{2,10},{3,11},{4,12},{5,13},{6,14},{7,15},{8,0},{9,1},... | collective-permute-start | bytes 1572872 | tf_op jit(solution)/shard_map/ppermute | solution.py:65
  70.2 2.0 %collective-permute-start.13 = (f32[4,256,128]{2,1,0:T(8,128)S(1)}, f32[4,256,128]{2,1,0:T(8,128)S(1)}, u32[]{:S(2)}, u32[]{:S(2)}) collective-permute-start(f32[4,256,128]{2,1,0:T(8,128)S(1)} %slice.42), channel_id=1, source_target_pairs={{0,8},{1,9},{2,10},{3,11},{4,12},{5,13},{6,14},{7,15},{8,0},{9,1},... | collective-permute-start | bytes 1572872 | tf_op jit(solution)/shard_map/ppermute | solution.py:65
  73.1 7.3 %collective-permute-start.16 = (f32[2,128,128]{2,1,0:T(8,128)S(1)}, f32[2,128,128]{2,1,0:T(8,128)S(1)}, u32[]{:S(2)}, u32[]{:S(2)}) collective-permute-start(f32[2,128,128]{2,1,0:T(8,128)S(1)} %bitcast.29), channel_id=1, source_target_pairs={{2,2},{10,6},{5,10},{13,14},{18,18},{26,22},{21,26},{29,30}} | collective-permute-start | bytes 393224 | tf_op jit(solution)/shard_map/ppermute | solution.py:65
  73.8 6.7 %collective-permute-start.17 = (f32[2,128,128]{2,1,0:T(8,128)S(1)}, f32[2,128,128]{2,1,0:T(8,128)S(1)}, u32[]{:S(2)}, u32[]{:S(2)}) collective-permute-start(f32[2,128,128]{2,1,0:T(8,128)S(1)} %bitcast.28), channel_id=1, source_target_pairs={{2,3},{10,7},{5,11},{13,15},{18,19},{26,23},{21,27},{29,31}} | collective-permute-start | bytes 393224 | tf_op jit(solution)/shard_map/ppermute | solution.py:65
  74.5 6.0 %collective-permute-start.15 = (f32[2,128,128]{2,1,0:T(8,128)S(1)}, f32[2,128,128]{2,1,0:T(8,128)S(1)}, u32[]{:S(2)}, u32[]{:S(2)}) collective-permute-start(f32[2,128,128]{2,1,0:T(8,128)S(1)} %bitcast.27), channel_id=1, source_target_pairs={{2,1},{10,5},{5,9},{13,13},{18,17},{26,21},{21,25},{29,29}} | collective-permute-start | bytes 393224 | tf_op jit(solution)/shard_map/ppermute | solution.py:65
  75.1 11.3 %collective-permute-start.14 = (f32[2,128,128]{2,1,0:T(8,128)S(1)}, f32[2,128,128]{2,1,0:T(8,128)S(1)}, u32[]{:S(2)}, u32[]{:S(2)}) collective-permute-start(f32[2,128,128]{2,1,0:T(8,128)S(1)} %bitcast.26), channel_id=1, source_target_pairs={{2,0},{10,4},{5,8},{13,12},{18,16},{26,20},{21,24},{29,28}} | collective-permute-start | bytes 393224 | tf_op jit(solution)/shard_map/ppermute | solution.py:65

commit v4 on v3

--- a/solution.py
+++ b/solution.py
@@ -536,7 +536,7 @@
         parts = parts.transpose(0, 2, 1, 3).reshape(half, 2, rows, tile_width)
         return [parts[part] for part in range(half)]
 
-    direct = tile_width == width and half <= 4 and scans <= width
+    direct = tile_width == width and half <= 4 and scans <= width and owned % 4 == 0
     pad = -scans % tile_width
     starts = jnp.pad(positions.astype(jnp.float32), ((0, 0), (0, pad)))
     starts = starts.reshape(-1, tile_width)
@@ -550,15 +550,15 @@
     far = [part for part in range(half) if part % 2 == 1]
     planes = volume.reshape(2 * owned, total, total)
     levels = [None] * half
-    cuts = (3 * owned // 4, 3 * owned // 2)
+    cuts = (owned // 4, 7 * owned // 4)
     if direct:
         pull, _ = lax.optimization_barrier((pull, message))
         measured = jnp.concatenate([measured, pull], 0)
+        for part in near:
+            levels[part] = send(measured, routes.to_hub(part, True))
         early, _ = lax.optimization_barrier((planes, measured))
         sums = [volume_sums(early, 0, cuts[0], 128)]
-        arrived, measured, sums[0] = lax.optimization_barrier((arrived, measured, sums[0]))
-        for part in near:
-            levels[part] = send(measured, routes.to_hub(part, True))
+        arrived, sums[0] = lax.optimization_barrier((arrived, sums[0]))
     else:
         sums = [volume_sums(planes, 0, owned, 128), volume_sums(planes, owned, owned, 128)]
         for part in range(half):

time: 113 us -> 110 us (0.973)
  waiting for transfers between devices: 12.9 us -> 7.44 us
  starting transfers between devices: 24.2 us -> 26.7 us
    ppermute x18, waiting for transfers between devices: 12.9 us -> 7.44 us  [send(): return lax.ppermute(value, AXES, pairs)]
    ppermute x18, starting transfers between devices: 24.2 us -> 26.7 us  [send(): return lax.ppermute(value, AXES, pairs)]
  transfers between devices with their start and end apart: 18 -> 18, of which waited for: 6 -> 4; matrix products, arithmetic and copies ran while one was open for 4% -> 5% of each run, Pallas kernels for 20% -> 20%
where the time goes in v4:
time: 110 us
  Pallas kernels  44.6 us (41%)
  starting transfers between devices  26.7 us (24%)
  blocking collectives  23.4 us (21%)
  waiting for transfers between devices  7.44 us (7%)
  other arithmetic  6.47 us (6%)
    ppermute x18, starting transfers between devices, send(): return lax.ppermute(value, AXES, pairs)  26.7 us
    pallas_call x3, Pallas kernels, gradient(): pl.pallas_call(functools.partial(gradient_kernel, floor, tuple(part_list)...  23.8 us
    pallas_call x3, Pallas kernels, volume_sums(): pl.pallas_call(functools.partial(sums_kernel, first), out_shape=(out, out...  14.7 us
    all_to_all x1, blocking collectives, shards(): lax.all_to_all(packed, AXES, split_axis=0, concat_axis=0, tiled=True)  13.4 us
    all_to_all x1, blocking collectives, shards(): fresh = lax.all_to_all(fresh, AXES, split_axis=0, concat_axis=0, tiled=True)  10 us
    ppermute x18, waiting for transfers between devices, send(): return lax.ppermute(value, AXES, pairs)  7.44 us
  transfers between devices with their start and end apart: 18, of which 4 were waited for; matrix products, arithmetic and copies ran while one was open for 5% of the time, Pallas kernels for 20%

profile of v4, /device:TPU:0, one launch (start us, length us, event | category | flops | bytes accessed | tf_op | source)
XLA Modules:
  0.0 109.9 jit_solution(5681387347804530267)
XLA Ops:
  0.6 0.0 copy-start.2
  0.6 0.7 convert_element_type.17
  1.3 0.9 select_maximum_fusion
  2.2 0.7 collective-permute-start.3
  2.9 0.7 collective-permute-start.2
  3.6 0.7 collective-permute-start.1
  4.3 6.2 %collective-permute-start = (f32[264,128]{1,0:T(8,128)S(1)}, f32[264,128]{1,0:T(8,128)S(1)}, u32[]{:S(2)}, u32[]{:S(2)}) collective-permute-start(f32[264,128]{1,0:T(8,128)S(1)} %select_maximum_fusion), channel_id=1, source_target_pairs={{0,2},{4,10},{8,5},{12,13},{16,18},{20,26},{24,21},{28,29}} | collective-permute-start | bytes 405512 | tf_op jit(solution)/shard_map/ppermute | solution.py:65
  10.5 0.7 convert_element_type.18
  11.1 0.1 broadcast_in_dim.22
  11.2 1.0 fusion
  12.2 1.9 %pad_maximum_fusion = f32[10,128,128]{2,1,0:T(8,128)} fusion(f32[2,128,128]{2,1,0:T(8,128)S(1)} %fusion, f32[8,128,128]{2,1,0:T(8,128)} %bitcast.24), kind=kLoop, calls=%fused_computation | loop fusion | flops 163840 | bytes 1310720 | tf_op jit(solution)/shard_map/concatenate | solution.py:556
  14.2 2.8 %shard_map.113 = (f32[1,1024]{1,0:T(1,128)S(1)}, f32[1,1024]{1,0:T(1,128)S(1)}) custom-call(f32[8,1024,1024]{2,1,0:T(8,128)} %bitcast.21), custom_call_target="tpu_custom_call" | custom-call | tf_op jit(solution)/shard_map/pallas_call | solution.py:368
  16.9 0.0 collective-permute-done.3.refs_3_
  16.9 0.0 collective-permute-done.2.refs_2_
  17.0 0.0 collective-permute-done.1.refs_1_
  17.0 0.0 collective-permute-done.refs_0_
  17.0 0.0 copy-done.2
  17.0 1.3 %collective-permute-start.5 = (f32[10,128,128]{2,1,0:T(8,128)}, f32[10,128,128]{2,1,0:T(8,128)}, u32[]{:S(2)}, u32[]{:S(2)}) collective-permute-start(f32[10,128,128]{2,1,0:T(8,128)} %pad_maximum_fusion), channel_id=1, source_target_pairs={{1,0},{14,15},{17,16},{30,31}} | collective-permute-start | bytes 1966088 | tf_op jit(solution)/shard_map/ppermute | solution.py:65
  18.3 0.7 collective-permute-start.7
  19.1 2.6 %collective-permute-start.4 = (f32[10,128,128]{2,1,0:T(8,128)}, f32[10,128,128]{2,1,0:T(8,128)S(1)}, u32[]{:S(2)}, u32[]{:S(2)}) collective-permute-start(f32[10,128,128]{2,1,0:T(8,128)} %pad_maximum_fusion), channel_id=1, source_target_pairs={{0,2},{4,10},{11,5},{15,13},{16,18},{20,26},{27,21},{31,29}} | collective-permute-start | bytes 1966088 | tf_op jit(solution)/shard_map/ppermute | solution.py:65
  21.7 0.7 collective-permute-start.8
  22.4 0.1 convert_element_type.20
  22.5 0.1 pad_add_fusion.meta
  22.5 1.5 %shard_map.115.refs_6_ = f32[8,128,128]{2,1,0:T(8,128)S(1)} custom-call(s32[34]{0:T(128)S(1)} %pad_add_fusion.meta, f32[2,128,128]{2,1,0:T(8,128)S(1)} %get-tuple-element.50.probe.refs_2_.refs_4_), custom_call_target="tpu_custom_call" | custom-call | tf_op jit(solution)/shard_map/pallas_call | solution.py:293
  24.1 7.1 %collective-permute-start.10 = (f32[4,128,128]{2,1,0:T(8,128)S(1)}, f32[4,128,128]{2,1,0:T(8,128)S(1)}, u32[]{:S(2)}, u32[]{:S(2)}) collective-permute-start(f32[4,128,128]{2,1,0:T(8,128)S(1)} %slice.40), channel_id=1, source_target_pairs={{0,8},{1,9},{2,10},{3,11},{4,12},{5,13},{6,14},{7,15},{8,0},{9,1},... | collective-permute-start | bytes 786440 | tf_op jit(solution)/shard_map/ppermute | solution.py:65
  31.1 0.0 collective-permute-done.5
  31.1 1.2 %broadcast_select_fusion = f32[10,128,128]{2,1,0:T(8,128)S(1)} fusion(f32[10,128,128]{2,1,0:T(8,128)} %collective-permute-done.5, f32[10,128,128]{2,1,0:T(8,128)} %pad_maximum_fusion, pred[]{:T(512)S(6)} %eq.11), kind=kLoop, calls=%fused_computation.1 | loop fusion | flops 163840 | bytes 1966081 | tf_op jit(solution)/shard_map/jit(_where)/select_n | solution.py:604
  32.3 1.3 %collective-permute-start.6 = (f32[10,128,128]{2,1,0:T(8,128)S(1)}, f32[10,128,128]{2,1,0:T(8,128)S(1)}, u32[]{:S(2)}, u32[]{:S(2)}) collective-permute-start(f32[10,128,128]{2,1,0:T(8,128)S(1)} %broadcast_select_fusion), channel_id=1, source_target_pairs={{0,2},{5,10},{10,5},{15,13},{16,18},{21,26},{26,21},{31,29}} | collective-permute-start | bytes 1966088 | tf_op jit(solution)/shard_map/ppermute | solution.py:65
  33.7 0.0 collective-permute-done.10.refs_7_
  33.7 0.1 collective-permute-start.9
  33.7 9.2 %shard_map.116 = (f32[6,1024]{1,0:T(8,128)S(1)}, f32[6,1024]{1,0:T(8,128)S(1)}) custom-call(f32[8,1024,1024]{2,1,0:T(8,128)} %bitcast.22), custom_call_target="tpu_custom_call" | custom-call | tf_op jit(solution)/shard_map/pallas_call | solution.py:368
  43.0 0.0 copy-start.1
  43.0 0.0 copy-start.4
  43.0 0.0 collective-permute-done.9.other
  43.0 0.0 collective-permute-done.7.refs_1_.refs_2_
  43.0 0.0 collective-permute-done.4.refs_0_
  43.0 0.0 copy-done
  43.0 6.1 %shard_map.117.refs_4_ = f32[8,256,128]{2,1,0:T(8,128)S(1)} custom-call(s32[34]{0:T(128)S(1)} %pad_add_fusion.meta, f32[4,256,128]{2,1,0:T(8,128)S(1)} %get-tuple-element.48.own, f32[4,256,128]{2,1,0:T(8,128)S(1)} %collective-permute-done.9.other, f32[10,128,128]{2,1,0:T(8,128)S(1)} %collective-permute-done.4.refs_0_, ...), custom_call_target="tpu_custom_call" | custom-call | tf_op jit(solution)/shard_map/pallas_call | solution.py:257
  49.2 0.0 collective-permute-done.8.refs_0_.refs_3_
  49.2 0.0 collective-permute-done.6.refs_1_.refs_2_
  49.2 6.3 %shard_map.118.refs_4_ = f32[8,256,128]{2,1,0:T(8,128)S(1)} custom-call(s32[34]{0:T(128)S(1)} %pad_add_fusion.meta, f32[4,256,128]{2,1,0:T(8,128)S(1)} %get-tuple-element.48.own, f32[4,256,128]{2,1,0:T(8,128)S(1)} %collective-permute-done.9.other, f32[10,128,128]{2,1,0:T(8,128)S(1)} %collective-permute-done.8.refs_0_.refs_3_, ...), custom_call_target="tpu_custom_call", output_to_operand_aliasing={{}: (7, {})} | custom-call | tf_op jit(solution)/shard_map/pallas_call | solution.py:257
  55.5 0.6 collective-permute-start.11
  56.0 1.5 %collective-permute-done.11.refs_5_ = f32[4,256,128]{2,1,0:T(8,128)S(1)} collective-permute-done((f32[4,256,128]{2,1,0:T(8,128)S(1)}, f32[4,256,128]{2,1,0:T(8,128)S(1)}, u32[]{:S(2)}, u32[]{:S(2)}) %collective-permute-start.11) | collective-permute-done | bytes 524320 | tf_op jit(solution)/shard_map/ppermute | solution.py:65
  57.6 0.8 shard_map.119.own
  58.4 0.4 collective-permute-start.12
  58.8 1.5 %collective-permute-done.12.other = f32[4,256,128]{2,1,0:T(8,128)S(1)} collective-permute-done((f32[4,256,128]{2,1,0:T(8,128)S(1)}, f32[4,256,128]{2,1,0:T(8,128)S(1)}, u32[]{:S(2)}, u32[]{:S(2)}) %collective-permute-start.12) | collective-permute-done | bytes 524320 | tf_op jit(solution)/shard_map/ppermute | solution.py:65
  60.4 11.4 %shard_map.120.refs_4_ = f32[8,256,128]{2,1,0:T(8,128)S(1)} custom-call(s32[34]{0:T(128)S(1)} %pad_add_fusion.meta, f32[4,256,128]{2,1,0:T(8,128)S(1)} %shard_map.119.own, f32[4,256,128]{2,1,0:T(8,128)S(1)} %collective-permute-done.12.other, f32[10,128,128]{2,1,0:T(8,128)S(1)} %collective-permute-done.4.refs_0_, ...), custom_call_target="tpu_custom_call" | custom-call | tf_op jit(solution)/shard_map/pallas_call | solution.py:257
  71.8 0.4 collective-permute-start.13
  72.3 1.5 %collective-permute-done.13.refs_5_ = f32[4,256,128]{2,1,0:T(8,128)S(1)} collective-permute-done((f32[4,256,128]{2,1,0:T(8,128)S(1)}, f32[4,256,128]{2,1,0:T(8,128)S(1)}, u32[]{:S(2)}, u32[]{:S(2)}) %collective-permute-start.13) | collective-permute-done | bytes 524320 | tf_op jit(solution)/shard_map/ppermute | solution.py:65
  73.8 0.8 shard_map.121
  74.7 0.7 collective-permute-start.16
  75.4 0.7 collective-permute-start.17
  76.0 0.7 collective-permute-start.15
  76.7 1.3 %collective-permute-start.14 = (f32[2,128,128]{2,1,0:T(8,128)S(1)}, f32[2,128,128]{2,1,0:T(8,128)S(1)}, u32[]{:S(2)}, u32[]{:S(2)}) collective-permute-start(f32[2,128,128]{2,1,0:T(8,128)S(1)} %bitcast.26), channel_id=1, source_target_pairs={{2,0},{10,4},{5,8},{13,12},{18,16},{26,20},{21,24},{29,28}} | collective-permute-start | bytes 393224 | tf_op jit(solution)/shard_map/ppermute | solution.py:65
  78.0 2.7 %shard_map.122 = (f32[1,1024]{1,0:T(1,128)S(1)}, f32[1,1024]{1,0:T(1,128)S(1)}) custom-call(f32[8,1024,1024]{2,1,0:T(8,128)} %bitcast.23), custom_call_target="tpu_custom_call" | custom-call | tf_op jit(solution)/shard_map/pallas_call | solution.py:368
  80.7 0.0 collective-permute-done.16.refs_2_
  80.8 0.0 collective-permute-done.17.refs_3_
  80.8 0.0 collective-permute-done.15.refs_1_
  80.8 2.8 %collective-permute-done.14.refs_0_ = f32[2,128,128]{2,1,0:T(8,128)S(1)} collective-permute-done((f32[2,128,128]{2,1,0:T(8,128)S(1)}, f32[2,128,128]{2,1,0:T(8,128)S(1)}, u32[]{:S(2)}, u32[]{:S(2)}) %collective-permute-start.14) | collective-permute-done | bytes 131104 | tf_op jit(solution)/shard_map/ppermute | solution.py:65
  83.6 0.6 shard_map.123
  84.2 13.4 %all_to_all.10.lines = f32[32,8,128]{2,1,0:T(8,128)S(1)} all-to-all(f32[32,8,128]{2,1,0:T(8,128)S(1)} %get-tuple-element.64), channel_id=1, replica_groups=mesh['view'=4,'tile'=8] {'view','tile'}, dimensions={0} | all-to-all | bytes 262144 | tf_op jit(solution)/shard_map/all_to_all | solution.py:648
  97.6 1.1 shard_map.124
  98.7 10.0 %all_to_all.11.packed = f32[32,8,128]{2,1,0:T(8,128)S(1)} all-to-all(f32[32,8,128]{2,1,0:T(8,128)S(1)} %shard_map.124), channel_id=1, replica_groups=mesh['view'=4,'tile'=8] {'view','tile'}, dimensions={0} | all-to-all | bytes 262144 | tf_op jit(solution)/shard_map/all_to_all | solution.py:657
  108.7 1.3 %shard_map.125 = (f32[2,128,128]{2,1,0:T(8,128)}, f32[2,128,128]{2,1,0:T(8,128)}) custom-call(s32[2]{0:T(128)S(1)} %copy-done.3, f32[32,8,128]{2,1,0:T(8,128)S(1)} %all_to_all.11.packed, f32[2,128,128]{2,1,0:T(8,128)S(1)} %get-tuple-element.71.psi, f32[2,128,128]{2,1,0:T(8,128)S(1)} %bitcast.20), custom_call_target="tpu_custom_call" | custom-call | tf_op jit(solution)/shard_map/pallas_call | solution.py:658
  (12 shorter events, 0.2 us)
Async XLA Ops:
  0.6 16.4 %copy-start.2 = (f32[2,128,128]{2,1,0:T(8,128)S(1)}, f32[2,128,128]{2,1,0:T(8,128)}, u32[]{:S(2)}) copy-start(f32[2,128,128]{2,1,0:T(8,128)} %refs_4_.1) | copy-start | bytes 393220
  2.2 14.7 %collective-permute-start.3 = (f32[264,128]{1,0:T(8,128)S(1)}, f32[264,128]{1,0:T(8,128)S(1)}, u32[]{:S(2)}, u32[]{:S(2)}) collective-permute-start(f32[264,128]{1,0:T(8,128)S(1)} %select_maximum_fusion), channel_id=1, source_target_pairs={{3,2},{7,10},{11,5},{15,13},{19,18},{23,26},{27,21},{31,29}} | collective-permute-start | bytes 405512 | tf_op jit(solution)/shard_map/ppermute | solution.py:65
  2.9 14.0 %collective-permute-start.2 = (f32[264,128]{1,0:T(8,128)S(1)}, f32[264,128]{1,0:T(8,128)S(1)}, u32[]{:S(2)}, u32[]{:S(2)}) collective-permute-start(f32[264,128]{1,0:T(8,128)S(1)} %select_maximum_fusion), channel_id=1, source_target_pairs={{2,2},{6,10},{10,5},{14,13},{18,18},{22,26},{26,21},{30,29}} | collective-permute-start | bytes 405512 | tf_op jit(solution)/shard_map/ppermute | solution.py:65
  3.6 13.4 %collective-permute-start.1 = (f32[264,128]{1,0:T(8,128)S(1)}, f32[264,128]{1,0:T(8,128)S(1)}, u32[]{:S(2)}, u32[]{:S(2)}) collective-permute-start(f32[264,128]{1,0:T(8,128)S(1)} %select_maximum_fusion), channel_id=1, source_target_pairs={{1,2},{5,10},{9,5},{13,13},{17,18},{21,26},{25,21},{29,29}} | collective-permute-start | bytes 405512 | tf_op jit(solution)/shard_map/ppermute | solution.py:65
  4.3 12.7 %collective-permute-start = (f32[264,128]{1,0:T(8,128)S(1)}, f32[264,128]{1,0:T(8,128)S(1)}, u32[]{:S(2)}, u32[]{:S(2)}) collective-permute-start(f32[264,128]{1,0:T(8,128)S(1)} %select_maximum_fusion), channel_id=1, source_target_pairs={{0,2},{4,10},{8,5},{12,13},{16,18},{20,26},{24,21},{28,29}} | collective-permute-start | bytes 405512 | tf_op jit(solution)/shard_map/ppermute | solution.py:65
  14.1 28.9 %copy-start = (bf16[2,2,256,256]{3,2,1,0:T(8,128)(2,1)S(1)}, bf16[2,2,256,256]{3,2,1,0:T(8,128)(2,1)}, u32[]{:S(2)}) copy-start(bf16[2,2,256,256]{3,2,1,0:T(8,128)(2,1)} %constant.24.clone.refs_3_.refs_5_) | copy-start | bytes 1572868
  14.1 43.4 %copy-start.3 = (s32[2]{0:T(128)S(1)}, s32[2]{0:T(128)}, u32[]{:S(2)}) copy-start(s32[2]{0:T(128)} %penalty.7) | copy-start | bytes 28
  17.0 14.1 %collective-permute-start.5 = (f32[10,128,128]{2,1,0:T(8,128)}, f32[10,128,128]{2,1,0:T(8,128)}, u32[]{:S(2)}, u32[]{:S(2)}) collective-permute-start(f32[10,128,128]{2,1,0:T(8,128)} %pad_maximum_fusion), channel_id=1, source_target_pairs={{1,0},{14,15},{17,16},{30,31}} | collective-permute-start | bytes 1966088 | tf_op jit(solution)/shard_map/ppermute | solution.py:65
  18.3 24.6 %collective-permute-start.7 = (f32[10,128,128]{2,1,0:T(8,128)}, f32[10,128,128]{2,1,0:T(8,128)S(1)}, u32[]{:S(2)}, u32[]{:S(2)}) collective-permute-start(f32[10,128,128]{2,1,0:T(8,128)} %pad_maximum_fusion), channel_id=1, source_target_pairs={{2,2},{6,10},{9,5},{13,13},{18,18},{22,26},{25,21},{29,29}} | collective-permute-start | bytes 1966088 | tf_op jit(solution)/shard_map/ppermute | solution.py:65
  19.1 23.9 %collective-permute-start.4 = (f32[10,128,128]{2,1,0:T(8,128)}, f32[10,128,128]{2,1,0:T(8,128)S(1)}, u32[]{:S(2)}, u32[]{:S(2)}) collective-permute-start(f32[10,128,128]{2,1,0:T(8,128)} %pad_maximum_fusion), channel_id=1, source_target_pairs={{0,2},{4,10},{11,5},{15,13},{16,18},{20,26},{27,21},{31,29}} | collective-permute-start | bytes 1966088 | tf_op jit(solution)/shard_map/ppermute | solution.py:65
  21.7 27.5 %collective-permute-start.8 = (f32[10,128,128]{2,1,0:T(8,128)}, f32[10,128,128]{2,1,0:T(8,128)S(1)}, u32[]{:S(2)}, u32[]{:S(2)}) collective-permute-start(f32[10,128,128]{2,1,0:T(8,128)} %pad_maximum_fusion), channel_id=1, source_target_pairs={{3,2},{7,10},{8,5},{12,13},{19,18},{23,26},{24,21},{28,29}} | collective-permute-start | bytes 1966088 | tf_op jit(solution)/shard_map/ppermute | solution.py:65
  24.1 9.6 %collective-permute-start.10 = (f32[4,128,128]{2,1,0:T(8,128)S(1)}, f32[4,128,128]{2,1,0:T(8,128)S(1)}, u32[]{:S(2)}, u32[]{:S(2)}) collective-permute-start(f32[4,128,128]{2,1,0:T(8,128)S(1)} %slice.40), channel_id=1, source_target_pairs={{0,8},{1,9},{2,10},{3,11},{4,12},{5,13},{6,14},{7,15},{8,0},{9,1},... | collective-permute-start | bytes 786440 | tf_op jit(solution)/shard_map/ppermute | solution.py:65
  32.3 16.8 %collective-permute-start.6 = (f32[10,128,128]{2,1,0:T(8,128)S(1)}, f32[10,128,128]{2,1,0:T(8,128)S(1)}, u32[]{:S(2)}, u32[]{:S(2)}) collective-permute-start(f32[10,128,128]{2,1,0:T(8,128)S(1)} %broadcast_select_fusion), channel_id=1, source_target_pairs={{0,2},{5,10},{10,5},{15,13},{16,18},{21,26},{26,21},{31,29}} | collective-permute-start | bytes 1966088 | tf_op jit(solution)/shard_map/ppermute | solution.py:65
  33.7 9.3 %collective-permute-start.9 = (f32[4,256,128]{2,1,0:T(8,128)S(1)}, f32[4,256,128]{2,1,0:T(8,128)S(1)}, u32[]{:S(2)}, u32[]{:S(2)}) collective-permute-start(f32[4,256,128]{2,1,0:T(8,128)S(1)} %get-tuple-element.48.own), channel_id=1, source_target_pairs={{0,8},{1,9},{2,10},{3,11},{4,12},{5,13},{6,14},{7,15},{8,0},{9,1},... | collective-permute-start | bytes 1572872 | tf_op jit(solution)/shard_map/ppermute | solution.py:65
  43.0 40.6 %copy-start.1 = (f32[1,2,128,128]{3,2,1,0:T(8,128)S(1)}, f32[1,2,128,128]{3,2,1,0:T(8,128)}, u32[]{:S(2)}) copy-start(f32[1,2,128,128]{3,2,1,0:T(8,128)} %param.15) | copy-start | bytes 393220
  43.0 54.6 %copy-start.4 = (s32[4]{0:T(128)S(1)}, s32[4]{0:T(128)}, u32[]{:S(2)}) copy-start(s32[4]{0:T(128)} %angles.1) | copy-start | bytes 52
  55.5 2.1 %collective-permute-start.11 = (f32[4,256,128]{2,1,0:T(8,128)S(1)}, f32[4,256,128]{2,1,0:T(8,128)S(1)}, u32[]{:S(2)}, u32[]{:S(2)}) collective-permute-start(f32[4,256,128]{2,1,0:T(8,128)S(1)} %slice.41), channel_id=1, source_target_pairs={{0,8},{1,9},{2,10},{3,11},{4,12},{5,13},{6,14},{7,15},{8,0},{9,1},... | collective-permute-start | bytes 1572872 | tf_op jit(solution)/shard_map/ppermute | solution.py:65
  58.4 2.0 %collective-permute-start.12 = (f32[4,256,128]{2,1,0:T(8,128)S(1)}, f32[4,256,128]{2,1,0:T(8,128)S(1)}, u32[]{:S(2)}, u32[]{:S(2)}) collective-permute-start(f32[4,256,128]{2,1,0:T(8,128)S(1)} %shard_map.119.own), channel_id=1, source_target_pairs={{0,8},{1,9},{2,10},{3,11},{4,12},{5,13},{6,14},{7,15},{8,0},{9,1},... | collective-permute-start | bytes 1572872 | tf_op jit(solution)/shard_map/ppermute | solution.py:65
  71.8 2.0 %collective-permute-start.13 = (f32[4,256,128]{2,1,0:T(8,128)S(1)}, f32[4,256,128]{2,1,0:T(8,128)S(1)}, u32[]{:S(2)}, u32[]{:S(2)}) collective-permute-start(f32[4,256,128]{2,1,0:T(8,128)S(1)} %slice.42), channel_id=1, source_target_pairs={{0,8},{1,9},{2,10},{3,11},{4,12},{5,13},{6,14},{7,15},{8,0},{9,1},... | collective-permute-start | bytes 1572872 | tf_op jit(solution)/shard_map/ppermute | solution.py:65
  74.7 6.1 %collective-permute-start.16 = (f32[2,128,128]{2,1,0:T(8,128)S(1)}, f32[2,128,128]{2,1,0:T(8,128)S(1)}, u32[]{:S(2)}, u32[]{:S(2)}) collective-permute-start(f32[2,128,128]{2,1,0:T(8,128)S(1)} %bitcast.29), channel_id=1, source_target_pairs={{2,2},{10,6},{5,10},{13,14},{18,18},{26,22},{21,26},{29,30}} | collective-permute-start | bytes 393224 | tf_op jit(solution)/shard_map/ppermute | solution.py:65
  75.4 5.4 %collective-permute-start.17 = (f32[2,128,128]{2,1,0:T(8,128)S(1)}, f32[2,128,128]{2,1,0:T(8,128)S(1)}, u32[]{:S(2)}, u32[]{:S(2)}) collective-permute-start(f32[2,128,128]{2,1,0:T(8,128)S(1)} %bitcast.28), channel_id=1, source_target_pairs={{2,3},{10,7},{5,11},{13,15},{18,19},{26,23},{21,27},{29,31}} | collective-permute-start | bytes 393224 | tf_op jit(solution)/shard_map/ppermute | solution.py:65
  76.0 4.7 %collective-permute-start.15 = (f32[2,128,128]{2,1,0:T(8,128)S(1)}, f32[2,128,128]{2,1,0:T(8,128)S(1)}, u32[]{:S(2)}, u32[]{:S(2)}) collective-permute-start(f32[2,128,128]{2,1,0:T(8,128)S(1)} %bitcast.27), channel_id=1, source_target_pairs={{2,1},{10,5},{5,9},{13,13},{18,17},{26,21},{21,25},{29,29}} | collective-permute-start | bytes 393224 | tf_op jit(solution)/shard_map/ppermute | solution.py:65
  76.7 6.9 %collective-permute-start.14 = (f32[2,128,128]{2,1,0:T(8,128)S(1)}, f32[2,128,128]{2,1,0:T(8,128)S(1)}, u32[]{:S(2)}, u32[]{:S(2)}) collective-permute-start(f32[2,128,128]{2,1,0:T(8,128)S(1)} %bitcast.26), channel_id=1, source_target_pairs={{2,0},{10,4},{5,8},{13,12},{18,16},{26,20},{21,24},{29,28}} | collective-permute-start | bytes 393224 | tf_op jit(solution)/shard_map/ppermute | solution.py:65

commit v5 on v4

--- a/solution.py
+++ b/solution.py
@@ -550,7 +550,7 @@
     far = [part for part in range(half) if part % 2 == 1]
     planes = volume.reshape(2 * owned, total, total)
     levels = [None] * half
-    cuts = (owned // 4, 7 * owned // 4)
+    cuts = (owned // 4, 3 * owned // 2)
     if direct:
         pull, _ = lax.optimization_barrier((pull, message))
         measured = jnp.concatenate([measured, pull], 0)

time: 110 us -> 109 us (level)
  transfers between devices with their start and end apart: 18 -> 18, of which waited for: 4 -> 4; matrix products, arithmetic and copies ran while one was open for 5% -> 5% of each run, Pallas kernels for 20% -> 21%
where the time goes in v5:
time: 109 us
  Pallas kernels  44.7 us (41%)
  starting transfers between devices  26.7 us (24%)
  blocking collectives  22.8 us (21%)
  waiting for transfers between devices  6.8 us (6%)
  other arithmetic  6.47 us (6%)
    ppermute x18, starting transfers between devices, send(): return lax.ppermute(value, AXES, pairs)  26.7 us
    pallas_call x3, Pallas kernels, gradient(): pl.pallas_call(functools.partial(gradient_kernel, floor, tuple(part_list)...  23.8 us
    pallas_call x3, Pallas kernels, volume_sums(): pl.pallas_call(functools.partial(sums_kernel, first), out_shape=(out, out...  14.8 us
    all_to_all x1, blocking collectives, shards(): lax.all_to_all(packed, AXES, split_axis=0, concat_axis=0, tiled=True)  12.8 us
    all_to_all x1, blocking collectives, shards(): fresh = lax.all_to_all(fresh, AXES, split_axis=0, concat_axis=0, tiled=True)  10 us
    ppermute x18, waiting for transfers between devices, send(): return lax.ppermute(value, AXES, pairs)  6.8 us
  transfers between devices with their start and end apart: 18, of which 4 were waited for; matrix products, arithmetic and copies ran while one was open for 5% of the time, Pallas kernels for 21%

profile of v5, /device:TPU:0, one launch (start us, length us, event | category | flops | bytes accessed | tf_op | source)
XLA Modules:
  0.0 108.7 jit_solution(11009549545988513116)
XLA Ops:
  0.6 0.0 copy-start.2
  0.6 0.7 convert_element_type.17
  1.3 0.9 select_maximum_fusion
  2.2 0.7 collective-permute-start.3
  2.9 0.7 collective-permute-start.2
  3.6 0.7 collective-permute-start.1
  4.3 6.2 %collective-permute-start = (f32[264,128]{1,0:T(8,128)S(1)}, f32[264,128]{1,0:T(8,128)S(1)}, u32[]{:S(2)}, u32[]{:S(2)}) collective-permute-start(f32[264,128]{1,0:T(8,128)S(1)} %select_maximum_fusion), channel_id=1, source_target_pairs={{0,2},{4,10},{8,5},{12,13},{16,18},{20,26},{24,21},{28,29}} | collective-permute-start | bytes 405512 | tf_op jit(solution)/shard_map/ppermute | solution.py:65
  10.5 0.7 convert_element_type.18
  11.1 0.1 broadcast_in_dim.22
  11.2 1.0 fusion
  12.2 1.9 %pad_maximum_fusion = f32[10,128,128]{2,1,0:T(8,128)} fusion(f32[2,128,128]{2,1,0:T(8,128)S(1)} %fusion, f32[8,128,128]{2,1,0:T(8,128)} %bitcast.24), kind=kLoop, calls=%fused_computation | loop fusion | flops 163840 | bytes 1310720 | tf_op jit(solution)/shard_map/concatenate | solution.py:556
  14.2 2.8 %shard_map.113 = (f32[1,1024]{1,0:T(1,128)S(1)}, f32[1,1024]{1,0:T(1,128)S(1)}) custom-call(f32[8,1024,1024]{2,1,0:T(8,128)} %bitcast.21), custom_call_target="tpu_custom_call" | custom-call | tf_op jit(solution)/shard_map/pallas_call | solution.py:368
  16.9 0.0 collective-permute-done.3.refs_3_
  16.9 0.0 collective-permute-done.2.refs_2_
  17.0 0.0 collective-permute-done.1.refs_1_
  17.0 0.0 collective-permute-done.refs_0_
  17.0 0.0 copy-done.2
  17.0 1.3 %collective-permute-start.5 = (f32[10,128,128]{2,1,0:T(8,128)}, f32[10,128,128]{2,1,0:T(8,128)}, u32[]{:S(2)}, u32[]{:S(2)}) collective-permute-start(f32[10,128,128]{2,1,0:T(8,128)} %pad_maximum_fusion), channel_id=1, source_target_pairs={{1,0},{14,15},{17,16},{30,31}} | collective-permute-start | bytes 1966088 | tf_op jit(solution)/shard_map/ppermute | solution.py:65
  18.3 0.7 collective-permute-start.7
  19.1 2.6 %collective-permute-start.4 = (f32[10,128,128]{2,1,0:T(8,128)}, f32[10,128,128]{2,1,0:T(8,128)S(1)}, u32[]{:S(2)}, u32[]{:S(2)}) collective-permute-start(f32[10,128,128]{2,1,0:T(8,128)} %pad_maximum_fusion), channel_id=1, source_target_pairs={{0,2},{4,10},{11,5},{15,13},{16,18},{20,26},{27,21},{31,29}} | collective-permute-start | bytes 1966088 | tf_op jit(solution)/shard_map/ppermute | solution.py:65
  21.7 0.7 collective-permute-start.8
  22.4 0.1 convert_element_type.20
  22.5 0.1 pad_add_fusion.meta
  22.5 1.5 %shard_map.115.refs_6_ = f32[8,128,128]{2,1,0:T(8,128)S(1)} custom-call(s32[34]{0:T(128)S(1)} %pad_add_fusion.meta, f32[2,128,128]{2,1,0:T(8,128)S(1)} %get-tuple-element.50.probe.refs_2_.refs_4_), custom_call_target="tpu_custom_call" | custom-call | tf_op jit(solution)/shard_map/pallas_call | solution.py:293
  24.1 7.1 %collective-permute-start.10 = (f32[4,128,128]{2,1,0:T(8,128)S(1)}, f32[4,128,128]{2,1,0:T(8,128)S(1)}, u32[]{:S(2)}, u32[]{:S(2)}) collective-permute-start(f32[4,128,128]{2,1,0:T(8,128)S(1)} %slice.40), channel_id=1, source_target_pairs={{0,8},{1,9},{2,10},{3,11},{4,12},{5,13},{6,14},{7,15},{8,0},{9,1},... | collective-permute-start | bytes 786440 | tf_op jit(solution)/shard_map/ppermute | solution.py:65
  31.1 0.0 collective-permute-done.5
  31.1 1.2 %broadcast_select_fusion = f32[10,128,128]{2,1,0:T(8,128)S(1)} fusion(f32[10,128,128]{2,1,0:T(8,128)} %collective-permute-done.5, f32[10,128,128]{2,1,0:T(8,128)} %pad_maximum_fusion, pred[]{:T(512)S(6)} %eq.11), kind=kLoop, calls=%fused_computation.1 | loop fusion | flops 163840 | bytes 1966081 | tf_op jit(solution)/shard_map/jit(_where)/select_n | solution.py:604
  32.3 1.3 %collective-permute-start.6 = (f32[10,128,128]{2,1,0:T(8,128)S(1)}, f32[10,128,128]{2,1,0:T(8,128)S(1)}, u32[]{:S(2)}, u32[]{:S(2)}) collective-permute-start(f32[10,128,128]{2,1,0:T(8,128)S(1)} %broadcast_select_fusion), channel_id=1, source_target_pairs={{0,2},{5,10},{10,5},{15,13},{16,18},{21,26},{26,21},{31,29}} | collective-permute-start | bytes 1966088 | tf_op jit(solution)/shard_map/ppermute | solution.py:65
  33.7 0.0 collective-permute-done.10.refs_7_
  33.7 0.1 collective-permute-start.9
  33.7 8.0 %shard_map.116 = (f32[5,1024]{1,0:T(8,128)S(1)}, f32[5,1024]{1,0:T(8,128)S(1)}) custom-call(f32[8,1024,1024]{2,1,0:T(8,128)} %bitcast.22), custom_call_target="tpu_custom_call" | custom-call | tf_op jit(solution)/shard_map/pallas_call | solution.py:368
  41.8 0.0 copy-start.1
  41.8 0.0 copy-start.4
  41.8 0.0 collective-permute-done.9.other
  41.8 0.0 collective-permute-done.7.refs_1_.refs_2_
  41.8 0.0 collective-permute-done.4.refs_0_
  41.8 6.1 %shard_map.117.refs_4_ = f32[8,256,128]{2,1,0:T(8,128)S(1)} custom-call(s32[34]{0:T(128)S(1)} %pad_add_fusion.meta, f32[4,256,128]{2,1,0:T(8,128)S(1)} %get-tuple-element.48.own, f32[4,256,128]{2,1,0:T(8,128)S(1)} %collective-permute-done.9.other, f32[10,128,128]{2,1,0:T(8,128)S(1)} %collective-permute-done.4.refs_0_, ...), custom_call_target="tpu_custom_call" | custom-call | tf_op jit(solution)/shard_map/pallas_call | solution.py:257
  48.0 0.0 collective-permute-done.8.refs_0_.refs_3_
  48.0 0.0 collective-permute-done.6.refs_1_.refs_2_
  48.0 6.3 %shard_map.118.refs_4_ = f32[8,256,128]{2,1,0:T(8,128)S(1)} custom-call(s32[34]{0:T(128)S(1)} %pad_add_fusion.meta, f32[4,256,128]{2,1,0:T(8,128)S(1)} %get-tuple-element.48.own, f32[4,256,128]{2,1,0:T(8,128)S(1)} %collective-permute-done.9.other, f32[10,128,128]{2,1,0:T(8,128)S(1)} %collective-permute-done.8.refs_0_.refs_3_, ...), custom_call_target="tpu_custom_call", output_to_operand_aliasing={{}: (7, {})} | custom-call | tf_op jit(solution)/shard_map/pallas_call | solution.py:257
  54.3 0.6 collective-permute-start.11
  54.8 1.5 %collective-permute-done.11.refs_5_ = f32[4,256,128]{2,1,0:T(8,128)S(1)} collective-permute-done((f32[4,256,128]{2,1,0:T(8,128)S(1)}, f32[4,256,128]{2,1,0:T(8,128)S(1)}, u32[]{:S(2)}, u32[]{:S(2)}) %collective-permute-start.11) | collective-permute-done | bytes 524320 | tf_op jit(solution)/shard_map/ppermute | solution.py:65
  56.4 0.0 copy-done.3
  56.4 0.8 shard_map.119.own
  57.2 0.4 collective-permute-start.12
  57.7 1.5 %collective-permute-done.12.other = f32[4,256,128]{2,1,0:T(8,128)S(1)} collective-permute-done((f32[4,256,128]{2,1,0:T(8,128)S(1)}, f32[4,256,128]{2,1,0:T(8,128)S(1)}, u32[]{:S(2)}, u32[]{:S(2)}) %collective-permute-start.12) | collective-permute-done | bytes 524320 | tf_op jit(solution)/shard_map/ppermute | solution.py:65
  59.2 11.4 %shard_map.120.refs_4_ = f32[8,256,128]{2,1,0:T(8,128)S(1)} custom-call(s32[34]{0:T(128)S(1)} %pad_add_fusion.meta, f32[4,256,128]{2,1,0:T(8,128)S(1)} %shard_map.119.own, f32[4,256,128]{2,1,0:T(8,128)S(1)} %collective-permute-done.12.other, f32[10,128,128]{2,1,0:T(8,128)S(1)} %collective-permute-done.4.refs_0_, ...), custom_call_target="tpu_custom_call" | custom-call | tf_op jit(solution)/shard_map/pallas_call | solution.py:257
  70.6 0.4 collective-permute-start.13
  71.1 1.5 %collective-permute-done.13.refs_5_ = f32[4,256,128]{2,1,0:T(8,128)S(1)} collective-permute-done((f32[4,256,128]{2,1,0:T(8,128)S(1)}, f32[4,256,128]{2,1,0:T(8,128)S(1)}, u32[]{:S(2)}, u32[]{:S(2)}) %collective-permute-start.13) | collective-permute-done | bytes 524320 | tf_op jit(solution)/shard_map/ppermute | solution.py:65
  72.6 0.8 shard_map.121
  73.5 0.7 collective-permute-start.16
  74.2 0.7 collective-permute-start.17
  74.8 0.7 collective-permute-start.15
  75.5 1.3 %collective-permute-start.14 = (f32[2,128,128]{2,1,0:T(8,128)S(1)}, f32[2,128,128]{2,1,0:T(8,128)S(1)}, u32[]{:S(2)}, u32[]{:S(2)}) collective-permute-start(f32[2,128,128]{2,1,0:T(8,128)S(1)} %bitcast.26), channel_id=1, source_target_pairs={{2,0},{10,4},{5,8},{13,12},{18,16},{26,20},{21,24},{29,28}} | collective-permute-start | bytes 393224 | tf_op jit(solution)/shard_map/ppermute | solution.py:65
  76.8 4.0 %shard_map.122 = (f32[2,1024]{1,0:T(2,128)S(1)}, f32[2,1024]{1,0:T(2,128)S(1)}) custom-call(f32[8,1024,1024]{2,1,0:T(8,128)} %bitcast.23), custom_call_target="tpu_custom_call" | custom-call | tf_op jit(solution)/shard_map/pallas_call | solution.py:368
  80.8 0.0 collective-permute-done.16.refs_2_
  80.8 0.0 collective-permute-done.17.refs_3_
  80.8 0.0 collective-permute-done.15.refs_1_
  80.8 2.2 %collective-permute-done.14.refs_0_ = f32[2,128,128]{2,1,0:T(8,128)S(1)} collective-permute-done((f32[2,128,128]{2,1,0:T(8,128)S(1)}, f32[2,128,128]{2,1,0:T(8,128)S(1)}, u32[]{:S(2)}, u32[]{:S(2)}) %collective-permute-start.14) | collective-permute-done | bytes 131104 | tf_op jit(solution)/shard_map/ppermute | solution.py:65
  83.0 0.6 shard_map.123
  83.6 12.8 %all_to_all.10.lines = f32[32,8,128]{2,1,0:T(8,128)S(1)} all-to-all(f32[32,8,128]{2,1,0:T(8,128)S(1)} %get-tuple-element.64), channel_id=1, replica_groups=mesh['view'=4,'tile'=8] {'view','tile'}, dimensions={0} | all-to-all | bytes 262144 | tf_op jit(solution)/shard_map/all_to_all | solution.py:648
  96.4 1.1 %shard_map.124 = f32[32,8,128]{2,1,0:T(8,128)S(1)} custom-call(s32[4]{0:T(128)S(1)} %copy-done.4, f32[32,8,128]{2,1,0:T(8,128)S(1)} %all_to_all.10.lines, f32[1,1024]{1,0:T(1,128)S(1)} %get-tuple-element.65.refs_0_, f32[1,1024]{1,0:T(1,128)S(1)} %get-tuple-element.66.refs_1_, f32[5,1024]{1,0:T(8,128)S(1)} %get-tuple-element.67.refs_2_, ...), custom_call_target="tpu_custom_call" | custom-call | tf_op jit(solution)/shard_map/pallas_call | solution.py:649
  97.5 10.0 %all_to_all.11.packed = f32[32,8,128]{2,1,0:T(8,128)S(1)} all-to-all(f32[32,8,128]{2,1,0:T(8,128)S(1)} %shard_map.124), channel_id=1, replica_groups=mesh['view'=4,'tile'=8] {'view','tile'}, dimensions={0} | all-to-all | bytes 262144 | tf_op jit(solution)/shard_map/all_to_all | solution.py:657
  107.5 1.3 %shard_map.125 = (f32[2,128,128]{2,1,0:T(8,128)}, f32[2,128,128]{2,1,0:T(8,128)}) custom-call(s32[2]{0:T(128)S(1)} %copy-done.3, f32[32,8,128]{2,1,0:T(8,128)S(1)} %all_to_all.11.packed, f32[2,128,128]{2,1,0:T(8,128)S(1)} %get-tuple-element.71.psi, f32[2,128,128]{2,1,0:T(8,128)S(1)} %bitcast.20), custom_call_target="tpu_custom_call" | custom-call | tf_op jit(solution)/shard_map/pallas_call | solution.py:658
  (12 shorter events, 0.2 us)
Async XLA Ops:
  0.6 16.4 %copy-start.2 = (f32[2,128,128]{2,1,0:T(8,128)S(1)}, f32[2,128,128]{2,1,0:T(8,128)}, u32[]{:S(2)}) copy-start(f32[2,128,128]{2,1,0:T(8,128)} %refs_4_.1) | copy-start | bytes 393220
  2.2 14.7 %collective-permute-start.3 = (f32[264,128]{1,0:T(8,128)S(1)}, f32[264,128]{1,0:T(8,128)S(1)}, u32[]{:S(2)}, u32[]{:S(2)}) collective-permute-start(f32[264,128]{1,0:T(8,128)S(1)} %select_maximum_fusion), channel_id=1, source_target_pairs={{3,2},{7,10},{11,5},{15,13},{19,18},{23,26},{27,21},{31,29}} | collective-permute-start | bytes 405512 | tf_op jit(solution)/shard_map/ppermute | solution.py:65
  2.9 14.0 %collective-permute-start.2 = (f32[264,128]{1,0:T(8,128)S(1)}, f32[264,128]{1,0:T(8,128)S(1)}, u32[]{:S(2)}, u32[]{:S(2)}) collective-permute-start(f32[264,128]{1,0:T(8,128)S(1)} %select_maximum_fusion), channel_id=1, source_target_pairs={{2,2},{6,10},{10,5},{14,13},{18,18},{22,26},{26,21},{30,29}} | collective-permute-start | bytes 405512 | tf_op jit(solution)/shard_map/ppermute | solution.py:65
  3.6 13.4 %collective-permute-start.1 = (f32[264,128]{1,0:T(8,128)S(1)}, f32[264,128]{1,0:T(8,128)S(1)}, u32[]{:S(2)}, u32[]{:S(2)}) collective-permute-start(f32[264,128]{1,0:T(8,128)S(1)} %select_maximum_fusion), channel_id=1, source_target_pairs={{1,2},{5,10},{9,5},{13,13},{17,18},{21,26},{25,21},{29,29}} | collective-permute-start | bytes 405512 | tf_op jit(solution)/shard_map/ppermute | solution.py:65
  4.3 12.7 %collective-permute-start = (f32[264,128]{1,0:T(8,128)S(1)}, f32[264,128]{1,0:T(8,128)S(1)}, u32[]{:S(2)}, u32[]{:S(2)}) collective-permute-start(f32[264,128]{1,0:T(8,128)S(1)} %select_maximum_fusion), channel_id=1, source_target_pairs={{0,2},{4,10},{8,5},{12,13},{16,18},{20,26},{24,21},{28,29}} | collective-permute-start | bytes 405512 | tf_op jit(solution)/shard_map/ppermute | solution.py:65
  14.1 27.7 %copy-start = (bf16[2,2,256,256]{3,2,1,0:T(8,128)(2,1)S(1)}, bf16[2,2,256,256]{3,2,1,0:T(8,128)(2,1)}, u32[]{:S(2)}) copy-start(bf16[2,2,256,256]{3,2,1,0:T(8,128)(2,1)} %constant.24.clone.refs_3_.refs_5_) | copy-start | bytes 1572868
  14.1 42.2 %copy-start.3 = (s32[2]{0:T(128)S(1)}, s32[2]{0:T(128)}, u32[]{:S(2)}) copy-start(s32[2]{0:T(128)} %penalty.7) | copy-start | bytes 28
  17.0 14.1 %collective-permute-start.5 = (f32[10,128,128]{2,1,0:T(8,128)}, f32[10,128,128]{2,1,0:T(8,128)}, u32[]{:S(2)}, u32[]{:S(2)}) collective-permute-start(f32[10,128,128]{2,1,0:T(8,128)} %pad_maximum_fusion), channel_id=1, source_target_pairs={{1,0},{14,15},{17,16},{30,31}} | collective-permute-start | bytes 1966088 | tf_op jit(solution)/shard_map/ppermute | solution.py:65
  18.3 23.4 %collective-permute-start.7 = (f32[10,128,128]{2,1,0:T(8,128)}, f32[10,128,128]{2,1,0:T(8,128)S(1)}, u32[]{:S(2)}, u32[]{:S(2)}) collective-permute-start(f32[10,128,128]{2,1,0:T(8,128)} %pad_maximum_fusion), channel_id=1, source_target_pairs={{2,2},{6,10},{9,5},{13,13},{18,18},{22,26},{25,21},{29,29}} | collective-permute-start | bytes 1966088 | tf_op jit(solution)/shard_map/ppermute | solution.py:65
  19.1 22.7 %collective-permute-start.4 = (f32[10,128,128]{2,1,0:T(8,128)}, f32[10,128,128]{2,1,0:T(8,128)S(1)}, u32[]{:S(2)}, u32[]{:S(2)}) collective-permute-start(f32[10,128,128]{2,1,0:T(8,128)} %pad_maximum_fusion), channel_id=1, source_target_pairs={{0,2},{4,10},{11,5},{15,13},{16,18},{20,26},{27,21},{31,29}} | collective-permute-start | bytes 1966088 | tf_op jit(solution)/shard_map/ppermute | solution.py:65
  21.7 26.3 %collective-permute-start.8 = (f32[10,128,128]{2,1,0:T(8,128)}, f32[10,128,128]{2,1,0:T(8,128)S(1)}, u32[]{:S(2)}, u32[]{:S(2)}) collective-permute-start(f32[10,128,128]{2,1,0:T(8,128)} %pad_maximum_fusion), channel_id=1, source_target_pairs={{3,2},{7,10},{8,5},{12,13},{19,18},{23,26},{24,21},{28,29}} | collective-permute-start | bytes 1966088 | tf_op jit(solution)/shard_map/ppermute | solution.py:65
  24.1 9.6 %collective-permute-start.10 = (f32[4,128,128]{2,1,0:T(8,128)S(1)}, f32[4,128,128]{2,1,0:T(8,128)S(1)}, u32[]{:S(2)}, u32[]{:S(2)}) collective-permute-start(f32[4,128,128]{2,1,0:T(8,128)S(1)} %slice.40), channel_id=1, source_target_pairs={{0,8},{1,9},{2,10},{3,11},{4,12},{5,13},{6,14},{7,15},{8,0},{9,1},... | collective-permute-start | bytes 786440 | tf_op jit(solution)/shard_map/ppermute | solution.py:65
  32.3 15.7 %collective-permute-start.6 = (f32[10,128,128]{2,1,0:T(8,128)S(1)}, f32[10,128,128]{2,1,0:T(8,128)S(1)}, u32[]{:S(2)}, u32[]{:S(2)}) collective-permute-start(f32[10,128,128]{2,1,0:T(8,128)S(1)} %broadcast_select_fusion), channel_id=1, source_target_pairs={{0,2},{5,10},{10,5},{15,13},{16,18},{21,26},{26,21},{31,29}} | collective-permute-start | bytes 1966088 | tf_op jit(solution)/shard_map/ppermute | solution.py:65
  33.7 8.1 %collective-permute-start.9 = (f32[4,256,128]{2,1,0:T(8,128)S(1)}, f32[4,256,128]{2,1,0:T(8,128)S(1)}, u32[]{:S(2)}, u32[]{:S(2)}) collective-permute-start(f32[4,256,128]{2,1,0:T(8,128)S(1)} %get-tuple-element.48.own), channel_id=1, source_target_pairs={{0,8},{1,9},{2,10},{3,11},{4,12},{5,13},{6,14},{7,15},{8,0},{9,1},... | collective-permute-start | bytes 1572872 | tf_op jit(solution)/shard_map/ppermute | solution.py:65
  41.8 41.2 %copy-start.1 = (f32[1,2,128,128]{3,2,1,0:T(8,128)S(1)}, f32[1,2,128,128]{3,2,1,0:T(8,128)}, u32[]{:S(2)}) copy-start(f32[1,2,128,128]{3,2,1,0:T(8,128)} %param.15) | copy-start | bytes 393220
  41.8 54.6 %copy-start.4 = (s32[4]{0:T(128)S(1)}, s32[4]{0:T(128)}, u32[]{:S(2)}) copy-start(s32[4]{0:T(128)} %angles.1) | copy-start | bytes 52
  54.3 2.1 %collective-permute-start.11 = (f32[4,256,128]{2,1,0:T(8,128)S(1)}, f32[4,256,128]{2,1,0:T(8,128)S(1)}, u32[]{:S(2)}, u32[]{:S(2)}) collective-permute-start(f32[4,256,128]{2,1,0:T(8,128)S(1)} %slice.41), channel_id=1, source_target_pairs={{0,8},{1,9},{2,10},{3,11},{4,12},{5,13},{6,14},{7,15},{8,0},{9,1},... | collective-permute-start | bytes 1572872 | tf_op jit(solution)/shard_map/ppermute | solution.py:65
  57.2 2.0 %collective-permute-start.12 = (f32[4,256,128]{2,1,0:T(8,128)S(1)}, f32[4,256,128]{2,1,0:T(8,128)S(1)}, u32[]{:S(2)}, u32[]{:S(2)}) collective-permute-start(f32[4,256,128]{2,1,0:T(8,128)S(1)} %shard_map.119.own), channel_id=1, source_target_pairs={{0,8},{1,9},{2,10},{3,11},{4,12},{5,13},{6,14},{7,15},{8,0},{9,1},... | collective-permute-start | bytes 1572872 | tf_op jit(solution)/shard_map/ppermute | solution.py:65
  70.6 2.0 %collective-permute-start.13 = (f32[4,256,128]{2,1,0:T(8,128)S(1)}, f32[4,256,128]{2,1,0:T(8,128)S(1)}, u32[]{:S(2)}, u32[]{:S(2)}) collective-permute-start(f32[4,256,128]{2,1,0:T(8,128)S(1)} %slice.42), channel_id=1, source_target_pairs={{0,8},{1,9},{2,10},{3,11},{4,12},{5,13},{6,14},{7,15},{8,0},{9,1},... | collective-permute-start | bytes 1572872 | tf_op jit(solution)/shard_map/ppermute | solution.py:65
  73.5 7.3 %collective-permute-start.16 = (f32[2,128,128]{2,1,0:T(8,128)S(1)}, f32[2,128,128]{2,1,0:T(8,128)S(1)}, u32[]{:S(2)}, u32[]{:S(2)}) collective-permute-start(f32[2,128,128]{2,1,0:T(8,128)S(1)} %bitcast.29), channel_id=1, source_target_pairs={{2,2},{10,6},{5,10},{13,14},{18,18},{26,22},{21,26},{29,30}} | collective-permute-start | bytes 393224 | tf_op jit(solution)/shard_map/ppermute | solution.py:65
  74.2 6.7 %collective-permute-start.17 = (f32[2,128,128]{2,1,0:T(8,128)S(1)}, f32[2,128,128]{2,1,0:T(8,128)S(1)}, u32[]{:S(2)}, u32[]{:S(2)}) collective-permute-start(f32[2,128,128]{2,1,0:T(8,128)S(1)} %bitcast.28), channel_id=1, source_target_pairs={{2,3},{10,7},{5,11},{13,15},{18,19},{26,23},{21,27},{29,31}} | collective-permute-start | bytes 393224 | tf_op jit(solution)/shard_map/ppermute | solution.py:65
  74.8 6.0 %collective-permute-start.15 = (f32[2,128,128]{2,1,0:T(8,128)S(1)}, f32[2,128,128]{2,1,0:T(8,128)S(1)}, u32[]{:S(2)}, u32[]{:S(2)}) collective-permute-start(f32[2,128,128]{2,1,0:T(8,128)S(1)} %bitcast.27), channel_id=1, source_target_pairs={{2,1},{10,5},{5,9},{13,13},{18,17},{26,21},{21,25},{29,29}} | collective-permute-start | bytes 393224 | tf_op jit(solution)/shard_map/ppermute | solution.py:65
  75.5 7.5 %collective-permute-start.14 = (f32[2,128,128]{2,1,0:T(8,128)S(1)}, f32[2,128,128]{2,1,0:T(8,128)S(1)}, u32[]{:S(2)}, u32[]{:S(2)}) collective-permute-start(f32[2,128,128]{2,1,0:T(8,128)S(1)} %bitcast.26), channel_id=1, source_target_pairs={{2,0},{10,4},{5,8},{13,12},{18,16},{26,20},{21,24},{29,28}} | collective-permute-start | bytes 393224 | tf_op jit(solution)/shard_map/ppermute | solution.py:65
